TPU v7x, 32 devices: a whole 2x2x4 slice. The times are simulated.
32 devices in a mesh: dp: 16 (over z, y, core), mp: 2 (over x).
Axes of the slice: x: 2, y: 2, z: 4, core: 2. Of those that a mesh axis runs over, the one named last changes fastest.
Arguments:
- block_input: bfloat16 [16384, 1024], P(('dp', 'mp')), may hold values from -6 to 6
- seq_lengths: int32 [16], replicated, may hold values from 576 to 1024, as said below
- seq_owner: int32 [16], replicated, may hold values from 0 to 15, as said below
- mix_gain: float32 [1024], replicated, may hold values from 0.5 to 1.5
- query_weight: bfloat16 [1024, 512], P('dp', 'mp'), may hold values from -0.1875 to 0.1875
- key_weight: bfloat16 [1024, 512], P('dp', 'mp'), may hold values from -0.1875 to 0.1875
- value_weight: bfloat16 [1024, 1024], P('dp', 'mp'), may hold values from -0.1875 to 0.1875
- gate_weight: bfloat16 [1024, 1024], P('dp', 'mp'), may hold values from -0.1875 to 0.1875
- decay_weight: bfloat16 [1024, 4], replicated, may hold values from -0.1875 to 0.1875
- beta_weight: bfloat16 [1024, 4], replicated, may hold values from -0.1875 to 0.1875
- query_filter: float32 [4, 512], replicated, may hold values from -3 to 3
- key_filter: float32 [4, 512], replicated, may hold values from -3 to 3
- value_filter: float32 [4, 1024], replicated, may hold values from -3 to 3
- decay_log: float32 [4], replicated, may hold values from -4 to 0
- decay_bias: float32 [4], replicated, may hold values from -5 to -1
- head_gain: float32 [256], replicated, may hold values from 0.5 to 1.5
- out_weight: bfloat16 [1024, 1024], P('mp', 'dp'), may hold values from -0.1875 to 0.1875
- ffn_gain: float32 [1024], replicated, may hold values from 0.5 to 1.5
- ffn_gate: bfloat16 [1024, 2816], P('dp', 'mp'), may hold values from -0.1875 to 0.1875
- ffn_up: bfloat16 [1024, 2816], P('dp', 'mp'), may hold values from -0.1875 to 0.1875
- ffn_down: bfloat16 [2816, 1024], P('mp', 'dp'), may hold values from -0.109375 to 0.109375
- cotangent: bfloat16 [16384, 1024], P(('dp', 'mp')), may hold values from -6 to 6
Outputs:
- block_output: bfloat16 [16384, 1024], P(('dp', 'mp'))
- input_grad: float32 [16384, 1024], P(('dp', 'mp'))
- mix_gain_grad: float32 [1024], replicated
- query_weight_grad: float32 [1024, 512], P('dp', 'mp')
- key_weight_grad: float32 [1024, 512], P('dp', 'mp')
- value_weight_grad: float32 [1024, 1024], P('dp', 'mp')
- gate_weight_grad: float32 [1024, 1024], P('dp', 'mp')
- decay_weight_grad: float32 [1024, 4], replicated
- beta_weight_grad: float32 [1024, 4], replicated
- query_filter_grad: float32 [4, 512], replicated
- key_filter_grad: float32 [4, 512], replicated
- value_filter_grad: float32 [4, 1024], replicated
- decay_log_grad: float32 [4], replicated
- decay_bias_grad: float32 [4], replicated
- head_gain_grad: float32 [256], replicated
- out_weight_grad: float32 [1024, 1024], P('mp', 'dp')
- ffn_gain_grad: float32 [1024], replicated
- ffn_gate_grad: float32 [1024, 2816], P('dp', 'mp')
- ffn_up_grad: float32 [1024, 2816], P('dp', 'mp')
- ffn_down_grad: float32 [2816, 1024], P('mp', 'dp')
Inputs may be any that keep to these rules, and one draw needn't show every extreme that they name: `seq_lengths`: each entry is a multiple of 64 from 576 to 1024; the entries that one index of dp holds sum to at most 1024, and some index's sum equals it. `seq_owner`: every index of dp holds exactly one entry.
All inputs are finite; a program needn't handle non-finite values.
Results may differ from a plain program's by a relative error of at most 0.023.
Values may be sent and summed in bfloat16 or wider, within the bound.
No kernel may reach another device: no remote copies, remote signals or barrier semaphores. Data moves between devices by JAX's collectives and lax.ppermute only.
A program may use at most 256 MiB of HBM per device.

v0:
```python
from functools import partial
import math

import jax
import jax.numpy as jnp
from jax import lax
from jax.sharding import PartitionSpec as P

DK = 128
DV = 256
KW = 4
SPAN = 64


EPS = 1e-06
PRECISE = lax.Precision.HIGHEST


def layout(seq_lengths, seq_owner, device, row_count):
    owned = seq_owner == device
    own_lengths = jnp.where(owned, seq_lengths, 0)
    offsets = jnp.cumsum(own_lengths) - own_lengths
    loaded = jnp.sum(own_lengths)
    span_starts = jnp.arange(row_count // SPAN, dtype=jnp.int32) * SPAN
    begins = jnp.any(
        (offsets[None, :] == span_starts[:, None]) & (own_lengths[None, :] > 0), axis=1
    )
    resets = begins | (span_starts == loaded)
    within = jnp.arange(SPAN, dtype=jnp.int32)
    keep_masks = jnp.stack(
        [
            jnp.logical_not(resets[:, None] & (within[None, :] < offset)).reshape(row_count)
            for offset in range(KW)
        ]
    ).astype(jnp.float32)
    valid_rows = (jnp.arange(row_count, dtype=jnp.int32) < loaded).astype(jnp.float32)
    return (keep_masks, resets, valid_rows)


def head_dot_product(formula, left, right):
    return jnp.einsum(formula, left, right, precision=PRECISE)


def across_rows(left, right):
    return lax.dot_general(
        left, right, (((0,), (0,)), ((), ())), preferred_element_type=jnp.float32
    )


def against(left, right):
    return lax.dot_general(
        left, right, (((1,), (1,)), ((), ())), preferred_element_type=jnp.float32
    )


def rms_forward(values):
    inv_rms = lax.rsqrt(jnp.mean(values * values, -1, keepdims=True) + EPS)
    return (values * inv_rms, inv_rms)


def rms_backward(upstream, normed, inv_rms):
    return inv_rms * (upstream - normed * jnp.mean(upstream * normed, -1, keepdims=True))


def causal_conv(signal, filters, keep_masks):
    summed = signal * filters[0]
    for offset in range(1, KW):
        delayed = jnp.concatenate(
            [jnp.zeros((offset, signal.shape[1]), jnp.float32), signal[:-offset]], axis=0
        )
        summed = summed + delayed * filters[offset] * keep_masks[offset][:, None]
    return summed


def unit_norm(vectors):
    return vectors * lax.rsqrt(jnp.sum(vectors * vectors, -1, keepdims=True) + EPS)


def delta_rule(queries, keys_unit, values_in, decays, betas, resets):
    row_count, heads_local = decays.shape
    blocks = row_count // SPAN

    def blocked(tensor):
        return jnp.swapaxes(tensor.reshape((blocks, SPAN) + tensor.shape[1:]), 1, 2)

    query_blocks = blocked(queries)
    key_blocks = blocked(keys_unit)
    value_blocks = blocked(values_in)
    beta_blocks = blocked(betas)
    cumulative = jnp.cumsum(blocked(decays), axis=-1)
    gap_matrix = cumulative[..., :, None] - cumulative[..., None, :]
    lower_mask = jnp.tril(jnp.ones((SPAN, SPAN), jnp.float32))
    strict = lower_mask - jnp.eye(SPAN, dtype=jnp.float32)
    factor = jnp.exp(gap_matrix * lower_mask) * lower_mask
    key_gram = head_dot_product("bhik,bhjk->bhij", key_blocks, key_blocks)
    query_key = head_dot_product("bhik,bhjk->bhij", query_blocks, key_blocks)
    coupling = beta_blocks[..., :, None] * factor * strict * key_gram
    inverse = jnp.eye(SPAN, dtype=jnp.float32) - coupling
    powered = coupling
    for round_index in range(SPAN.bit_length() - 2):
        powered = head_dot_product("bhij,bhjk->bhik", powered, powered)
        inverse = inverse + head_dot_product("bhij,bhjk->bhik", inverse, powered)
    growth = jnp.exp(cumulative)
    span_end = cumulative[..., -1:]
    value_part = head_dot_product("bhij,bhjv->bhiv", inverse, beta_blocks[..., None] * value_blocks)
    key_part = head_dot_product(
        "bhij,bhjk->bhik", inverse, (beta_blocks * growth)[..., None] * key_blocks
    )
    query_grown = growth[..., None] * query_blocks
    key_tail = jnp.exp(span_end - cumulative)[..., None] * key_blocks
    tail_decay = jnp.exp(span_end)
    mixing_all = factor * query_key

    def advance(state, inputs):
        (
            restart,
            projected_value,
            projected_key,
            query_gathered_rows,
            key_at_step,
            tail_decay_cumulative,
            token_mixer_output,
        ) = inputs
        starting_state = jnp.where(restart, jnp.zeros_like(state), state)
        written_value_rows = projected_value - head_dot_product(
            "dqw,dwy->dqy", projected_key, starting_state
        )
        block_result_output = head_dot_product(
            "dqw,dwy->dqy", query_gathered_rows, starting_state
        ) + head_dot_product("mgy,myt->mgt", token_mixer_output, written_value_rows)
        state_after_update = tail_decay_cumulative[:, :, None] * starting_state + head_dot_product(
            "gny,gnr->gyr", key_at_step, written_value_rows
        )
        return (state_after_update, block_result_output)

    initial = jnp.zeros((heads_local, DK, DV), jnp.float32)
    final_state, outputs = lax.scan(
        advance,
        initial,
        (resets, value_part, key_part, query_grown, key_tail, tail_decay, mixing_all),
    )
    return jnp.swapaxes(outputs, 1, 2).reshape(row_count, heads_local, DV)


def packed_mixer(projections, smalls, keep_masks, resets):
    proj_q, proj_k, proj_v, proj_gate, proj_decay, proj_beta = projections
    query_filter, key_filter, value_filter, decay_log, decay_bias, head_gain = smalls
    row_count = proj_q.shape[0]
    heads_local = decay_log.shape[0]
    queries = unit_norm(
        jax.nn.silu(causal_conv(proj_q, query_filter, keep_masks)).reshape(
            row_count, heads_local, DK
        )
    ) * (1.0 / math.sqrt(DK))
    keys_unit = unit_norm(
        jax.nn.silu(causal_conv(proj_k, key_filter, keep_masks)).reshape(row_count, heads_local, DK)
    )
    values_in = jax.nn.silu(causal_conv(proj_v, value_filter, keep_masks)).reshape(
        row_count, heads_local, DV
    )
    betas = jax.nn.sigmoid(proj_beta)
    decays = -jnp.exp(decay_log) * jax.nn.softplus(proj_decay + decay_bias)
    outputs = delta_rule(queries, keys_unit, values_in, decays, betas, resets)
    normed = outputs * lax.rsqrt(jnp.mean(outputs * outputs, -1, keepdims=True) + EPS)
    gated = normed * head_gain * jax.nn.silu(proj_gate.reshape(row_count, heads_local, DV))
    return gated.reshape(row_count, heads_local * DV)


def on_device(
    block_input,
    seq_lengths,
    seq_owner,
    mix_gain,
    query_weight,
    key_weight,
    value_weight,
    gate_weight,
    decay_weight,
    beta_weight,
    query_filter,
    key_filter,
    value_filter,
    decay_log,
    decay_bias,
    head_gain,
    out_weight,
    ffn_gain,
    ffn_gate,
    ffn_up,
    ffn_down,
    cotangent,
):
    local_rows = block_input.shape[0]
    model_count = lax.axis_size("mp")
    model_index = lax.axis_index("mp")
    keep_masks, resets, valid_rows = layout(
        seq_lengths, seq_owner, lax.axis_index("dp"), local_rows * model_count
    )
    valid_col = lax.dynamic_slice_in_dim(valid_rows, model_index * local_rows, local_rows)[:, None]
    heads_local = decay_log.shape[0] // model_count

    def own_columns(array, col_count):
        return lax.dynamic_slice_in_dim(array, model_index * col_count, col_count, array.ndim - 1)

    def widen(grad_part, whole):
        col_count = grad_part.shape[-1]
        return lax.dynamic_update_slice_in_dim(
            jnp.zeros(whole.shape, jnp.float32),
            grad_part,
            model_index * col_count,
            grad_part.ndim - 1,
        )

    forward_weights = (
        lax.all_gather(query_weight, "dp", axis=0, tiled=True),
        lax.all_gather(key_weight, "dp", axis=0, tiled=True),
        lax.all_gather(value_weight, "dp", axis=0, tiled=True),
        lax.all_gather(gate_weight, "dp", axis=0, tiled=True),
        lax.all_gather(out_weight, "dp", axis=1, tiled=True),
        lax.all_gather(ffn_gate, "dp", axis=0, tiled=True),
        lax.all_gather(ffn_up, "dp", axis=0, tiled=True),
        lax.all_gather(ffn_down, "dp", axis=1, tiled=True),
    )
    (
        query_full,
        key_full,
        value_full,
        gate_full,
        out_full,
        ffn_gate_full,
        ffn_up_full,
        ffn_down_full,
    ) = forward_weights
    decay_own = own_columns(decay_weight, heads_local)
    beta_own = own_columns(beta_weight, heads_local)
    smalls = (
        own_columns(query_filter, heads_local * DK),
        own_columns(key_filter, heads_local * DK),
        own_columns(value_filter, heads_local * DV),
        own_columns(decay_log, heads_local),
        own_columns(decay_bias, heads_local),
        head_gain,
    )
    inputs_f = block_input.astype(jnp.float32)
    normed1, inv_rms1 = rms_forward(inputs_f)
    mixed_in = (normed1 * mix_gain).astype(jnp.bfloat16)
    mixed_all = lax.all_gather(mixed_in, "mp", axis=0, tiled=True)
    forward_proj = (query_full, key_full, value_full, gate_full, decay_own, beta_own)
    projections = tuple(
        (
            jnp.dot(mixed_all, weight_mat, preferred_element_type=jnp.float32)
            for weight_mat in forward_proj
        )
    )
    gated, pullback = jax.vjp(
        partial(packed_mixer, keep_masks=keep_masks, resets=resets), projections, smalls
    )
    gated_b = gated.astype(jnp.bfloat16)
    mix_part = jnp.dot(gated_b, out_full, preferred_element_type=jnp.float32)
    resid = inputs_f + valid_col * lax.psum_scatter(
        mix_part.astype(jnp.bfloat16), "mp", scatter_dimension=0, tiled=True
    ).astype(jnp.float32)
    normed2, inv_rms2 = rms_forward(resid)
    ffn_in = (normed2 * ffn_gain).astype(jnp.bfloat16)
    ffn_all = lax.all_gather(ffn_in, "mp", axis=0, tiled=True)
    gate_pre = jnp.dot(ffn_all, ffn_gate_full, preferred_element_type=jnp.float32)
    up_pre = jnp.dot(ffn_all, ffn_up_full, preferred_element_type=jnp.float32)
    sigmoid_gate = jax.nn.sigmoid(gate_pre)
    activated = gate_pre * sigmoid_gate
    hidden = (activated * up_pre).astype(jnp.bfloat16)
    ffn_part = jnp.dot(hidden, ffn_down_full, preferred_element_type=jnp.float32)
    block_output = (
        resid
        + valid_col
        * lax.psum_scatter(
            ffn_part.astype(jnp.bfloat16), "mp", scatter_dimension=0, tiled=True
        ).astype(jnp.float32)
    ).astype(jnp.bfloat16)
    back_weights = (
        lax.all_gather(query_weight, "dp", axis=0, tiled=True),
        lax.all_gather(key_weight, "dp", axis=0, tiled=True),
        lax.all_gather(value_weight, "dp", axis=0, tiled=True),
        lax.all_gather(gate_weight, "dp", axis=0, tiled=True),
        lax.all_gather(out_weight, "dp", axis=1, tiled=True),
        lax.all_gather(ffn_gate, "dp", axis=0, tiled=True),
        lax.all_gather(ffn_up, "dp", axis=0, tiled=True),
        lax.all_gather(ffn_down, "dp", axis=1, tiled=True),
    )
    (
        query_back,
        key_back,
        value_back,
        gate_back,
        out_back,
        ffn_gate_back,
        ffn_up_back,
        ffn_down_back,
    ) = back_weights
    cot_masked = cotangent * valid_col.astype(jnp.bfloat16)
    cot_all = lax.all_gather(cot_masked, "mp", axis=0, tiled=True)
    down_grad = across_rows(hidden, cot_all)
    hidden_grad = against(cot_all, ffn_down_back)
    gate_grad_pre = (
        hidden_grad * up_pre * sigmoid_gate * (1.0 + gate_pre * (1.0 - sigmoid_gate))
    ).astype(jnp.bfloat16)
    up_grad_pre = (hidden_grad * activated).astype(jnp.bfloat16)
    ffn_gate_grad = across_rows(ffn_all, gate_grad_pre)
    ffn_up_grad = across_rows(ffn_all, up_grad_pre)
    ffn_in_part = against(gate_grad_pre, ffn_gate_back) + against(up_grad_pre, ffn_up_back)
    ffn_in_grad = lax.psum_scatter(
        ffn_in_part.astype(jnp.bfloat16), "mp", scatter_dimension=0, tiled=True
    ).astype(jnp.float32)
    ffn_gain_part = jnp.sum(ffn_in_grad * normed2, 0)
    resid_grad = cotangent.astype(jnp.float32) + rms_backward(
        ffn_in_grad * ffn_gain, normed2, inv_rms2
    )
    ffn_sums = (ffn_gate_grad, ffn_up_grad, down_grad)
    mix_cot = (resid_grad * valid_col).astype(jnp.bfloat16)
    mix_cot_all = lax.all_gather(mix_cot, "mp", axis=0, tiled=True)
    out_grad = across_rows(gated_b, mix_cot_all)
    gated_grad = against(mix_cot_all, out_back)
    proj_grads, small_grads = pullback(gated_grad)
    proj_grads_b = tuple((grad_piece.astype(jnp.bfloat16) for grad_piece in proj_grads))
    weight_grads = tuple((across_rows(mixed_all, grad_piece) for grad_piece in proj_grads_b))
    backward_proj = (query_back, key_back, value_back, gate_back, decay_own, beta_own)
    mix_in_part = jnp.zeros((mixed_all.shape[0], mixed_all.shape[1]), jnp.float32)
    for grad_piece, weight_mat in zip(proj_grads_b, backward_proj):
        mix_in_part = mix_in_part + against(grad_piece, weight_mat)
    mix_in_grad = lax.psum_scatter(
        mix_in_part.astype(jnp.bfloat16), "mp", scatter_dimension=0, tiled=True
    ).astype(jnp.float32)
    mix_gain_part = jnp.sum(mix_in_grad * normed1, 0)
    input_grad = resid_grad + rms_backward(mix_in_grad * mix_gain, normed1, inv_rms1)
    all_sums = (
        lax.psum_scatter(weight_grads[0], "dp", scatter_dimension=0, tiled=True),
        lax.psum_scatter(weight_grads[1], "dp", scatter_dimension=0, tiled=True),
        lax.psum_scatter(weight_grads[2], "dp", scatter_dimension=0, tiled=True),
        lax.psum_scatter(weight_grads[3], "dp", scatter_dimension=0, tiled=True),
        lax.psum_scatter(out_grad, "dp", scatter_dimension=1, tiled=True),
        lax.psum_scatter(ffn_sums[0], "dp", scatter_dimension=0, tiled=True),
        lax.psum_scatter(ffn_sums[1], "dp", scatter_dimension=0, tiled=True),
        lax.psum_scatter(ffn_sums[2], "dp", scatter_dimension=1, tiled=True),
    )
    mix_sums = all_sums[:5]
    ffn_done = all_sums[5:]
    summed = lax.psum(
        (
            mix_gain_part,
            widen(weight_grads[4], decay_weight),
            widen(weight_grads[5], beta_weight),
            widen(small_grads[0], query_filter),
            widen(small_grads[1], key_filter),
            widen(small_grads[2], value_filter),
            widen(small_grads[3], decay_log),
            widen(small_grads[4], decay_bias),
            small_grads[5],
            ffn_gain_part,
        ),
        ("dp", "mp"),
    )
    return (
        block_output,
        input_grad,
        summed[0],
        mix_sums[0],
        mix_sums[1],
        mix_sums[2],
        mix_sums[3],
        summed[1],
        summed[2],
        summed[3],
        summed[4],
        summed[5],
        summed[6],
        summed[7],
        summed[8],
        mix_sums[4],
        summed[9],
        ffn_done[0],
        ffn_done[1],
        ffn_done[2],
    )


def solution(mesh):
    in_specs = (
        P(("dp", "mp"), None),
        P(),
        P(),
        P(),
        P("dp", "mp"),
        P("dp", "mp"),
        P("dp", "mp"),
        P("dp", "mp"),
        P(),
        P(),
        P(),
        P(),
        P(),
        P(),
        P(),
        P(),
        P("mp", "dp"),
        P(),
        P("dp", "mp"),
        P("dp", "mp"),
        P("mp", "dp"),
        P(("dp", "mp"), None),
    )
    out_specs = (
        P(("dp", "mp"), None),
        P(("dp", "mp"), None),
        P(),
        P("dp", "mp"),
        P("dp", "mp"),
        P("dp", "mp"),
        P("dp", "mp"),
        P(),
        P(),
        P(),
        P(),
        P(),
        P(),
        P(),
        P(),
        P("mp", "dp"),
        P(),
        P("dp", "mp"),
        P("dp", "mp"),
        P("mp", "dp"),
    )
    return jax.shard_map(
        on_device, mesh=mesh, in_specs=in_specs, out_specs=out_specs, check_vma=False
    )
```

profile of v0, /device:TPU:0, one launch (start us, length us, event | category | flops | bytes accessed | tf_op | source)
XLA Modules:
  0.0 1907.2 jit_solution(7831426513347601906)
XLA Ops:
  16.9 24.6 %all_gather.47 = bf16[1024,256]{1,0:T(8,128)(2,1)S(1)} all-gather(bf16[64,256]{1,0:T(8,128)(2,1)S(1)} %copy-done.114), channel_id=1, replica_groups=mesh['dp'=16,'mp'=2] {'dp'}, dimensions={0}, use_global_device_ids=true | all-gather | bytes 557056 | tf_op jit(solution)/shard_map/all_gather | solution.py:215
  41.5 18.9 all_gather.45
  69.0 4.1 multiply_reduce_fusion.17
  110.4 3.9 reshape.495
  114.3 3.8 convolution_add_fusion.10
  121.6 3.6 fusion.101
  134.9 4.9 fusion.135
  148.3 199.2 %while.46 = (s32[]{:T(128)}, f32[2,128,256]{2,1,0:T(8,128)S(1)}, f32[16,2,64,256]{3,2,1,0:T(8,128)}, f32[16,2,128,256]{3,2,1,0:T(8,128)}, f32[16,2,64,256]{3,2,1...) while((s32[]{:T(128)}, f32[2,128,256]{2,1,0:T(8,128)S(1)}, ...), condition=%wide.region_8.9_spmd.clone, body=%wide.region_7.8_spmd.clone.sunk | while | flops 176881664 | bytes 2890940 | solution.py:137
  358.2 5.8 multiply_convert_fusion.5
  364.0 4.2 convolution_convert_fusion.1
  369.6 29.6 %reduce-scatter.13.cloned.1.call-done = bf16[512,1024]{1,0:T(8,128)(2,1)} async-done(((bf16[1024,1024]{1,0:T(8,128)(2,1)}), bf16[512,1024]{1,0:T(8,128)(2,1)}) %reduce-scatter.13.cloned.1.call-update) | async-done | bytes 1048592 | tf_op jit(solution)/shard_map/reduce_scatter | solution.py:260
  406.4 39.5 %all-gather.21.cloned.1.call-done = bf16[1024,1408]{1,0:T(8,128)(2,1)} async-done(((bf16[64,1408]{1,0:T(8,128)(2,1)}), bf16[1024,1408]{1,0:T(8,128)(2,1)}) %all-gather.21.cloned.1.call-update) | async-done | bytes 2883600 | tf_op jit(solution)/shard_map/all_gather | solution.py:220
  446.0 33.1 %all-gather.19.cloned.1.call-done = bf16[1024,1024]{1,0:T(8,128)(2,1)} async-done(((bf16[512,1024]{1,0:T(8,128)(2,1)}), bf16[1024,1024]{1,0:T(8,128)(2,1)}) %all-gather.19.cloned.1.call-update) | async-done | bytes 2097168 | tf_op jit(solution)/shard_map/all_gather | solution.py:265
  479.0 8.3 fusion.220
  487.4 38.6 %all-gather.23.cloned.1.call-done = bf16[1024,1408]{1,0:T(8,128)(2,1)} async-done(((bf16[64,1408]{1,0:T(8,128)(2,1)}), bf16[1024,1408]{1,0:T(8,128)(2,1)}) %all-gather.23.cloned.1.call-update) | async-done | bytes 2883600 | tf_op jit(solution)/shard_map/all_gather | solution.py:221
  526.0 8.4 fusion.221
  534.4 24.7 %all-gather.27.cloned.1.call-done = bf16[1024,1024]{1,0:T(8,128)(2,1)} async-done(((bf16[512,1024]{1,0:T(8,128)(2,1)}), bf16[1024,1024]{1,0:T(8,128)(2,1)}) %all-gather.27.cloned.1.call-update) | async-done | bytes 2097168 | tf_op jit(solution)/shard_map/all_gather | solution.py:300
  559.1 46.8 %all-gather.25.cloned.1.call-done = bf16[1408,1024]{0,1:T(8,128)(2,1)} async-done(((bf16[1408,64]{0,1:T(8,128)(2,1)}), bf16[1408,1024]{0,1:T(8,128)(2,1)}) %all-gather.25.cloned.1.call-update) | async-done | bytes 2883600 | tf_op jit(solution)/shard_map/all_gather | solution.py:222
  605.9 11.7 multiply_convert_fusion
  621.5 4.7 add_convert_fusion.1
  626.2 30.2 %reduce-scatter.17.cloned.1.call-done = bf16[512,1024]{1,0:T(8,128)(2,1)} async-done(((bf16[1024,1024]{1,0:T(8,128)(2,1)}), bf16[512,1024]{1,0:T(8,128)(2,1)}) %reduce-scatter.17.cloned.1.call-update) | async-done | bytes 1048592 | tf_op jit(solution)/shard_map/reduce_scatter | solution.py:310
  662.9 3.6 reshape.500
  669.2 25.7 %all-gather.29.cloned.1.call-done = bf16[1024,1024]{1,0:T(8,128)(2,1)} async-done(((bf16[512,1024]{1,0:T(8,128)(2,1)}), bf16[1024,1024]{1,0:T(8,128)(2,1)}) %all-gather.29.cloned.1.call-update) | async-done | bytes 2097168 | tf_op jit(solution)/shard_map/all_gather | solution.py:319
  694.9 7.2 fusion.97
  702.1 3.7 reshape.499
  705.7 4.1 multiply_reduce_fusion
  718.2 270.5 %while.47 = (s32[]{:T(128)}, f32[2,128,256]{2,1,0:T(8,128)S(1)}, f32[16,2,64,256]{3,2,1,0:T(8,128)}, f32[16,2,64,128]{3,2,1,0:T(8,128)}, f32[16,2,64,128]{3,2,1,...) while((s32[]{:T(128)}, f32[2,128,256]{2,1,0:T(8,128)S(1)}, ...), condition=%wide.region_18.19_spmd.clone, body=%wide.region_16.18_spmd.clone.sunk | while | flops 353075200 | bytes 4728682 | solution.py:137
  988.8 5.9 fusion.98
  1035.6 3.7 convolution_add_fusion.26
  1039.3 4.0 multiply_reduce_fusion.16
  1050.6 5.1 broadcast_multiply_fusion.4
  1102.8 4.7 multiply_reduce_fusion.1
  1116.1 7.5 convolution_convert_fusion
  1128.9 8.4 fusion.237
  1137.6 8.5 fusion.238
  1146.1 8.4 fusion.239
  1155.8 4.6 fusion.236
  1173.5 8.6 reduce-scatter.15.cloned.1.call-done
  1182.1 4.4 fusion.83
  1186.5 57.0 %reduce-scatter.23.cloned.1.call-done = f32[64,256]{1,0:T(8,128)} async-done(((f32[1024,256]{1,0:T(8,128)}), f32[64,256]{1,0:T(8,128)}) %reduce-scatter.23.cloned.1.call-update) | async-done | bytes 65552 | tf_op jit(solution)/shard_map/reduce_scatter | solution.py:336
  1243.5 60.9 %reduce-scatter.21.cloned.1.call-done = f32[64,256]{1,0:T(8,128)} async-done(((f32[1024,256]{1,0:T(8,128)}), f32[64,256]{1,0:T(8,128)}) %reduce-scatter.21.cloned.1.call-update) | async-done | bytes 65552 | tf_op jit(solution)/shard_map/reduce_scatter | solution.py:335
  1304.5 84.9 %reduce-scatter.31.cloned.1.call-done = f32[64,1408]{1,0:T(8,128)} async-done(((f32[1024,1408]{1,0:T(8,128)}), f32[64,1408]{1,0:T(8,128)}) %reduce-scatter.31.cloned.1.call-update) | async-done | bytes 360464 | tf_op jit(solution)/shard_map/reduce_scatter | solution.py:340
  1389.4 85.1 %reduce-scatter.33.cloned.1.call-done = f32[64,1408]{1,0:T(8,128)} async-done(((f32[1024,1408]{1,0:T(8,128)}), f32[64,1408]{1,0:T(8,128)}) %reduce-scatter.33.cloned.1.call-update) | async-done | bytes 360464 | tf_op jit(solution)/shard_map/reduce_scatter | solution.py:341
  1474.5 85.3 %reduce-scatter.35.cloned.1.call-done = f32[1408,64]{0,1:T(8,128)} async-done(((f32[1408,1024]{0,1:T(8,128)}), f32[1408,64]{0,1:T(8,128)}) %reduce-scatter.35.cloned.1.call-update) | async-done | bytes 360464 | tf_op jit(solution)/shard_map/reduce_scatter | solution.py:342
  1559.8 65.0 %reduce-scatter.29.cloned.1.call-done = f32[512,64]{0,1:T(8,128)} async-done(((f32[512,1024]{0,1:T(8,128)}), f32[512,64]{0,1:T(8,128)}) %reduce-scatter.29.cloned.1.call-update) | async-done | bytes 131088 | tf_op jit(solution)/shard_map/reduce_scatter | solution.py:339
  1624.8 65.4 %reduce-scatter.25.cloned.1.call-done = f32[64,512]{1,0:T(8,128)} async-done(((f32[1024,512]{1,0:T(8,128)}), f32[64,512]{1,0:T(8,128)}) %reduce-scatter.25.cloned.1.call-update) | async-done | bytes 131088 | tf_op jit(solution)/shard_map/reduce_scatter | solution.py:337
  1690.2 64.9 %reduce-scatter.27.cloned.1.call-done = f32[64,512]{1,0:T(8,128)} async-done(((f32[1024,512]{1,0:T(8,128)}), f32[64,512]{1,0:T(8,128)}) %reduce-scatter.27.cloned.1.call-update) | async-done | bytes 131088 | tf_op jit(solution)/shard_map/reduce_scatter | solution.py:338
  1755.1 132.7 %all-reduce.34.cloned.1.call-done = (f32[1024]{0:T(1024)}, f32[1024,4]{0,1:T(4,128)}, f32[1024,4]{0,1:T(4,128)}, f32[4,512]{1,0:T(4,128)}, f32[4,512]{1,0:T(4,12...) async-done(((f32[1024]{0:T(1024)}, f32[1024,4]{0,1:T(4,128)}, f32[1024,4]{0,1:T(4,128)}, f32[4,512]{1,0:T(4,128)}, ...) | async-done | bytes 74800 | tf_op jit(solution)/shard_map/psum | solution.py:346
  (959 shorter events, 720.5 us)
Async XLA Ops:
  7.2 55.3 %copy-start = (bf16[1024,4]{0,1:T(4,128)(2,1)S(1)}, bf16[1024,4]{0,1:T(4,128)(2,1)}, u32[]{:S(2)}) copy-start(bf16[1024,4]{0,1:T(4,128)(2,1)} %param.34) | copy-start | bytes 24580
  7.2 55.3 %all-gather.11.cloned.1.call-start = ((), (), s32[]{:S(2)}) async-start(), calls=%async_computation.12 | async-start | bytes 3145728 | tf_op jit(solution)/shard_map/all_gather | solution.py:247
  8.8 32.7 %copy-start.115 = (bf16[64,256]{1,0:T(8,128)(2,1)S(1)}, bf16[64,256]{1,0:T(8,128)(2,1)}, u32[]{:S(2)}) copy-start(bf16[64,256]{1,0:T(8,128)(2,1)} %param.31) | copy-start | bytes 98308
  8.8 51.5 %copy-start.164 = (f32[4]{0:T(128)S(1)}, f32[4]{0:T(128)}, u32[]{:S(2)}) copy-start(f32[4]{0:T(128)} %param.39) | copy-start | bytes 52
  8.8 51.6 %copy-start.170 = (f32[4]{0:T(128)S(1)}, f32[4]{0:T(128)}, u32[]{:S(2)}) copy-start(f32[4]{0:T(128)} %param.40) | copy-start | bytes 52
  8.9 51.7 %copy-start.142 = (f32[256]{0:T(256)S(1)}, f32[256]{0:T(256)}, u32[]{:S(2)}) copy-start(f32[256]{0:T(256)} %param.41) | copy-start | bytes 3076
  8.9 52.2 %copy-start.150 = (f32[4,1024]{1,0:T(4,128)S(1)}, f32[4,1024]{1,0:T(4,128)}, u32[]{:S(2)}) copy-start(f32[4,1024]{1,0:T(4,128)} %param.38) | copy-start | bytes 49156
  8.9 52.9 %copy-start.156 = (f32[4,512]{1,0:T(4,128)S(1)}, f32[4,512]{1,0:T(4,128)}, u32[]{:S(2)}) copy-start(f32[4,512]{1,0:T(4,128)} %param.37) | copy-start | bytes 24580
  8.9 52.9 %copy-start.157 = (f32[4,512]{1,0:T(4,128)S(1)}, f32[4,512]{1,0:T(4,128)}, u32[]{:S(2)}) copy-start(f32[4,512]{1,0:T(4,128)} %param.36) | copy-start | bytes 24580
  11.5 93.0 %all-gather.13.cloned.1.call-start = ((), (), s32[]{:S(2)}) async-start(), calls=%async_computation.13 | async-start | bytes 1114112 | tf_op jit(solution)/shard_map/all_gather | solution.py:217
  12.2 346.0 %all-gather.15.cloned.1.call-start = ((), (), s32[]{:S(2)}) async-start(), calls=%async_computation.14 | async-start | bytes 1114112 | tf_op jit(solution)/shard_map/all_gather | solution.py:218
  12.9 351.1 %all-gather.17.cloned.1.call-start = ((), (), s32[]{:S(2)}) async-start(), calls=%async_computation.15 | async-start | bytes 1114112 | tf_op jit(solution)/shard_map/all_gather | solution.py:219
  13.5 385.6 %reduce-scatter.13.cloned.1.call-start = ((), (), s32[]{:S(2)}) async-start(), calls=%async_computation.16 | async-start | bytes 3145728 | tf_op jit(solution)/shard_map/reduce_scatter | solution.py:260
  16.9 52.0 %copy-start.92 = (f32[1,1024]{1,0:T(1,128)}, f32[1,1024]{1,0:T(1,128)S(1)}, u32[]{:S(2)}) copy-start(f32[1,1024]{1,0:T(1,128)S(1)} %get-tuple-element.745) | copy-start | bytes 12292
  41.5 26.6 %copy-start.57 = (bf16[1024,256]{1,0:T(8,128)(2,1)}, bf16[1024,256]{1,0:T(8,128)(2,1)S(1)}, u32[]{:S(2)}) copy-start(bf16[1024,256]{1,0:T(8,128)(2,1)S(1)} %all_gather.47) | copy-start | bytes 1572868
  66.1 37.7 %copy-start.70 = (f32[16,2,64]{2,0,1:T(8,128)}, f32[16,2,64]{2,0,1:T(8,128)S(1)}, u32[]{:S(2)}) copy-start(f32[16,2,64]{2,0,1:T(8,128)S(1)} %reduce_window_sum.29) | copy-start | bytes 24580
  104.5 13.7 copy-start.77
  368.2 31.0 %copy-start.9 = (bf16[512,1024]{1,0:T(8,128)(2,1)S(1)}, bf16[512,1024]{1,0:T(8,128)(2,1)}, u32[]{:S(2)}) copy-start(bf16[512,1024]{1,0:T(8,128)(2,1)} %param.26) | copy-start | bytes 3145732
  368.2 32.9 %copy-start.103 = (f32[1024]{0:T(1024)S(1)}, f32[1024]{0:T(1024)}, u32[]{:S(2)}) copy-start(f32[1024]{0:T(1024)} %param.43) | copy-start | bytes 12292
  368.2 77.8 %all-gather.21.cloned.1.call-start = ((), (), s32[]{:S(2)}) async-start(), calls=%async_computation.18 | async-start | bytes 3063808 | tf_op jit(solution)/shard_map/all_gather | solution.py:220
  368.8 110.3 %all-gather.19.cloned.1.call-start = ((), (), s32[]{:S(2)}) async-start(), calls=%async_computation.17 | async-start | bytes 3145728 | tf_op jit(solution)/shard_map/all_gather | solution.py:265
  369.6 290.0 %copy-start.101 = (f32[512]{0:T(512)}, f32[512]{0:T(512)S(1)}, u32[]{:S(2)}) copy-start(f32[512]{0:T(512)S(1)} %get-tuple-element.702) | copy-start | bytes 6148
  401.1 258.4 %copy-start.110 = (f32[512]{0:T(512)}, f32[512]{0:T(512)S(1)}, u32[]{:S(2)}) copy-start(f32[512]{0:T(512)S(1)} %add_rsqrt_fusion.2) | copy-start | bytes 6148
  402.6 123.4 %all-gather.23.cloned.1.call-start = ((), (), s32[]{:S(2)}) async-start(), calls=%async_computation.19 | async-start | bytes 3063808 | tf_op jit(solution)/shard_map/all_gather | solution.py:221
  403.3 155.8 %all-gather.27.cloned.1.call-start = ((), (), s32[]{:S(2)}) async-start(), calls=%async_computation.22 | async-start | bytes 3145728 | tf_op jit(solution)/shard_map/all_gather | solution.py:300
  405.8 200.1 %all-gather.25.cloned.1.call-start = ((), (), s32[]{:S(2)}) async-start(), calls=%async_computation.20 | async-start | bytes 3063808 | tf_op jit(solution)/shard_map/all_gather | solution.py:222
  406.4 250.1 %reduce-scatter.17.cloned.1.call-start = ((), (), s32[]{:S(2)}) async-start(), calls=%async_computation.23 | async-start | bytes 3145728 | tf_op jit(solution)/shard_map/reduce_scatter | solution.py:310
  605.9 11.7 copy-start.166
  626.2 68.7 %all-gather.29.cloned.1.call-start = ((), (), s32[]{:S(2)}) async-start(), calls=%async_computation.24 | async-start | bytes 3145728 | tf_op jit(solution)/shard_map/all_gather | solution.py:319
  661.6 508.5 %reduce-scatter.19.cloned.1.call-start = ((), (), s32[]{:S(2)}) async-start(), calls=%async_computation.25 | async-start | bytes 3145728 | tf_op jit(solution)/shard_map/reduce_scatter | solution.py:329
  667.8 27.0 %copy-start.155 = (f32[1,2,2,128]{3,1,2,0:T(2,128)S(1)}, f32[1,2,2,128]{3,1,2,0:T(2,128)}, u32[]{:S(2)}) copy-start(f32[1,2,2,128]{3,1,2,0:T(2,128)} %copy.540) | copy-start | bytes 6148
  718.2 270.5 %copy-start.24 = (f32[16,64,2,256]{3,2,1,0:T(2,128)S(1)}, f32[16,64,2,256]{3,2,1,0:T(2,128)}, u32[]{:S(2)}) copy-start(f32[16,64,2,256]{3,2,1,0:T(2,128)} %reshape.495) | copy-start | bytes 6291460
  1116.0 66.0 %reduce-scatter.15.cloned.1.call-start = ((), (), s32[]{:S(2)}) async-start(), calls=%async_computation.21 | async-start | bytes 3145728 | tf_op jit(solution)/shard_map/reduce_scatter | solution.py:275
  1123.6 119.9 %reduce-scatter.23.cloned.1.call-start = ((), (), s32[]{:S(2)}) async-start(), calls=%async_computation.27 | async-start | bytes 1114112 | tf_op jit(solution)/shard_map/reduce_scatter | solution.py:336
  1127.0 177.5 %reduce-scatter.21.cloned.1.call-start = ((), (), s32[]{:S(2)}) async-start(), calls=%async_computation.26 | async-start | bytes 1114112 | tf_op jit(solution)/shard_map/reduce_scatter | solution.py:335
  1128.9 260.5 %reduce-scatter.31.cloned.1.call-start = ((), (), s32[]{:S(2)}) async-start(), calls=%async_computation.31 | async-start | bytes 6127616 | tf_op jit(solution)/shard_map/reduce_scatter | solution.py:340
  1137.3 337.2 %reduce-scatter.33.cloned.1.call-start = ((), (), s32[]{:S(2)}) async-start(), calls=%async_computation.32 | async-start | bytes 6127616 | tf_op jit(solution)/shard_map/reduce_scatter | solution.py:341
  1146.1 413.7 %reduce-scatter.35.cloned.1.call-start = ((), (), s32[]{:S(2)}) async-start(), calls=%async_computation.33 | async-start | bytes 6127616 | tf_op jit(solution)/shard_map/reduce_scatter | solution.py:342
  1154.6 470.2 %reduce-scatter.29.cloned.1.call-start = ((), (), s32[]{:S(2)}) async-start(), calls=%async_computation.30 | async-start | bytes 2228224 | tf_op jit(solution)/shard_map/reduce_scatter | solution.py:339
  1160.4 529.8 %reduce-scatter.25.cloned.1.call-start = ((), (), s32[]{:S(2)}) async-start(), calls=%async_computation.28 | async-start | bytes 2228224 | tf_op jit(solution)/shard_map/reduce_scatter | solution.py:337
  1164.2 590.8 %reduce-scatter.27.cloned.1.call-start = ((), (), s32[]{:S(2)}) async-start(), calls=%async_computation.29 | async-start | bytes 2228224 | tf_op jit(solution)/shard_map/reduce_scatter | solution.py:338
  1168.1 719.6 %all-reduce.34.cloned.1.call-start = ((), (), s32[]{:S(2)}) async-start(), calls=%async_computation.34 | async-start | bytes 151552 | tf_op jit(solution)/shard_map/psum | solution.py:346
  1169.6 12.5 copy-start.102
  1169.6 12.4 copy-start.104
  1169.6 12.4 copy-start.111
  1169.6 12.4 copy-start.129
  1170.1 12.0 copy-start.28
  1170.1 12.0 copy-start.50
  (166 other events, 610.6 us)
Sparse Core Ops, SparseCore 0:
  11.6 35.8 all-gather.10
  49.6 37.9 all-gather.12
  89.8 36.8 all-gather.14
  128.7 36.8 all-gather.16
  368.3 30.7 reduce-scatter.12
  401.5 44.3 all-gather.20
  447.6 31.4 all-gather.18
  481.6 44.3 all-gather.22
  527.6 31.4 all-gather.26
  561.5 44.3 all-gather.24
  626.3 30.1 reduce-scatter.16
  661.7 33.1 all-gather.28
  1116.1 31.8 reduce-scatter.18
  1150.2 31.8 reduce-scatter.14
  1186.1 57.3 reduce-scatter.22
  1248.0 56.3 reduce-scatter.20
  1308.8 80.5 reduce-scatter.30
  1393.7 80.7 reduce-scatter.32
  1479.0 80.7 reduce-scatter.34
  1564.0 60.7 reduce-scatter.28
  1629.6 60.5 reduce-scatter.24
  1694.5 60.5 reduce-scatter.26
  1764.3 123.3 all-reduce.33
where the time goes:
time: 1920 us; the launch traced here: 1910 us
  waiting for transfers between devices  982 us (51%)
  matrix products  573 us (30%)
  local copies, waits for them, and re-layouts  177 us (9%)
  other arithmetic  113 us (6%)
  blocking collectives  43.4 us (2%)
    dot_general x234, matrix products, head_dot_product(): return jnp.einsum(formula, left, right, precision=PRECISE)  451 us
    psum x1, waiting for transfers between devices, on_device(): lax.psum((mix_gain_part, widen(weight_grads[4], decay_weight), widen(weig...  133 us
    reduce_scatter x1, waiting for transfers between devices, on_device(): lax.psum_scatter(ffn_sums[2], 'dp', scatter_dimension=1, tiled=True)  85.3 us
    reduce_scatter x1, waiting for transfers between devices, on_device(): lax.psum_scatter(ffn_sums[1], 'dp', scatter_dimension=0, tiled=True)  85.1 us
    reduce_scatter x1, waiting for transfers between devices, on_device(): lax.psum_scatter(ffn_sums[0], 'dp', scatter_dimension=0, tiled=True)  84.9 us
    reduce_scatter x1, waiting for transfers between devices, on_device(): lax.psum_scatter(weight_grads[2], 'dp', scatter_dimension=0, tiled=True)  65.4 us
    reduce_scatter x1, waiting for transfers between devices, on_device(): lax.psum_scatter(out_grad, 'dp', scatter_dimension=1, tiled=True)  65 us
    reduce_scatter x1, waiting for transfers between devices, on_device(): lax.psum_scatter(weight_grads[3], 'dp', scatter_dimension=0, tiled=True)  64.9 us
  transfers between devices with their start and end apart: 23, of which 18 were waited for; matrix products, arithmetic and copies ran while one was open for 20% of the time, Pallas kernels for 0%

commit v1 on v0

v1 whole, which is shorter than its diff:
```python
from functools import partial
import math

import jax
import jax.numpy as jnp
from jax import lax
from jax.sharding import PartitionSpec as P

DK = 128
DV = 256
KW = 4
SPAN = 64


EPS = 1e-06
PRECISE = lax.Precision.HIGHEST


def layout(seq_lengths, seq_owner, device, row_count):
    owned = seq_owner == device
    own_lengths = jnp.where(owned, seq_lengths, 0)
    offsets = jnp.cumsum(own_lengths) - own_lengths
    loaded = jnp.sum(own_lengths)
    span_starts = jnp.arange(row_count // SPAN, dtype=jnp.int32) * SPAN
    begins = jnp.any(
        (offsets[None, :] == span_starts[:, None]) & (own_lengths[None, :] > 0), axis=1
    )
    resets = begins | (span_starts == loaded)
    within = jnp.arange(SPAN, dtype=jnp.int32)
    keep_masks = jnp.stack(
        [
            jnp.logical_not(resets[:, None] & (within[None, :] < offset)).reshape(row_count)
            for offset in range(KW)
        ]
    ).astype(jnp.float32)
    valid_rows = (jnp.arange(row_count, dtype=jnp.int32) < loaded).astype(jnp.float32)
    return (keep_masks, resets, valid_rows)


def head_dot_product(formula, left, right):
    return jnp.einsum(formula, left, right, precision=PRECISE)


def across_rows(left, right):
    return lax.dot_general(
        left, right, (((0,), (0,)), ((), ())), preferred_element_type=jnp.float32
    )


def against(left, right):
    return lax.dot_general(
        left, right, (((1,), (1,)), ((), ())), preferred_element_type=jnp.float32
    )


def rms_forward(values):
    inv_rms = lax.rsqrt(jnp.mean(values * values, -1, keepdims=True) + EPS)
    return (values * inv_rms, inv_rms)


def rms_backward(upstream, normed, inv_rms):
    return inv_rms * (upstream - normed * jnp.mean(upstream * normed, -1, keepdims=True))


def causal_conv(signal, filters, keep_masks):
    summed = signal * filters[0]
    for offset in range(1, KW):
        delayed = jnp.concatenate(
            [jnp.zeros((offset, signal.shape[1]), jnp.float32), signal[:-offset]], axis=0
        )
        summed = summed + delayed * filters[offset] * keep_masks[offset][:, None]
    return summed


def unit_norm(vectors):
    return vectors * lax.rsqrt(jnp.sum(vectors * vectors, -1, keepdims=True) + EPS)


def delta_rule(queries, keys_unit, values_in, decays, betas, resets):
    row_count, heads_local = decays.shape
    blocks = row_count // SPAN

    def blocked(tensor):
        return jnp.swapaxes(tensor.reshape((blocks, SPAN) + tensor.shape[1:]), 1, 2)

    query_blocks = blocked(queries)
    key_blocks = blocked(keys_unit)
    value_blocks = blocked(values_in)
    beta_blocks = blocked(betas)
    cumulative = jnp.cumsum(blocked(decays), axis=-1)
    gap_matrix = cumulative[..., :, None] - cumulative[..., None, :]
    lower_mask = jnp.tril(jnp.ones((SPAN, SPAN), jnp.float32))
    strict = lower_mask - jnp.eye(SPAN, dtype=jnp.float32)
    factor = jnp.exp(gap_matrix * lower_mask) * lower_mask
    key_gram = head_dot_product("bhik,bhjk->bhij", key_blocks, key_blocks)
    query_key = head_dot_product("bhik,bhjk->bhij", query_blocks, key_blocks)
    coupling = beta_blocks[..., :, None] * factor * strict * key_gram
    inverse = jnp.eye(SPAN, dtype=jnp.float32) - coupling
    powered = coupling
    for round_index in range(SPAN.bit_length() - 2):
        powered = head_dot_product("bhij,bhjk->bhik", powered, powered)
        inverse = inverse + head_dot_product("bhij,bhjk->bhik", inverse, powered)
    growth = jnp.exp(cumulative)
    span_end = cumulative[..., -1:]
    value_part = head_dot_product("bhij,bhjv->bhiv", inverse, beta_blocks[..., None] * value_blocks)
    key_part = head_dot_product(
        "bhij,bhjk->bhik", inverse, (beta_blocks * growth)[..., None] * key_blocks
    )
    query_grown = growth[..., None] * query_blocks
    key_tail = jnp.exp(span_end - cumulative)[..., None] * key_blocks
    tail_decay = jnp.exp(span_end)
    mixing_all = factor * query_key

    def advance(state, inputs):
        (
            restart,
            projected_value,
            projected_key,
            query_gathered_rows,
            key_at_step,
            tail_decay_cumulative,
            token_mixer_output,
        ) = inputs
        starting_state = jnp.where(restart, jnp.zeros_like(state), state)
        written_value_rows = projected_value - head_dot_product(
            "dqw,dwy->dqy", projected_key, starting_state
        )
        block_result_output = head_dot_product(
            "dqw,dwy->dqy", query_gathered_rows, starting_state
        ) + head_dot_product("mgy,myt->mgt", token_mixer_output, written_value_rows)
        state_after_update = tail_decay_cumulative[:, :, None] * starting_state + head_dot_product(
            "gny,gnr->gyr", key_at_step, written_value_rows
        )
        return (state_after_update, block_result_output)

    initial = jnp.zeros((heads_local, DK, DV), jnp.float32)
    final_state, outputs = lax.scan(
        advance,
        initial,
        (resets, value_part, key_part, query_grown, key_tail, tail_decay, mixing_all),
    )
    return jnp.swapaxes(outputs, 1, 2).reshape(row_count, heads_local, DV)


def packed_mixer(projections, smalls, keep_masks, resets):
    proj_q, proj_k, proj_v, proj_gate, proj_decay, proj_beta = projections
    query_filter, key_filter, value_filter, decay_log, decay_bias, head_gain = smalls
    row_count = proj_q.shape[0]
    heads_local = decay_log.shape[0]
    queries = unit_norm(
        jax.nn.silu(causal_conv(proj_q, query_filter, keep_masks)).reshape(
            row_count, heads_local, DK
        )
    ) * (1.0 / math.sqrt(DK))
    keys_unit = unit_norm(
        jax.nn.silu(causal_conv(proj_k, key_filter, keep_masks)).reshape(row_count, heads_local, DK)
    )
    values_in = jax.nn.silu(causal_conv(proj_v, value_filter, keep_masks)).reshape(
        row_count, heads_local, DV
    )
    betas = jax.nn.sigmoid(proj_beta)
    decays = -jnp.exp(decay_log) * jax.nn.softplus(proj_decay + decay_bias)
    outputs = delta_rule(queries, keys_unit, values_in, decays, betas, resets)
    normed = outputs * lax.rsqrt(jnp.mean(outputs * outputs, -1, keepdims=True) + EPS)
    gated = normed * head_gain * jax.nn.silu(proj_gate.reshape(row_count, heads_local, DV))
    return gated.reshape(row_count, heads_local * DV)


def swap_halves(array):
    return lax.ppermute(array, "mp", [(0, 1), (1, 0)])


def dp_total(array):
    count = lax.axis_size("dp")
    step = 1
    while step < count:
        array = array + lax.ppermute(array, "dp", [(i, i ^ step) for i in range(count)])
        step *= 2
    return array


def in_order(own, other, model_index, axis):
    first = jnp.where(model_index == 0, own, other)
    second = jnp.where(model_index == 0, other, own)
    return jnp.concatenate([first, second], axis=axis)


def on_device(
    block_input,
    seq_lengths,
    seq_owner,
    mix_gain,
    query_weight,
    key_weight,
    value_weight,
    gate_weight,
    decay_weight,
    beta_weight,
    query_filter,
    key_filter,
    value_filter,
    decay_log,
    decay_bias,
    head_gain,
    out_weight,
    ffn_gain,
    ffn_gate,
    ffn_up,
    ffn_down,
    cotangent,
):
    bf16 = jnp.bfloat16
    f32 = jnp.float32
    local_rows, width = block_input.shape
    dp_index = lax.axis_index("dp")
    model_count = lax.axis_size("mp")
    model_index = lax.axis_index("mp")
    row_count = local_rows * model_count
    keep_masks, resets, valid_rows = layout(seq_lengths, seq_owner, dp_index, row_count)
    valid_all = valid_rows[:, None]
    heads_local = decay_log.shape[0] // model_count
    qk_cols = heads_local * DK
    v_cols = heads_local * DV
    ff_cols = ffn_gate.shape[1]
    shard_rows = query_weight.shape[0]
    proj_cols = 2 * qk_cols + 2 * v_cols

    def own_columns(array, col_count):
        return lax.dynamic_slice_in_dim(array, model_index * col_count, col_count, array.ndim - 1)

    def own_shard(array):
        return lax.dynamic_slice_in_dim(array, dp_index * shard_rows, shard_rows, 0)

    small_weight = jnp.concatenate(
        [own_columns(decay_weight, heads_local), own_columns(beta_weight, heads_local)], axis=1
    )
    small_weight = jnp.pad(small_weight, ((0, 0), (0, 128 - 2 * heads_local)))
    shard_mix = jnp.concatenate(
        [query_weight, key_weight, value_weight, gate_weight, own_shard(small_weight)], axis=1
    )
    mix_weight = lax.all_gather(shard_mix, "dp", axis=0, tiled=True)
    input_other = swap_halves(block_input)
    out_rows = out_weight.T
    out_other = swap_halves(out_rows)
    shard_rest = jnp.concatenate([out_rows, out_other, ffn_gate, ffn_up, ffn_down.T], axis=1)
    rest_weight = lax.all_gather(shard_rest, "dp", axis=0, tiled=True)
    out_both = rest_weight[:, : 2 * v_cols]
    ffn_in_weight = rest_weight[:, 2 * v_cols : 2 * v_cols + 2 * ff_cols]
    down_weight = rest_weight[:, 2 * v_cols + 2 * ff_cols :]
    cot_other = swap_halves(cotangent)

    smalls = (
        own_columns(query_filter, qk_cols),
        own_columns(key_filter, qk_cols),
        own_columns(value_filter, v_cols),
        own_columns(decay_log, heads_local),
        own_columns(decay_bias, heads_local),
        head_gain,
    )
    inputs_f = in_order(block_input, input_other, model_index, 0).astype(f32)
    cot_all = in_order(cotangent, cot_other, model_index, 0)
    normed1, inv_rms1 = rms_forward(inputs_f)
    mixed_in = (normed1 * mix_gain).astype(bf16)
    proj = jnp.dot(mixed_in, mix_weight, preferred_element_type=f32)
    cuts = (qk_cols, 2 * qk_cols, 2 * qk_cols + v_cols, proj_cols, proj_cols + heads_local)

    def split(array):
        return (
            array[:, : cuts[0]],
            array[:, cuts[0] : cuts[1]],
            array[:, cuts[1] : cuts[2]],
            array[:, cuts[2] : cuts[3]],
            array[:, cuts[3] : cuts[4]],
            array[:, cuts[4] : cuts[4] + heads_local],
        )

    gated, pullback = jax.vjp(
        partial(packed_mixer, keep_masks=keep_masks, resets=resets), split(proj), smalls
    )
    gated_b = gated.astype(bf16)
    gated_both = jnp.concatenate([gated_b, swap_halves(gated_b)], axis=1)
    resid = inputs_f + valid_all * against(gated_both, out_both)
    normed2, inv_rms2 = rms_forward(resid)
    ffn_in = (normed2 * ffn_gain).astype(bf16)
    pre = jnp.dot(ffn_in, ffn_in_weight, preferred_element_type=f32)
    gate_pre, up_pre = pre[:, :ff_cols], pre[:, ff_cols:]
    sigmoid_gate = jax.nn.sigmoid(gate_pre)
    activated = gate_pre * sigmoid_gate
    hidden = (activated * up_pre).astype(bf16)
    cot_masked = cot_all * valid_all.astype(bf16)
    hidden_grad = jnp.dot(cot_masked, down_weight, preferred_element_type=f32)
    gate_grad_pre = (
        hidden_grad * up_pre * sigmoid_gate * (1.0 + gate_pre * (1.0 - sigmoid_gate))
    ).astype(bf16)
    up_grad_pre = (hidden_grad * activated).astype(bf16)
    pre_grad = jnp.concatenate([gate_grad_pre, up_grad_pre], axis=1)
    ffn_in_part = against(pre_grad, ffn_in_weight)
    ffn_in_sent = ffn_in_part.astype(bf16)
    ffn_in_grad = ffn_in_sent.astype(f32) + swap_halves(ffn_in_sent).astype(f32)

    def own_half(array):
        return lax.dynamic_slice_in_dim(array, model_index * local_rows, local_rows, 0)

    def other_half(array):
        return lax.dynamic_slice_in_dim(array, (1 - model_index) * local_rows, local_rows, 0)

    ffn_part = against(hidden, down_weight)
    ffn_sum = own_half(ffn_part) + swap_halves(other_half(ffn_part).astype(bf16)).astype(f32)
    block_output = (own_half(resid) + own_half(valid_all) * ffn_sum).astype(bf16)
    rest_grads = jnp.concatenate(
        [across_rows(ffn_in, pre_grad).astype(bf16), across_rows(cot_masked, hidden).astype(bf16)],
        axis=1,
    )
    ffn_shard = lax.psum_scatter(rest_grads, "dp", scatter_dimension=0, tiled=True)
    ffn_gain_part = jnp.sum(ffn_in_part * normed2, 0)
    resid_grad = cot_all.astype(f32) + rms_backward(ffn_in_grad * ffn_gain, normed2, inv_rms2)
    mix_cot = (resid_grad * valid_all).astype(bf16)
    gated_grad = jnp.dot(mix_cot, out_both[:, :v_cols], preferred_element_type=f32)
    proj_grads, small_grads = pullback(gated_grad)
    pad = jnp.zeros((row_count, 128 - 2 * heads_local), f32)
    proj_grad = jnp.concatenate(list(proj_grads) + [pad], axis=1).astype(bf16)
    mix_grads = jnp.concatenate(
        [
            across_rows(mixed_in, proj_grad[:, :proj_cols]).astype(bf16),
            across_rows(mix_cot, gated_b).astype(bf16),
        ],
        axis=1,
    )
    mix_shard = lax.psum_scatter(mix_grads, "dp", scatter_dimension=0, tiled=True)
    rate_grads = across_rows(proj_grad[:, proj_cols:], mixed_in)[: 2 * heads_local]
    mix_in_part = against(proj_grad, mix_weight)
    mix_in_sum = own_half(mix_in_part) + swap_halves(
        other_half(mix_in_part).astype(bf16)
    ).astype(f32)
    mix_gain_part = jnp.sum(mix_in_part * normed1, 0)
    input_grad = own_half(resid_grad) + rms_backward(
        mix_in_sum * mix_gain, own_half(normed1), own_half(inv_rms1)
    )
    common = jnp.concatenate(
        [mix_gain_part, ffn_gain_part, small_grads[5], jnp.zeros((width - DV,), f32)]
    ).reshape(3, width)
    tail_row = jnp.concatenate(
        [small_grads[3], small_grads[4], jnp.zeros((width - 2 * heads_local,), f32)]
    )
    split_rows = jnp.concatenate(
        [
            rate_grads,
            small_grads[0].reshape(-1, width),
            small_grads[1].reshape(-1, width),
            small_grads[2].reshape(-1, width),
            tail_row[None],
        ],
        axis=0,
    )
    totals = dp_total(jnp.concatenate([common, split_rows], axis=0))
    totals_other = swap_halves(totals)
    common = totals[:3] + totals_other[:3]
    lower = jnp.where(model_index == 0, totals, totals_other)[3:]
    upper = jnp.where(model_index == 0, totals_other, totals)[3:]

    def joined(start, rows, cols):
        return jnp.concatenate(
            [
                lower[start : start + rows].reshape(-1, cols),
                upper[start : start + rows].reshape(-1, cols),
            ],
            axis=1,
        )

    q_rows = KW * qk_cols // width
    v_rows = KW * v_cols // width
    at_q = 2 * heads_local
    at_k = at_q + q_rows
    at_v = at_k + q_rows
    at_tail = at_v + v_rows

    def rate_weight_grad(start):
        return jnp.concatenate(
            [lower[start : start + heads_local], upper[start : start + heads_local]], axis=0
        ).T

    def rate_grad(start):
        return jnp.concatenate(
            [
                lower[at_tail, start : start + heads_local],
                upper[at_tail, start : start + heads_local],
            ]
        )

    mix_shard = mix_shard.astype(f32)
    ffn_shard = ffn_shard.astype(f32)
    return (
        block_output,
        input_grad,
        common[0],
        mix_shard[:, : cuts[0]],
        mix_shard[:, cuts[0] : cuts[1]],
        mix_shard[:, cuts[1] : cuts[2]],
        mix_shard[:, cuts[2] : cuts[3]],
        rate_weight_grad(0),
        rate_weight_grad(heads_local),
        joined(at_q, q_rows, qk_cols),
        joined(at_k, q_rows, qk_cols),
        joined(at_v, v_rows, v_cols),
        rate_grad(0),
        rate_grad(heads_local),
        common[2, :DV],
        mix_shard[:, proj_cols:].T,
        common[1],
        ffn_shard[:, :ff_cols],
        ffn_shard[:, ff_cols : 2 * ff_cols],
        ffn_shard[:, 2 * ff_cols :].T,
    )


def solution(mesh):
    in_specs = (
        P(("dp", "mp"), None),
        P(),
        P(),
        P(),
        P("dp", "mp"),
        P("dp", "mp"),
        P("dp", "mp"),
        P("dp", "mp"),
        P(),
        P(),
        P(),
        P(),
        P(),
        P(),
        P(),
        P(),
        P("mp", "dp"),
        P(),
        P("dp", "mp"),
        P("dp", "mp"),
        P("mp", "dp"),
        P(("dp", "mp"), None),
    )
    out_specs = (
        P(("dp", "mp"), None),
        P(("dp", "mp"), None),
        P(),
        P("dp", "mp"),
        P("dp", "mp"),
        P("dp", "mp"),
        P("dp", "mp"),
        P(),
        P(),
        P(),
        P(),
        P(),
        P(),
        P(),
        P(),
        P("mp", "dp"),
        P(),
        P("dp", "mp"),
        P("dp", "mp"),
        P("mp", "dp"),
    )
    return jax.shard_map(
        on_device, mesh=mesh, in_specs=in_specs, out_specs=out_specs, check_vma=False
    )
```

time: 1920 us -> 1130 us (0.59)
  waiting for transfers between devices: 982 us -> 187 us
  local copies, waits for them, and re-layouts: 177 us -> 243 us
  matrix products: 573 us -> 510 us
  blocking collectives: 43.4 us -> 0 us
  other arithmetic: 113 us -> 142 us
    reduce_scatter x12 -> x2, waiting for transfers between devices: 637 us -> 68 us  [the longest x1 68 us: on_device(): lax.psum_scatter(rest_grads, 'dp', scatter_dimension=0, tiled=True)]
    all_gather x10 -> x2, waiting for transfers between devices: 208 us -> 16.5 us  [the longest x1 16.5 us: on_device(): mix_weight = lax.all_gather(shard_mix, 'dp', axis=0, tiled=True)]
    psum x1 -> x0, waiting for transfers between devices: 133 us -> none  [on_device(): lax.psum((mix_gain_part, widen(weight_grads[4], decay_weight), widen(weig...]
    ppermute x0 -> x12, waiting for transfers between devices: none -> 102 us  [the longest x8 94 us: swap_halves(): return lax.ppermute(array, 'mp', [(0, 1), (1, 0)])]
    all_gather x2 -> x0, blocking collectives: 43.4 us -> none  [the longest x1 24.6 us: on_device(): lax.all_gather(query_weight, 'dp', axis=0, tiled=True)]
    dynamic_slice x32 -> x48, local copies, waits for them, and re-layouts: 28.6 us -> 54.6 us  [delta_rule(): lax.scan(advance, initial, (resets, value_part, key_part, query_grown, ke...]
    dot_general x10 -> x5, matrix products: 39.5 us -> 18.9 us  [across_rows(): lax.dot_general(left, right, (((0,), (0,)), ((), ())), preferred_element_...]
    dot_general x10 -> x4, matrix products: 41.8 us -> 29.7 us  [the longest x1 9.88 us: on_device(): pre = jnp.dot(ffn_in, ffn_in_weight, preferred_element_type=f32)]
  transfers between devices with their start and end apart: 23 -> 16, of which waited for: 18 -> 10; matrix products, arithmetic and copies ran while one was open for 20% -> 35% of each run, Pallas kernels for 0% -> 0%
where the time goes in v1:
time: 1130 us; the launch traced here: 1120 us
  matrix products  510 us (45%)
  local copies, waits for them, and re-layouts  243 us (22%)
  waiting for transfers between devices  187 us (17%)
  other arithmetic  142 us (13%)
  between operations  17.3 us (2%)
  starting transfers between devices  16.6 us (1%)
    dot_general x234, matrix products, head_dot_product(): return jnp.einsum(formula, left, right, precision=PRECISE)  432 us
    ppermute x8, waiting for transfers between devices, swap_halves(): return lax.ppermute(array, 'mp', [(0, 1), (1, 0)])  94 us
    reduce_scatter x1, waiting for transfers between devices, on_device(): lax.psum_scatter(rest_grads, 'dp', scatter_dimension=0, tiled=True)  68 us
    dynamic_slice x48, local copies, waits for them, and re-layouts, delta_rule(): lax.scan(advance, initial, (resets, value_part, key_part, query_grown, ke...  54.6 us
    unnamed x459, local copies, waits for them, and re-layouts  46.3 us
    dynamic_update_slice x48, local copies, waits for them, and re-layouts, delta_rule(): lax.scan(advance, initial, (resets, value_part, key_part, query_grown, ke...  39 us
    dot_general x4, matrix products, against(): lax.dot_general(left, right, (((1,), (1,)), ((), ())), preferred_element_...  29.5 us
  transfers between devices with their start and end apart: 16, of which 10 were waited for; matrix products, arithmetic and copies ran while one was open for 35% of the time, Pallas kernels for 0%

profile of v1, /device:TPU:0, one launch (start us, length us, event | category | flops | bytes accessed | tf_op | source)
XLA Modules:
  0.0 1116.7 jit_solution(8815145519043716876)
XLA Ops:
  12.4 3.0 collective-permute-start.2
  26.0 17.2 %collective-permute-done = bf16[512,1024]{0,1:T(8,128)(2,1)} collective-permute-done((bf16[512,1024]{0,1:T(8,128)(2,1)S(1)}, bf16[512,1024]{0,1:T(8,128)(2,1)}, u32[]{:S(2)}, u32[]{:S(2)}) %collective-permute-start) | collective-permute-done | bytes 1048608 | tf_op jit(solution)/shard_map/ppermute | solution.py:170
  45.0 16.5 %all-gather.3.cloned.1.call-done = bf16[1024,1664]{1,0:T(8,128)(2,1)} async-done(((bf16[64,1664]{1,0:T(8,128)(2,1)}), bf16[1024,1664]{1,0:T(8,128)(2,1)}) %all-gather.3.cloned.1.call-update) | async-done | bytes 3407888 | tf_op jit(solution)/shard_map/all_gather | solution.py:241
  61.6 6.1 fusion.213
  71.9 3.3 fusion.212
  81.3 3.1 slice.311
  84.4 3.2 slice.310
  87.6 3.1 slice.309
  121.4 4.6 fusion.98
  126.0 3.6 reshape.548
  130.5 3.7 convolution_add_fusion.10
  134.2 3.7 fusion.100
  137.9 3.7 fusion.143
  147.5 4.7 fusion.138
  155.4 201.6 %while.46 = (s32[]{:T(128)}, f32[2,128,256]{2,1,0:T(8,128)S(1)}, f32[16,2,64,256]{3,1,2,0:T(2,128)}, f32[16,2,128,256]{3,2,1,0:T(8,128)}, f32[16,2,64,256]{3,2,1...) while((s32[]{:T(128)}, f32[2,128,256]{2,1,0:T(8,128)S(1)}, ...), condition=%wide.region_8.9_spmd.clone, body=%wide.region_7.8_spmd.clone.sunk | while | flops 176881664 | bytes 3150555 | solution.py:137
  357.0 3.2 copy.754
  369.1 3.8 fusion.222
  375.7 3.0 broadcast_select_fusion.1
  378.7 19.6 %collective-permute-done.1 = bf16[1024,512]{1,0:T(8,128)(2,1)} collective-permute-done((bf16[1024,512]{1,0:T(8,128)(2,1)S(1)}, bf16[1024,512]{1,0:T(8,128)(2,1)}, u32[]{:S(2)}, u32[]{:S(2)}) %collective-permute-start.1) | collective-permute-done | bytes 1048608 | tf_op jit(solution)/shard_map/ppermute | solution.py:170
  398.3 5.5 multiply_reduce_fusion.3
  404.2 9.9 fusion.68
  414.1 9.9 multiply_convert_fusion.1
  424.0 8.1 fusion.235
  435.9 3.5 reshape.553
  439.4 39.9 %collective-permute-done.5 = bf16[1024,1024]{0,1:T(8,128)(2,1)} collective-permute-done((bf16[1024,1024]{0,1:T(8,128)(2,1)}, bf16[1024,1024]{0,1:T(8,128)(2,1)}, u32[]{:S(2)}, u32[]{:S(2)}) %collective-permute-start.5) | collective-permute-done | bytes 2097184 | tf_op jit(solution)/shard_map/ppermute | solution.py:170
  479.4 6.8 multiply_reduce_fusion
  486.2 3.4 multiply_add_fusion
  491.6 3.9 fusion.116
  495.5 3.7 reshape.552
  499.2 8.3 fusion.94
  512.4 6.4 fusion.83
  525.5 290.2 %while.47 = (s32[]{:T(128)}, f32[2,128,256]{2,1,0:T(8,128)S(1)}, f32[16,2,64,256]{3,2,1,0:T(8,128)}, f32[16,2,64,128]{3,2,1,0:T(8,128)}, f32[16,2,64,128]{3,2,1,...) while((s32[]{:T(128)}, f32[2,128,256]{2,1,0:T(8,128)S(1)}, ...), condition=%wide.region_15.16_spmd.clone, body=%wide.region_13.15_spmd.clone.sunk | while | flops 353075200 | bytes 4987679 | solution.py:137
  815.8 3.5 fusion.142
  819.3 4.0 fusion.105
  875.0 3.8 broadcast_multiply_fusion.3
  896.1 3.2 bitcast_multiply_fusion.1
  916.3 3.5 convolution_convert_fusion.2
  924.0 5.6 convolution_convert_fusion.1
  929.7 6.6 convolution_convert_fusion
  936.3 3.8 pad_maximum_fusion
  942.1 5.3 fusion.80
  962.7 6.2 concatenate.110
  969.1 10.6 multiply_reduce_fusion.1
  983.3 3.6 collective-permute-done.8
  989.6 3.6 collective-permute-done.9
  994.6 3.2 add_convert_fusion.1
  1009.1 16.9 %collective-permute-done.6 = bf16[512,1024]{0,1:T(8,128)(2,1)S(1)} collective-permute-done((bf16[512,1024]{0,1:T(8,128)(2,1)S(1)}, bf16[512,1024]{0,1:T(8,128)(2,1)S(1)}, u32[]{:S(2)}, u32[]{:S(2)}) %collective-permute-start.6) | collective-permute-done | bytes 1048608 | tf_op jit(solution)/shard_map/ppermute | solution.py:170
  1038.9 68.0 %reduce-scatter.5.cloned.1.call-done = bf16[64,4224]{1,0:T(8,128)(2,1)} async-done(((bf16[1024,4224]{1,0:T(8,128)(2,1)}), bf16[64,4224]{1,0:T(8,128)(2,1)}) %reduce-scatter.5.cloned.1.call-update) | async-done | bytes 540688 | tf_op jit(solution)/shard_map/reduce_scatter | solution.py:314
  (1064 shorter events, 729.0 us)
Async XLA Ops:
  7.2 54.4 %all-gather.3.cloned.1.call-start = ((), (), s32[]{:S(2)}) async-start(), calls=%async_computation.2 | async-start | bytes 3620864 | tf_op jit(solution)/shard_map/all_gather | solution.py:241
  12.2 386.1 %all-gather.5.cloned.1.call-start = ((), (), s32[]{:S(2)}) async-start(), calls=%async_computation.3 | async-start | bytes 11419648 | tf_op jit(solution)/shard_map/all_gather | solution.py:246
  12.3 11.7 %copy-start.179 = (f32[256]{0:T(256)S(1)}, f32[256]{0:T(256)}, u32[]{:S(2)}) copy-start(f32[256]{0:T(256)} %param.41) | copy-start | bytes 3076
  12.3 11.8 %copy-start.141 = (bf16[512,64]{0,1:T(8,128)(2,1)S(1)}, bf16[512,64]{0,1:T(8,128)(2,1)}, u32[]{:S(2)}) copy-start(bf16[512,64]{0,1:T(8,128)(2,1)} %param.42) | copy-start | bytes 196612
  12.3 11.8 %copy-start.209 = (f32[4]{0:T(128)S(1)}, f32[4]{0:T(128)}, u32[]{:S(2)}) copy-start(f32[4]{0:T(128)} %param.39) | copy-start | bytes 52
  12.3 12.5 %copy-start.211 = (f32[4]{0:T(128)S(1)}, f32[4]{0:T(128)}, u32[]{:S(2)}) copy-start(f32[4]{0:T(128)} %param.40) | copy-start | bytes 52
  12.3 12.6 %copy-start.112 = (bf16[64,1408]{1,0:T(8,128)(2,1)S(1)}, bf16[64,1408]{1,0:T(8,128)(2,1)}, u32[]{:S(2)}) copy-start(bf16[64,1408]{1,0:T(8,128)(2,1)} %param.44) | copy-start | bytes 540676
  12.4 12.6 %copy-start.113 = (bf16[64,1408]{1,0:T(8,128)(2,1)S(1)}, bf16[64,1408]{1,0:T(8,128)(2,1)}, u32[]{:S(2)}) copy-start(bf16[64,1408]{1,0:T(8,128)(2,1)} %param.45) | copy-start | bytes 540676
  12.4 12.6 %collective-permute-start.2 = (bf16[64,512]{1,0:T(8,128)(2,1)}, bf16[64,512]{1,0:T(8,128)(2,1)S(1)}, u32[]{:S(2)}, u32[]{:S(2)}) collective-permute-start(bf16[64,512]{1,0:T(8,128)(2,1)} %bitcast.484), channel_id=1, source_target_pairs={{0,1},{1,0},{2,3},{3,2},{4,5},{5,4},{6,7},{7,6},{8,9},{9,8},{10,11... | collective-permute-start | bytes 196616 | tf_op jit(solution)/shard_map/ppermute | solution.py:170
  16.9 26.3 %collective-permute-start = (bf16[512,1024]{0,1:T(8,128)(2,1)S(1)}, bf16[512,1024]{0,1:T(8,128)(2,1)}, u32[]{:S(2)}, u32[]{:S(2)}) collective-permute-start(bf16[512,1024]{0,1:T(8,128)(2,1)S(1)} %copy.529), channel_id=1, source_target_pairs={{0,1},{1,0},{2,3},{3,2},{4,5},{5,4},{6,7},{7,6},{8,9},{9,8},{10,11... | collective-permute-start | bytes 3145736 | tf_op jit(solution)/shard_map/ppermute | solution.py:170
  18.4 357.2 %collective-permute-start.4 = (bf16[512,1024]{0,1:T(8,128)(2,1)}, bf16[512,1024]{0,1:T(8,128)(2,1)}, u32[]{:S(2)}, u32[]{:S(2)}) collective-permute-start(bf16[512,1024]{0,1:T(8,128)(2,1)} %copy.572), channel_id=1, source_target_pairs={{0,1},{1,0},{2,3},{3,2},{4,5},{5,4},{6,7},{7,6},{8,9},{9,8},{10,11... | collective-permute-start | bytes 3145736 | tf_op jit(solution)/shard_map/ppermute | solution.py:170
  23.3 45.0 %copy-start.164 = (f32[1,256]{1,0:T(1,128)}, f32[1,256]{1,0:T(1,128)S(1)}, u32[]{:S(2)}) copy-start(f32[1,256]{1,0:T(1,128)S(1)} %get-tuple-element.1031) | copy-start | bytes 3076
  23.3 45.0 %copy-start.166 = (f32[1,256]{1,0:T(1,128)}, f32[1,256]{1,0:T(1,128)S(1)}, u32[]{:S(2)}) copy-start(f32[1,256]{1,0:T(1,128)S(1)} %get-tuple-element.1033) | copy-start | bytes 3076
  23.3 45.0 %copy-start.168 = (f32[1,256]{1,0:T(1,128)}, f32[1,256]{1,0:T(1,128)S(1)}, u32[]{:S(2)}) copy-start(f32[1,256]{1,0:T(1,128)S(1)} %get-tuple-element.1032) | copy-start | bytes 3076
  23.3 45.0 %copy-start.170 = (f32[1,256]{1,0:T(1,128)}, f32[1,256]{1,0:T(1,128)S(1)}, u32[]{:S(2)}) copy-start(f32[1,256]{1,0:T(1,128)S(1)} %get-tuple-element.1003) | copy-start | bytes 3076
  23.3 45.0 %copy-start.172 = (f32[1,256]{1,0:T(1,128)}, f32[1,256]{1,0:T(1,128)S(1)}, u32[]{:S(2)}) copy-start(f32[1,256]{1,0:T(1,128)S(1)} %get-tuple-element.1001) | copy-start | bytes 3076
  23.3 45.0 %copy-start.174 = (f32[1,256]{1,0:T(1,128)}, f32[1,256]{1,0:T(1,128)S(1)}, u32[]{:S(2)}) copy-start(f32[1,256]{1,0:T(1,128)S(1)} %get-tuple-element.1002) | copy-start | bytes 3076
  23.3 45.0 %copy-start.180 = (f32[1,256]{1,0:T(1,128)}, f32[1,256]{1,0:T(1,128)S(1)}, u32[]{:S(2)}) copy-start(f32[1,256]{1,0:T(1,128)S(1)} %get-tuple-element.1000) | copy-start | bytes 3076
  23.3 45.0 %copy-start.182 = (f32[1,256]{1,0:T(1,128)}, f32[1,256]{1,0:T(1,128)S(1)}, u32[]{:S(2)}) copy-start(f32[1,256]{1,0:T(1,128)S(1)} %get-tuple-element.1034) | copy-start | bytes 3076
  24.1 44.2 %copy-start.123 = (f32[1,1024]{1,0:T(1,128)}, f32[1,1024]{1,0:T(1,128)S(1)}, u32[]{:S(2)}) copy-start(f32[1,1024]{1,0:T(1,128)S(1)} %get-tuple-element.989) | copy-start | bytes 12292
  24.1 44.2 %copy-start.126 = (f32[1,1024]{1,0:T(1,128)}, f32[1,1024]{1,0:T(1,128)S(1)}, u32[]{:S(2)}) copy-start(f32[1,1024]{1,0:T(1,128)S(1)} %get-tuple-element.991) | copy-start | bytes 12292
  24.1 44.2 %copy-start.129 = (f32[1,1024]{1,0:T(1,128)}, f32[1,1024]{1,0:T(1,128)S(1)}, u32[]{:S(2)}) copy-start(f32[1,1024]{1,0:T(1,128)S(1)} %get-tuple-element.990) | copy-start | bytes 12292
  24.3 54.0 %copy-start.202 = (f32[2]{0:T(128)}, f32[2]{0:T(128)S(1)}, u32[]{:S(2)}) copy-start(f32[2]{0:T(128)S(1)} %fusion.203) | copy-start | bytes 28
  24.9 53.3 %copy-start.204 = (f32[2]{0:T(128)}, f32[2]{0:T(128)S(1)}, u32[]{:S(2)}) copy-start(f32[2]{0:T(128)S(1)} %dynamic_slice.160) | copy-start | bytes 28
  25.9 1008.3 %reduce-scatter.3.cloned.1.call-start = ((), (), s32[]{:S(2)}) async-start(), calls=%async_computation.4 | async-start | bytes 4456448 | tf_op jit(solution)/shard_map/reduce_scatter | solution.py:329
  44.5 23.2 %copy-start.69 = (bf16[512,1024]{0,1:T(8,128)(2,1)}, bf16[512,1024]{0,1:T(8,128)(2,1)S(1)}, u32[]{:S(2)}) copy-start(bf16[512,1024]{0,1:T(8,128)(2,1)S(1)} %get-tuple-element.952) | copy-start | bytes 3145732
  44.5 23.2 %copy-start.72 = (bf16[512,1024]{0,1:T(8,128)(2,1)}, bf16[512,1024]{0,1:T(8,128)(2,1)S(1)}, u32[]{:S(2)}) copy-start(bf16[512,1024]{0,1:T(8,128)(2,1)S(1)} %get-tuple-element.953) | copy-start | bytes 3145732
  44.5 17.0 %copy-start.158 = (f32[1024]{0:T(1024)S(1)}, f32[1024]{0:T(1024)}, u32[]{:S(2)}) copy-start(f32[1024]{0:T(1024)} %param.29) | copy-start | bytes 12292
  45.0 16.5 %copy-start.176 = (f32[1024]{0:T(1024)}, f32[1024]{0:T(1024)S(1)}, u32[]{:S(2)}) copy-start(f32[1024]{0:T(1024)S(1)} %add_rsqrt_fusion.3) | copy-start | bytes 12292
  75.2 15.4 %copy-start.39 = (f32[1024,256]{1,0:T(8,128)}, f32[1024,256]{1,0:T(8,128)S(1)}, u32[]{:S(2)}) copy-start(f32[1024,256]{1,0:T(8,128)S(1)} %get-tuple-element.916) | copy-start | bytes 3145732
  81.1 14.9 %copy-start.103 = (f32[16,2,64]{2,0,1:T(8,128)}, f32[16,2,64]{2,0,1:T(8,128)S(1)}, u32[]{:S(2)}) copy-start(f32[16,2,64]{2,0,1:T(8,128)S(1)} %reduce_window_sum.29) | copy-start | bytes 24580
  372.9 25.4 %collective-permute-start.1 = (bf16[1024,512]{1,0:T(8,128)(2,1)S(1)}, bf16[1024,512]{1,0:T(8,128)(2,1)}, u32[]{:S(2)}, u32[]{:S(2)}) collective-permute-start(bf16[1024,512]{1,0:T(8,128)(2,1)S(1)} %get-tuple-element.934), channel_id=1, source_target_pairs={{0,1},{1,0},{2,3},{3,2},{4,5},{5,4},{6,7},{7,6},{8,9},{9,8},{10,11... | collective-permute-start | bytes 3145736 | tf_op jit(solution)/shard_map/ppermute | solution.py:170
  375.0 39.1 %copy-start.198 = (bf16[1024]{0:T(1024)(128)(2,1)}, bf16[1024]{0:T(1024)(128)(2,1)S(1)}, u32[]{:S(2)}) copy-start(bf16[1024]{0:T(1024)(128)(2,1)S(1)} %fusion.193) | copy-start | bytes 6148
  375.6 22.6 %copy-start.120 = (f32[1024]{0:T(1024)}, f32[1024]{0:T(1024)S(1)}, u32[]{:S(2)}) copy-start(f32[1024]{0:T(1024)S(1)} %fusion.192) | copy-start | bytes 12292
  378.7 25.1 %copy-start.161 = (f32[1024]{0:T(1024)S(1)}, f32[1024]{0:T(1024)}, u32[]{:S(2)}) copy-start(f32[1024]{0:T(1024)} %param.43) | copy-start | bytes 12292
  432.1 47.3 %collective-permute-start.5 = (bf16[1024,1024]{0,1:T(8,128)(2,1)}, bf16[1024,1024]{0,1:T(8,128)(2,1)}, u32[]{:S(2)}, u32[]{:S(2)}) collective-permute-start(bf16[1024,1024]{0,1:T(8,128)(2,1)} %get-tuple-element.1018), channel_id=1, source_target_pairs={{0,1},{1,0},{2,3},{3,2},{4,5},{5,4},{6,7},{7,6},{8,9},{9,8},{10,11... | collective-permute-start | bytes 6291464 | tf_op jit(solution)/shard_map/ppermute | solution.py:170
  922.5 184.4 %reduce-scatter.5.cloned.1.call-start = ((), (), s32[]{:S(2)}) async-start(), calls=%async_computation.5 | async-start | bytes 9191424 | tf_op jit(solution)/shard_map/reduce_scatter | solution.py:314
  950.6 44.0 %collective-permute-start.3 = (bf16[512,1024]{0,1:T(8,128)(2,1)}, bf16[512,1024]{0,1:T(8,128)(2,1)}, u32[]{:S(2)}, u32[]{:S(2)}) collective-permute-start(bf16[512,1024]{0,1:T(8,128)(2,1)} %dynamic-slice_convert_fusion.1), channel_id=1, source_target_pairs={{0,1},{1,0},{2,3},{3,2},{4,5},{5,4},{6,7},{7,6},{8,9},{9,8},{10,11... | collective-permute-start | bytes 3145736 | tf_op jit(solution)/shard_map/ppermute | solution.py:170
  969.1 11.1 copy-start.74
  969.1 11.1 copy-start.98
  969.1 11.1 copy-start.99
  969.1 11.1 copy-start.160
  981.2 1.3 collective-permute-start.7
  982.6 4.3 collective-permute-start.8
  986.9 6.3 collective-permute-start.9
  993.2 5.8 collective-permute-start.10
  999.1 4.3 collective-permute-start.11
  1002.4 23.6 %collective-permute-start.6 = (bf16[512,1024]{0,1:T(8,128)(2,1)S(1)}, bf16[512,1024]{0,1:T(8,128)(2,1)S(1)}, u32[]{:S(2)}, u32[]{:S(2)}) collective-permute-start(bf16[512,1024]{0,1:T(8,128)(2,1)S(1)} %dynamic-slice_convert_fusion), channel_id=1, source_target_pairs={{0,1},{1,0},{2,3},{3,2},{4,5},{5,4},{6,7},{7,6},{8,9},{9,8},{10,11... | collective-permute-start | bytes 3145736 | tf_op jit(solution)/shard_map/ppermute | solution.py:170
  (187 other events, 795.7 us)
Sparse Core Ops, SparseCore 0:
  12.3 49.2 all-gather.2
  63.8 88.4 all-gather.4
  922.6 72.3 reduce-scatter.2
  999.4 107.4 reduce-scatter.4

commit v2 on v1

--- a/solution.py
+++ b/solution.py
@@ -4,6 +4,8 @@
 import jax
 import jax.numpy as jnp
 from jax import lax
+from jax.experimental import pallas as pl
+from jax.experimental.pallas import tpu as pltpu
 from jax.sharding import PartitionSpec as P
 
 DK = 128
@@ -13,7 +15,6 @@
 
 
 EPS = 1e-06
-PRECISE = lax.Precision.HIGHEST
 
 
 def layout(seq_lengths, seq_owner, device, row_count):
@@ -37,10 +38,6 @@
     return (keep_masks, resets, valid_rows)
 
 
-def head_dot_product(formula, left, right):
-    return jnp.einsum(formula, left, right, precision=PRECISE)
-
-
 def across_rows(left, right):
     return lax.dot_general(
         left, right, (((0,), (0,)), ((), ())), preferred_element_type=jnp.float32
@@ -62,108 +59,468 @@
     return inv_rms * (upstream - normed * jnp.mean(upstream * normed, -1, keepdims=True))
 
 
-def causal_conv(signal, filters, keep_masks):
-    summed = signal * filters[0]
+ROWS = 128
+NN = ((1,), (0,))
+NT = ((1,), (1,))
+TN = ((0,), (0,))
+FINE_GRAM = False
+FINE_INVERSE = True
+FINE_APPLY = False
+FINE_STATE = False
+FINE_BACK = False
+
+
+def dot(left, right, dims):
+    return lax.dot_general(left, right, (dims, ((), ())), preferred_element_type=jnp.float32)
+
+
+def high_low(values):
+    high = values.astype(jnp.bfloat16)
+    return high, (values - high.astype(jnp.float32)).astype(jnp.bfloat16)
+
+
+def product(left, right, dims, fine=False):
+    if not fine:
+        return dot(left.astype(jnp.bfloat16), right.astype(jnp.bfloat16), dims)
+    left_high, left_low = high_low(left)
+    right_high, right_low = high_low(right)
+    return dot(left_high, right_high, dims) + (
+        dot(left_high, right_low, dims) + dot(left_low, right_high, dims)
+    )
+
+
+def summed_by(mask, values, dims=NN):
+    high, low = high_low(values)
+    return dot(mask, high, dims) + dot(mask, low, dims)
+
+
+def chunk_masks(resets_ref, chunk):
+    first = 1.0 - resets_ref[2 * chunk].astype(jnp.float32)
+    second = 1.0 - resets_ref[2 * chunk + 1].astype(jnp.float32)
+    row = lax.broadcasted_iota(jnp.int32, (ROWS, ROWS), 0)
+    col = lax.broadcasted_iota(jnp.int32, (ROWS, ROWS), 1)
+    late = row >= SPAN
+    reached = jnp.where(late, first * second, first)
+    reaching = jnp.where(late, 1.0, second)
+    joined = jnp.where(late & (col < SPAN), second, 1.0)
+    return row, col, reached, reaching, joined, first * second
+
+
+def unit_lower_inverse(coupling, row, col):
+    eye = jnp.where(row == col, 1.0, 0.0)
+    base = 16
+    near = jnp.where((row // base) == (col // base), coupling, 0.0)
+    inverse = eye - near
+    powered = near
+    size = 2
+    while size < base:
+        powered = product(powered, powered, NN, FINE_INVERSE)
+        inverse = inverse + product(inverse, powered, NN, FINE_INVERSE)
+        size *= 2
+    while base < ROWS:
+        wide = 2 * base
+        link = jnp.where(
+            ((row // wide) == (col // wide)) & ((row // base) != (col // base)), coupling, 0.0
+        )
+        inverse = inverse - product(
+            inverse, product(link, inverse, NN, FINE_INVERSE), NN, FINE_INVERSE
+        )
+        base = wide
+    return inverse
+
+
+def sigmoid(values):
+    return 1.0 / (1.0 + jnp.exp(-values))
+
+
+def lane_sum(values):
+    return jnp.sum(values, -1, keepdims=True)
+
+
+def forward_kernel(
+    heads,
+    resets_ref,
+    proj_ref,
+    keep_ref,
+    filter_ref,
+    rates_ref,
+    gain_ref,
+    gated_ref,
+    conv_ref,
+    mixed_ref,
+    state_ref,
+    inverse_ref,
+    parts_ref,
+    written_ref,
+    factor_ref,
+    grams_ref,
+    rows_buf,
+    state_buf,
+):
+    chunk = pl.program_id(0)
+    qk = heads * DK
+    conv_cols = 2 * qk + heads * DV
+    proj_cols = conv_cols + heads * DV
+
+    @pl.when(chunk == 0)
+    def _():
+        rows_buf[0:8, :] = jnp.zeros((8, conv_cols), jnp.float32)
+        state_buf[...] = jnp.zeros_like(state_buf)
+
+    rows_buf[8 : 8 + ROWS, :] = proj_ref[:, :conv_cols]
+    conv = rows_buf[8 : 8 + ROWS, :] * filter_ref[0:1, :]
     for offset in range(1, KW):
-        delayed = jnp.concatenate(
-            [jnp.zeros((offset, signal.shape[1]), jnp.float32), signal[:-offset]], axis=0
-        )
-        summed = summed + delayed * filters[offset] * keep_masks[offset][:, None]
-    return summed
-
-
-def unit_norm(vectors):
-    return vectors * lax.rsqrt(jnp.sum(vectors * vectors, -1, keepdims=True) + EPS)
-
-
-def delta_rule(queries, keys_unit, values_in, decays, betas, resets):
-    row_count, heads_local = decays.shape
-    blocks = row_count // SPAN
-
-    def blocked(tensor):
-        return jnp.swapaxes(tensor.reshape((blocks, SPAN) + tensor.shape[1:]), 1, 2)
-
-    query_blocks = blocked(queries)
-    key_blocks = blocked(keys_unit)
-    value_blocks = blocked(values_in)
-    beta_blocks = blocked(betas)
-    cumulative = jnp.cumsum(blocked(decays), axis=-1)
-    gap_matrix = cumulative[..., :, None] - cumulative[..., None, :]
-    lower_mask = jnp.tril(jnp.ones((SPAN, SPAN), jnp.float32))
-    strict = lower_mask - jnp.eye(SPAN, dtype=jnp.float32)
-    factor = jnp.exp(gap_matrix * lower_mask) * lower_mask
-    key_gram = head_dot_product("bhik,bhjk->bhij", key_blocks, key_blocks)
-    query_key = head_dot_product("bhik,bhjk->bhij", query_blocks, key_blocks)
-    coupling = beta_blocks[..., :, None] * factor * strict * key_gram
-    inverse = jnp.eye(SPAN, dtype=jnp.float32) - coupling
-    powered = coupling
-    for round_index in range(SPAN.bit_length() - 2):
-        powered = head_dot_product("bhij,bhjk->bhik", powered, powered)
-        inverse = inverse + head_dot_product("bhij,bhjk->bhik", inverse, powered)
-    growth = jnp.exp(cumulative)
-    span_end = cumulative[..., -1:]
-    value_part = head_dot_product("bhij,bhjv->bhiv", inverse, beta_blocks[..., None] * value_blocks)
-    key_part = head_dot_product(
-        "bhij,bhjk->bhik", inverse, (beta_blocks * growth)[..., None] * key_blocks
-    )
-    query_grown = growth[..., None] * query_blocks
-    key_tail = jnp.exp(span_end - cumulative)[..., None] * key_blocks
-    tail_decay = jnp.exp(span_end)
-    mixing_all = factor * query_key
-
-    def advance(state, inputs):
-        (
-            restart,
-            projected_value,
-            projected_key,
-            query_gathered_rows,
-            key_at_step,
-            tail_decay_cumulative,
-            token_mixer_output,
-        ) = inputs
-        starting_state = jnp.where(restart, jnp.zeros_like(state), state)
-        written_value_rows = projected_value - head_dot_product(
-            "dqw,dwy->dqy", projected_key, starting_state
-        )
-        block_result_output = head_dot_product(
-            "dqw,dwy->dqy", query_gathered_rows, starting_state
-        ) + head_dot_product("mgy,myt->mgt", token_mixer_output, written_value_rows)
-        state_after_update = tail_decay_cumulative[:, :, None] * starting_state + head_dot_product(
-            "gny,gnr->gyr", key_at_step, written_value_rows
-        )
-        return (state_after_update, block_result_output)
-
-    initial = jnp.zeros((heads_local, DK, DV), jnp.float32)
-    final_state, outputs = lax.scan(
-        advance,
-        initial,
-        (resets, value_part, key_part, query_grown, key_tail, tail_decay, mixing_all),
-    )
-    return jnp.swapaxes(outputs, 1, 2).reshape(row_count, heads_local, DV)
-
-
-def packed_mixer(projections, smalls, keep_masks, resets):
-    proj_q, proj_k, proj_v, proj_gate, proj_decay, proj_beta = projections
-    query_filter, key_filter, value_filter, decay_log, decay_bias, head_gain = smalls
-    row_count = proj_q.shape[0]
-    heads_local = decay_log.shape[0]
-    queries = unit_norm(
-        jax.nn.silu(causal_conv(proj_q, query_filter, keep_masks)).reshape(
-            row_count, heads_local, DK
-        )
-    ) * (1.0 / math.sqrt(DK))
-    keys_unit = unit_norm(
-        jax.nn.silu(causal_conv(proj_k, key_filter, keep_masks)).reshape(row_count, heads_local, DK)
-    )
-    values_in = jax.nn.silu(causal_conv(proj_v, value_filter, keep_masks)).reshape(
-        row_count, heads_local, DV
-    )
-    betas = jax.nn.sigmoid(proj_beta)
-    decays = -jnp.exp(decay_log) * jax.nn.softplus(proj_decay + decay_bias)
-    outputs = delta_rule(queries, keys_unit, values_in, decays, betas, resets)
-    normed = outputs * lax.rsqrt(jnp.mean(outputs * outputs, -1, keepdims=True) + EPS)
-    gated = normed * head_gain * jax.nn.silu(proj_gate.reshape(row_count, heads_local, DV))
-    return gated.reshape(row_count, heads_local * DV)
+        conv = conv + rows_buf[8 - offset : 8 - offset + ROWS, :] * (
+            filter_ref[offset : offset + 1, :] * keep_ref[:, offset : offset + 1]
+        )
+    rows_buf[0:8, :] = rows_buf[ROWS : ROWS + 8, :]
+    conv_ref[...] = conv
+
+    row, col, reached, reaching, joined, passed = chunk_masks(resets_ref, chunk)
+    lower = jnp.where(row >= col, 1.0, 0.0)
+    lower_b = lower.astype(jnp.bfloat16)
+    rate = proj_ref[:, proj_cols : proj_cols + 128]
+    shifted = rate + rates_ref[0:1, :]
+    decay_all = rates_ref[1:2, :] * (
+        jnp.maximum(shifted, 0.0) + jnp.log1p(jnp.exp(-jnp.abs(shifted)))
+    )
+    beta_all = sigmoid(rate)
+    for head in range(heads):
+        decay = jnp.broadcast_to(decay_all[:, head : head + 1], (ROWS, ROWS))
+        beta = beta_all[:, heads + head : heads + head + 1]
+        sums = summed_by(
+            lower_b, jnp.concatenate([jnp.where(row > col, decay, 0.0), decay], axis=1)
+        )
+        factor = jnp.exp(sums[:, :ROWS]) * (lower * joined)
+        total = sums[:, ROWS:]
+        total_end = total[ROWS - 1 : ROWS, :]
+        grown = jnp.exp(total) * reached
+        tail = jnp.exp(total_end - total) * reaching
+        end_decay = jnp.exp(total_end[:, :1]) * passed
+
+        conv_q = conv[:, head * DK : (head + 1) * DK]
+        conv_k = conv[:, qk + head * DK : qk + (head + 1) * DK]
+        conv_v = conv[:, 2 * qk + head * DV : 2 * qk + (head + 1) * DV]
+        query = conv_q * sigmoid(conv_q)
+        query = query * (lax.rsqrt(lane_sum(query * query) + EPS) * (1.0 / math.sqrt(DK)))
+        key = conv_k * sigmoid(conv_k)
+        key = key * lax.rsqrt(lane_sum(key * key) + EPS)
+        value = conv_v * sigmoid(conv_v)
+
+        grams = product(jnp.concatenate([key, query], axis=0), key, NT, FINE_GRAM)
+        coupling = jnp.where(row > col, factor * grams[:ROWS] * beta, 0.0)
+        inverse = unit_lower_inverse(coupling, row, col)
+        parts = product(
+            inverse,
+            jnp.concatenate([beta * value, (beta * grown) * key], axis=1),
+            NN,
+            FINE_APPLY,
+        )
+        state = state_buf[head]
+        from_state = product(
+            jnp.concatenate([parts[:, DV:], grown * query], axis=0), state, NN, FINE_STATE
+        )
+        written = parts[:, :DV] - from_state[:ROWS]
+        mixed = from_state[ROWS:] + product(factor * grams[ROWS:], written, NN, FINE_STATE)
+        state_buf[head] = end_decay * state + product(tail * key, written, TN, FINE_STATE)
+
+        gate = proj_ref[:, conv_cols + head * DV : conv_cols + (head + 1) * DV]
+        normed = mixed * lax.rsqrt(lane_sum(mixed * mixed) * (1.0 / DV) + EPS)
+        gated_ref[:, head * DV : (head + 1) * DV] = (
+            normed * gain_ref[...] * (gate * sigmoid(gate))
+        ).astype(jnp.bfloat16)
+        mixed_ref[:, head * DV : (head + 1) * DV] = mixed
+        state_ref[0, head] = state
+        inverse_ref[0, head] = inverse
+        parts_ref[0, head] = parts
+        written_ref[0, head] = written
+        factor_ref[0, head] = factor
+        grams_ref[0, head] = grams
+
+
+def backward_kernel(
+    heads,
+    chunks,
+    resets_ref,
+    upstream_ref,
+    proj_ref,
+    keep_ref,
+    filter_ref,
+    rates_ref,
+    gain_ref,
+    conv_ref,
+    mixed_ref,
+    state_ref,
+    inverse_ref,
+    parts_ref,
+    written_ref,
+    factor_ref,
+    grams_ref,
+    dproj_ref,
+    dfilter_ref,
+    dsmall_ref,
+    rows_buf,
+    dstate_buf,
+):
+    step = pl.program_id(0)
+    chunk = chunks - 1 - step
+    qk = heads * DK
+    conv_cols = 2 * qk + heads * DV
+    proj_cols = conv_cols + heads * DV
+
+    @pl.when(step == 0)
+    def _():
+        rows_buf[ROWS : ROWS + 8, :] = jnp.zeros((8, conv_cols), jnp.float32)
+        dstate_buf[...] = jnp.zeros_like(dstate_buf)
+        dfilter_ref[...] = jnp.zeros_like(dfilter_ref)
+        dsmall_ref[...] = jnp.zeros_like(dsmall_ref)
+
+    row, col, reached, reaching, joined, passed = chunk_masks(resets_ref, chunk)
+    lower = jnp.where(row >= col, 1.0, 0.0)
+    lower_b = lower.astype(jnp.bfloat16)
+    upper_b = jnp.where(row <= col, 1.0, 0.0).astype(jnp.bfloat16)
+    rate = proj_ref[:, proj_cols : proj_cols + 128]
+    shifted = rate + rates_ref[0:1, :]
+    decay_all = rates_ref[1:2, :] * (
+        jnp.maximum(shifted, 0.0) + jnp.log1p(jnp.exp(-jnp.abs(shifted)))
+    )
+    slope_all = rates_ref[1:2, :] * sigmoid(shifted)
+    beta_all = sigmoid(rate)
+    drate = jnp.zeros((ROWS, 128), jnp.float32)
+    dsums = jnp.zeros((ROWS, 128), jnp.float32)
+    lane = lax.broadcasted_iota(jnp.int32, (ROWS, 128), 1)
+    dgain = jnp.zeros((1, DV), jnp.float32)
+    for head in range(heads):
+        decay = jnp.broadcast_to(decay_all[:, head : head + 1], (ROWS, ROWS))
+        beta = beta_all[:, heads + head : heads + head + 1]
+        total = summed_by(lower_b, decay)
+        total_end = total[ROWS - 1 : ROWS, :]
+        grown = jnp.exp(total) * reached
+        tail = jnp.exp(total_end - total) * reaching
+        end_decay = jnp.exp(total_end[:, :1]) * passed
+
+        v_at = slice(head * DV, (head + 1) * DV)
+        gate_at = slice(conv_cols + head * DV, conv_cols + (head + 1) * DV)
+        q_at = slice(head * DK, (head + 1) * DK)
+        k_at = slice(qk + head * DK, qk + (head + 1) * DK)
+        value_at = slice(2 * qk + head * DV, 2 * qk + (head + 1) * DV)
+        conv_q = conv_ref[:, q_at]
+        conv_k = conv_ref[:, k_at]
+        conv_v = conv_ref[:, value_at]
+        sig_q = sigmoid(conv_q)
+        sig_k = sigmoid(conv_k)
+        sig_v = sigmoid(conv_v)
+        query = conv_q * sig_q
+        inv_q = lax.rsqrt(lane_sum(query * query) + EPS)
+        query = query * (inv_q * (1.0 / math.sqrt(DK)))
+        key = conv_k * sig_k
+        inv_k = lax.rsqrt(lane_sum(key * key) + EPS)
+        key = key * inv_k
+        value = conv_v * sig_v
+
+        mixed = mixed_ref[:, v_at]
+        inv_o = lax.rsqrt(lane_sum(mixed * mixed) * (1.0 / DV) + EPS)
+        normed = mixed * inv_o
+        gate = proj_ref[:, gate_at]
+        sig_g = sigmoid(gate)
+        upstream = upstream_ref[:, v_at]
+        up_normed = upstream * normed
+        dgain = dgain + jnp.sum(up_normed * (gate * sig_g), 0, keepdims=True)
+        dproj_ref[:, gate_at] = (
+            up_normed * gain_ref[...] * (sig_g * (1.0 + gate * (1.0 - sig_g)))
+        ).astype(jnp.bfloat16)
+        dnormed = upstream * gain_ref[...] * (gate * sig_g)
+        dmixed = inv_o * (dnormed - normed * (lane_sum(dnormed * normed) * (1.0 / DV)))
+
+        state = state_ref[0, head]
+        dstate = dstate_buf[head]
+        inverse = inverse_ref[0, head]
+        parts = parts_ref[0, head]
+        written = written_ref[0, head]
+        factor = factor_ref[0, head]
+        key_gram = grams_ref[0, head, :ROWS]
+        query_key = grams_ref[0, head, ROWS:]
+        mixing = factor * query_key
+        query_grown = grown * query
+        key_tail = tail * key
+
+        dwritten = product(mixing, dmixed, TN, FINE_BACK) + product(
+            key_tail, dstate, NN, FINE_BACK
+        )
+        stacked = jnp.concatenate([dmixed, -dwritten], axis=0)
+        through = product(stacked, state, NT, FINE_BACK)
+        dquery_grown = through[:ROWS]
+        dprojected_key = through[ROWS:]
+        dmixing = product(dmixed, written, NT, FINE_BACK)
+        dkey_tail = product(written, dstate, NT, FINE_BACK)
+        end_grad = end_decay * lane_sum(jnp.sum(state * dstate, 0, keepdims=True))
+        dstate_buf[head] = end_decay * dstate + product(
+            jnp.concatenate([query_grown, parts[:, DV:]], axis=0), stacked, TN, FINE_BACK
+        )
+        solved = product(
+            inverse, jnp.concatenate([dwritten, dprojected_key], axis=1), TN, FINE_BACK
+        )
+        dcoupling = product(solved, parts, NT, FINE_BACK)
+        dcoupling = jnp.where(row > col, -dcoupling * factor, 0.0)
+        dcoupling_gram = dcoupling * key_gram
+        dbeta = lane_sum(dcoupling_gram)
+        dgap = beta * dcoupling_gram + dmixing * mixing
+        dgrams = jnp.concatenate([beta * dcoupling, dmixing * factor], axis=0)
+        by_key = product(dgrams, key, NN, FINE_BACK)
+        dkey = by_key[:ROWS] + product(
+            dgrams, jnp.concatenate([key, query], axis=0), TN, FINE_BACK
+        )
+        dquery = by_key[ROWS:] + grown * dquery_grown
+        dvalue_scaled = solved[:, :DV]
+        dkey_scaled = solved[:, DV:]
+        scaled_rows = lane_sum(dkey_scaled * (grown * key))
+        dbeta = dbeta + lane_sum(dvalue_scaled * value) + scaled_rows
+        tail_rows = lane_sum(dkey_tail * key_tail)
+        dkey = dkey + tail * dkey_tail + (beta * grown) * dkey_scaled
+        dtotal = lane_sum(dquery_grown * query_grown) + beta * scaled_rows - tail_rows
+        sums = summed_by(
+            upper_b, jnp.concatenate([dgap, jnp.broadcast_to(dtotal, (ROWS, ROWS))], axis=1)
+        )
+        ddecay = (
+            lane_sum(jnp.where(col < row, sums[:, :ROWS], 0.0))
+            + sums[:, ROWS : ROWS + 1]
+            + (end_grad + jnp.sum(tail_rows, 0, keepdims=True))
+        )
+        dshifted = ddecay * slope_all[:, head : head + 1]
+        drate = drate + jnp.where(lane == head, dshifted, 0.0)
+        drate = drate + jnp.where(lane == heads + head, dbeta * (beta * (1.0 - beta)), 0.0)
+        dsums = dsums + jnp.where(lane == head, ddecay * decay, 0.0)
+        dsums = dsums + jnp.where(lane == heads + head, dshifted, 0.0)
+
+        unit = query * math.sqrt(DK)
+        dunit = dquery * (1.0 / math.sqrt(DK))
+        dsilu = inv_q * (dunit - unit * lane_sum(dunit * unit))
+        rows_buf[0:ROWS, q_at] = dsilu * (sig_q * (1.0 + conv_q * (1.0 - sig_q)))
+        dsilu = inv_k * (dkey - key * lane_sum(dkey * key))
+        rows_buf[0:ROWS, k_at] = dsilu * (sig_k * (1.0 + conv_k * (1.0 - sig_k)))
+        rows_buf[0:ROWS, value_at] = (beta * dvalue_scaled) * (
+            sig_v * (1.0 + conv_v * (1.0 - sig_v))
+        )
+
+    signal = proj_ref[:, :conv_cols]
+    shifted_grad = rows_buf[0:ROWS, :]
+    dsignal = shifted_grad * filter_ref[0:1, :]
+    dfilter_ref[0:1, :] += jnp.sum(signal * shifted_grad, 0, keepdims=True)
+    for offset in range(1, KW):
+        shifted_grad = (
+            rows_buf[offset : offset + ROWS, :] * keep_ref[:, KW + offset : KW + offset + 1]
+        )
+        dsignal = dsignal + shifted_grad * filter_ref[offset : offset + 1, :]
+        dfilter_ref[offset : offset + 1, :] += jnp.sum(signal * shifted_grad, 0, keepdims=True)
+    rows_buf[ROWS : ROWS + 8, :] = rows_buf[0:8, :]
+    dproj_ref[:, :conv_cols] = dsignal.astype(jnp.bfloat16)
+    dproj_ref[:, proj_cols : proj_cols + 128] = drate.astype(jnp.bfloat16)
+    dsmall_ref[0:1, :] += dgain
+    dsmall_ref[1:2, 0:128] += jnp.sum(dsums, 0, keepdims=True)
+
+
+def mixer_forward(resets, proj, keep, filters, rates, head_gain, heads):
+    row_count, proj_width = proj.shape
+    chunks = row_count // ROWS
+    conv_cols = 2 * heads * DK + heads * DV
+    f32 = jnp.float32
+
+    def rows_of(cols, dtype=f32):
+        return jax.ShapeDtypeStruct((row_count, cols), dtype)
+
+    def saved(rows, cols):
+        return jax.ShapeDtypeStruct((chunks, heads, rows, cols), f32)
+
+    def row_block(cols):
+        return pl.BlockSpec((ROWS, cols), lambda c, r: (c, 0))
+
+    def saved_block(rows, cols):
+        return pl.BlockSpec((1, heads, rows, cols), lambda c, r: (c, 0, 0, 0))
+
+    def whole(array):
+        return pl.BlockSpec(array.shape, lambda c, r: (0, 0))
+
+    return pl.pallas_call(
+        partial(forward_kernel, heads),
+        grid_spec=pltpu.PrefetchScalarGridSpec(
+            num_scalar_prefetch=1,
+            grid=(chunks,),
+            in_specs=[
+                row_block(proj_width),
+                row_block(keep.shape[1]),
+                whole(filters),
+                whole(rates),
+                whole(head_gain),
+            ],
+            out_specs=[
+                row_block(heads * DV),
+                row_block(conv_cols),
+                row_block(heads * DV),
+                saved_block(DK, DV),
+                saved_block(ROWS, ROWS),
+                saved_block(ROWS, DV + DK),
+                saved_block(ROWS, DV),
+                saved_block(ROWS, ROWS),
+                saved_block(2 * ROWS, ROWS),
+            ],
+            scratch_shapes=[
+                pltpu.VMEM((ROWS + 8, conv_cols), f32),
+                pltpu.VMEM((heads, DK, DV), f32),
+            ],
+        ),
+        out_shape=[
+            rows_of(heads * DV, jnp.bfloat16),
+            rows_of(conv_cols),
+            rows_of(heads * DV),
+            saved(DK, DV),
+            saved(ROWS, ROWS),
+            saved(ROWS, DV + DK),
+            saved(ROWS, DV),
+            saved(ROWS, ROWS),
+            saved(2 * ROWS, ROWS),
+        ],
+        compiler_params=pltpu.CompilerParams(vmem_limit_bytes=40 << 20),
+        name="mixer_forward",
+    )(resets, proj, keep, filters, rates, head_gain)
+
+
+def mixer_backward(resets, upstream, proj, keep, filters, rates, head_gain, saved, heads):
+    row_count, proj_width = proj.shape
+    chunks = row_count // ROWS
+    conv_cols = 2 * heads * DK + heads * DV
+    f32 = jnp.float32
+
+    def row_block(array):
+        return pl.BlockSpec((ROWS, array.shape[1]), lambda c, r: (chunks - 1 - c, 0))
+
+    def saved_block(array):
+        return pl.BlockSpec((1,) + array.shape[1:], lambda c, r: (chunks - 1 - c, 0, 0, 0))
+
+    def whole(array):
+        return pl.BlockSpec(array.shape, lambda c, r: (0, 0))
+
+    dproj = jax.ShapeDtypeStruct((row_count, proj_width), jnp.bfloat16)
+    dfilter = jax.ShapeDtypeStruct((8, conv_cols), f32)
+    dsmall = jax.ShapeDtypeStruct((8, DV), f32)
+    return pl.pallas_call(
+        partial(backward_kernel, heads, chunks),
+        grid_spec=pltpu.PrefetchScalarGridSpec(
+            num_scalar_prefetch=1,
+            grid=(chunks,),
+            in_specs=[row_block(upstream), row_block(proj), row_block(keep)]
+            + [whole(filters), whole(rates), whole(head_gain)]
+            + [row_block(saved[0]), row_block(saved[1])]
+            + [saved_block(array) for array in saved[2:]],
+            out_specs=[row_block(dproj), whole(dfilter), whole(dsmall)],
+            scratch_shapes=[
+                pltpu.VMEM((ROWS + 8, conv_cols), f32),
+                pltpu.VMEM((heads, DK, DV), f32),
+            ],
+        ),
+        out_shape=[dproj, dfilter, dsmall],
+        compiler_params=pltpu.CompilerParams(vmem_limit_bytes=40 << 20),
+        name="mixer_backward",
+    )(resets, upstream, proj, keep, filters, rates, head_gain, *saved)
 
 
 def swap_halves(array):
@@ -249,35 +606,35 @@
     down_weight = rest_weight[:, 2 * v_cols + 2 * ff_cols :]
     cot_other = swap_halves(cotangent)
 
-    smalls = (
-        own_columns(query_filter, qk_cols),
-        own_columns(key_filter, qk_cols),
-        own_columns(value_filter, v_cols),
-        own_columns(decay_log, heads_local),
-        own_columns(decay_bias, heads_local),
-        head_gain,
-    )
+    filters = jnp.concatenate(
+        [
+            own_columns(query_filter, qk_cols),
+            own_columns(key_filter, qk_cols),
+            own_columns(value_filter, v_cols),
+        ],
+        axis=1,
+    )
+    filters = jnp.pad(filters, ((0, 8 - KW), (0, 0)))
+    rates = jnp.stack(
+        [own_columns(decay_bias, heads_local), -jnp.exp(own_columns(decay_log, heads_local))]
+    )
+    rates = jnp.pad(rates, ((0, 6), (0, 128 - heads_local)))
+    gain_row = head_gain[None]
+    restarts = resets.astype(jnp.int32)
+    later_masks = [
+        jnp.concatenate([keep_masks[offset, offset:], jnp.ones((offset,), f32)])
+        for offset in range(KW)
+    ]
+    keep_cols = jnp.stack([keep_masks[offset] for offset in range(KW)] + later_masks, axis=1)
     inputs_f = in_order(block_input, input_other, model_index, 0).astype(f32)
     cot_all = in_order(cotangent, cot_other, model_index, 0)
     normed1, inv_rms1 = rms_forward(inputs_f)
     mixed_in = (normed1 * mix_gain).astype(bf16)
     proj = jnp.dot(mixed_in, mix_weight, preferred_element_type=f32)
-    cuts = (qk_cols, 2 * qk_cols, 2 * qk_cols + v_cols, proj_cols, proj_cols + heads_local)
-
-    def split(array):
-        return (
-            array[:, : cuts[0]],
-            array[:, cuts[0] : cuts[1]],
-            array[:, cuts[1] : cuts[2]],
-            array[:, cuts[2] : cuts[3]],
-            array[:, cuts[3] : cuts[4]],
-            array[:, cuts[4] : cuts[4] + heads_local],
-        )
-
-    gated, pullback = jax.vjp(
-        partial(packed_mixer, keep_masks=keep_masks, resets=resets), split(proj), smalls
-    )
-    gated_b = gated.astype(bf16)
+    cuts = (qk_cols, 2 * qk_cols, 2 * qk_cols + v_cols, proj_cols)
+    gated_b, *saved = mixer_forward(
+        restarts, proj, keep_cols, filters, rates, gain_row, heads_local
+    )
     gated_both = jnp.concatenate([gated_b, swap_halves(gated_b)], axis=1)
     resid = inputs_f + valid_all * against(gated_both, out_both)
     normed2, inv_rms2 = rms_forward(resid)
@@ -316,9 +673,9 @@
     resid_grad = cot_all.astype(f32) + rms_backward(ffn_in_grad * ffn_gain, normed2, inv_rms2)
     mix_cot = (resid_grad * valid_all).astype(bf16)
     gated_grad = jnp.dot(mix_cot, out_both[:, :v_cols], preferred_element_type=f32)
-    proj_grads, small_grads = pullback(gated_grad)
-    pad = jnp.zeros((row_count, 128 - 2 * heads_local), f32)
-    proj_grad = jnp.concatenate(list(proj_grads) + [pad], axis=1).astype(bf16)
+    proj_grad, filter_grads, small_grads = mixer_backward(
+        restarts, gated_grad, proj, keep_cols, filters, rates, gain_row, saved, heads_local
+    )
     mix_grads = jnp.concatenate(
         [
             across_rows(mixed_in, proj_grad[:, :proj_cols]).astype(bf16),
@@ -337,17 +694,17 @@
         mix_in_sum * mix_gain, own_half(normed1), own_half(inv_rms1)
     )
     common = jnp.concatenate(
-        [mix_gain_part, ffn_gain_part, small_grads[5], jnp.zeros((width - DV,), f32)]
+        [mix_gain_part, ffn_gain_part, small_grads[0], jnp.zeros((width - DV,), f32)]
     ).reshape(3, width)
     tail_row = jnp.concatenate(
-        [small_grads[3], small_grads[4], jnp.zeros((width - 2 * heads_local,), f32)]
+        [small_grads[1, : 2 * heads_local], jnp.zeros((width - 2 * heads_local,), f32)]
     )
     split_rows = jnp.concatenate(
         [
             rate_grads,
-            small_grads[0].reshape(-1, width),
-            small_grads[1].reshape(-1, width),
-            small_grads[2].reshape(-1, width),
+            filter_grads[:KW, : cuts[0]].reshape(-1, width),
+            filter_grads[:KW, cuts[0] : cuts[1]].reshape(-1, width),
+            filter_grads[:KW, cuts[1] : cuts[2]].reshape(-1, width),
             tail_row[None],
         ],
         axis=0,

time: 1130 us -> 494 us (0.44)
  matrix products: 510 us -> 94.4 us
  local copies, waits for them, and re-layouts: 243 us -> 39.6 us
  other arithmetic: 142 us -> 34.5 us
  Pallas kernels: 0 us -> 68.7 us
  waiting for transfers between devices: 187 us -> 221 us
    dot_general x234 -> x0, matrix products: 432 us -> none  [head_dot_product(): return jnp.einsum(formula, left, right, precision=PRECISE)]
    pallas_call x0 -> x2, Pallas kernels: none -> 68.7 us  [the longest x1 44 us: mixer_forward(): pl.pallas_call(partial(forward_kernel, heads), grid_spec=pltpu.PrefetchSc...]
    dynamic_slice x48 -> x0, local copies, waits for them, and re-layouts: 54.6 us -> none  [delta_rule(): lax.scan(advance, initial, (resets, value_part, key_part, query_grown, ke...]
    reduce_sum x33 -> x0, other arithmetic: 49.8 us -> none  [the longest x16 17.3 us: advance(): tail_decay_cumulative[:, :, None] * starting_state]
    dynamic_update_slice x48 -> x0, local copies, waits for them, and re-layouts: 39 us -> none  [delta_rule(): lax.scan(advance, initial, (resets, value_part, key_part, query_grown, ke...]
    mul x41 -> x0, local copies, waits for them, and re-layouts: 31.4 us -> none  [the longest x32 21 us: advance(): tail_decay_cumulative[:, :, None] * starting_state]
    dynamic_update_slice x16 -> x0, other arithmetic: 22 us -> none  [delta_rule(): lax.scan(advance, initial, (resets, value_part, key_part, query_grown, ke...]
    reduce_scatter x1, waiting for transfers between devices: 68 us -> 88.5 us  [on_device(): lax.psum_scatter(rest_grads, 'dp', scatter_dimension=0, tiled=True)]
  transfers between devices with their start and end apart: 16 -> 16, of which waited for: 10 -> 14; matrix products, arithmetic and copies ran while one was open for 35% -> 17% of each run, Pallas kernels for 0% -> 9%
where the time goes in v2:
time: 494 us; the launch traced here: 489 us
  waiting for transfers between devices  221 us (45%)
  matrix products  94.4 us (19%)
  Pallas kernels  68.7 us (14%)
  local copies, waits for them, and re-layouts  39.6 us (8%)
  other arithmetic  34.5 us (7%)
  starting transfers between devices  15.6 us (3%)
  between operations  14.8 us (3%)
    ppermute x8, waiting for transfers between devices, swap_halves(): return lax.ppermute(array, 'mp', [(0, 1), (1, 0)])  105 us
    reduce_scatter x1, waiting for transfers between devices, on_device(): lax.psum_scatter(rest_grads, 'dp', scatter_dimension=0, tiled=True)  88.5 us
    pallas_call x1, Pallas kernels, mixer_forward(): pl.pallas_call(partial(forward_kernel, heads), grid_spec=pltpu.PrefetchSc...  44 us
    dot_general x5, matrix products, across_rows(): lax.dot_general(left, right, (((0,), (0,)), ((), ())), preferred_element_...  30.5 us
    dot_general x4, matrix products, against(): lax.dot_general(left, right, (((1,), (1,)), ((), ())), preferred_element_...  28.1 us
    unnamed x109, local copies, waits for them, and re-layouts  26 us
    pallas_call x1, Pallas kernels, mixer_backward(): pl.pallas_call(partial(backward_kernel, heads, chunks), grid_spec=pltpu.P...  24.6 us
    dot_general x1, matrix products, on_device(): pre = jnp.dot(ffn_in, ffn_in_weight, preferred_element_type=f32)  13.5 us
  transfers between devices with their start and end apart: 16, of which 14 were waited for; matrix products, arithmetic and copies ran while one was open for 17% of the time, Pallas kernels for 9%

profile of v2, /device:TPU:0, one launch (start us, length us, event | category | flops | bytes accessed | tf_op | source)
XLA Modules:
  0.0 488.7 jit_solution(15500132495143971105)
XLA Ops:
  12.3 3.0 collective-permute-start.2
  16.2 1.6 collective-permute-done.2
  21.5 1.5 copy.107
  23.1 2.1 collective-permute-start
  29.6 19.8 %collective-permute-done = bf16[512,1024]{0,1:T(8,128)(2,1)} collective-permute-done((bf16[512,1024]{0,1:T(8,128)(2,1)S(1)}, bf16[512,1024]{0,1:T(8,128)(2,1)}, u32[]{:S(2)}, u32[]{:S(2)}) %collective-permute-start) | collective-permute-done | bytes 1048608 | tf_op jit(solution)/shard_map/ppermute | solution.py:527
  49.3 1.7 broadcast_select_fusion.3
  51.5 10.2 %all-gather.3.cloned.1.call-done = bf16[1024,1664]{1,0:T(8,128)(2,1)} async-done(((bf16[64,1664]{1,0:T(8,128)(2,1)}), bf16[1024,1664]{1,0:T(8,128)(2,1)}) %all-gather.3.cloned.1.call-update) | async-done | bytes 3407888 | tf_op jit(solution)/shard_map/all_gather | solution.py:598
  61.8 8.2 %fusion.33.proj_ref = f32[1024,1664]{1,0:T(8,128)} fusion(bf16[1024,1664]{1,0:T(8,128)(2,1)} %all-gather.3.cloned.1.call-done, f32[1024]{0:T(1024)S(1)} %copy-done.34, f32[1024]{0:T(1024)S(1)} %add_rsqrt_fusion.1, bf16[512,1024]{0,1:T(8,128)(2,1)S(1)} %get-tuple-element.142, bf16[512,1024]{0,1:T(8,128)(2,1)S(1)} %get-tuple-element.141), kind=kOutput, calls=%fused_computation.140 | convolution fusion | flops 3497000960 | bytes 12328960 | tf_op jit(solution)/shard_map/dot_general | solution.py:633
  70.0 44.0 %mixer_forward.1 = (bf16[1024,512]{1,0:T(8,128)(2,1)S(1)}, f32[1024,1024]{1,0:T(8,128)}, f32[1024,512]{1,0:T(8,128)S(1)}, f32[8,2,128,256]{3,2,1,0:T(8,128)S(1)}...) custom-call(s32[16]{0:T(128)S(1)} %get-tuple-element.130.resets_ref,, ...), custom_call_target="tpu_custom_call" | custom-call | tf_op jit(solution)/shard_map/mixer_forward/pallas_call | solution.py:443
  115.4 1.4 copy-done.4
  121.1 1.5 collective-permute-start.1
  123.9 3.0 broadcast_select_fusion.1
  126.9 19.6 %collective-permute-done.1 = bf16[1024,512]{1,0:T(8,128)(2,1)} collective-permute-done((bf16[1024,512]{1,0:T(8,128)(2,1)S(1)}, bf16[1024,512]{1,0:T(8,128)(2,1)}, u32[]{:S(2)}, u32[]{:S(2)}) %collective-permute-start.1) | collective-permute-done | bytes 1048608 | tf_op jit(solution)/shard_map/ppermute | solution.py:527
  146.5 6.0 %all-gather.5.cloned.1.call-done = bf16[1024,5248]{1,0:T(8,128)(2,1)} async-done(((bf16[64,5248]{1,0:T(8,128)(2,1)}), bf16[1024,5248]{1,0:T(8,128)(2,1)}) %all-gather.5.cloned.1.call-update) | async-done | bytes 10747920 | tf_op jit(solution)/shard_map/all_gather | solution.py:603
  152.5 5.3 %multiply_reduce_fusion.3 = (f32[1024]{0:T(1024)S(1)}, f32[1024,1024]{0,1:T(8,128)S(1)}) fusion(bf16[1024,5248]{1,0:T(8,128)(2,1)} %all-gather.5.cloned.1.call-done, bf16[1024,512]{1,0:T(8,128)(2,1)} %collective-permute-done.1, bf16[1024,512]{1,0:T(8,128)(2,1)} %copy-done.13, f32[1024]{0:T(1024)S(1)} %fusion.26, bf16[512,1024]{0,1:T(8,128)(2,1)} %copy-done.22, ...), kind=kOutput, calls=%fused_computation.24 | convolution fusion | flops 2160065536 | bytes 10493952 | tf_op jit(solution)/shard_map/dot_general | solution.py:48
  157.9 13.5 %fusion.3 = f32[1024,2816]{1,0:T(8,128)} fusion(bf16[1024,5248]{1,0:T(8,128)(2,1)} %all-gather.5.cloned.1.call-done, f32[1024,1024]{0,1:T(8,128)S(1)} %get-tuple-element.173, f32[1024]{0:T(1024)S(1)} %copy-done.35, f32[1024]{0:T(1024)S(1)} %add_rsqrt_fusion), kind=kOutput, calls=%fused_computation.13 | convolution fusion | flops 5908725760 | bytes 21504000 | tf_op jit(solution)/shard_map/dot_general | solution.py:642
  171.3 11.4 %multiply_convert_fusion.1 = (bf16[1024,1408]{1,0:T(8,128)(2,1)S(1)}, bf16[1024,1408]{1,0:T(8,128)(2,1)}, bf16[1024,1408]{1,0:T(8,128)(2,1)}) fusion(f32[1024,2816]{1,0:T(8,128)} %fusion.3, bf16[1024,5248]{1,0:T(8,128)(2,1)} %all-gather.5.cloned.1.call-done, bf16[1024]{0:T(1024)(128)(2,1)S(1)} %fusion.27, bf16[512,1024]{0,1:T(8,128)(2,1)S(1)} %copy-done.28, ...), kind=kOutput, calls=%fused_computation.6 | convolution fusion | flops 2980708352 | bytes 25167872 | tf_op jit(solution)/shard_map/dot_general | solution.py:648
  182.8 10.1 %fusion.42 = (bf16[1024,1024]{0,1:T(8,128)(2,1)S(1)}, f32[1024,1024]{0,1:T(8,128)S(1)}) fusion(bf16[1024,5248]{1,0:T(8,128)(2,1)} %all-gather.5.cloned.1.call-done, bf16[1024,1408]{1,0:T(8,128)(2,1)} %get-tuple-element.135, bf16[1024,1408]{1,0:T(8,128)(2,1)S(1)} %get-tuple-element.134), kind=kOutput, calls=%fused_computation.149 | convolution fusion | flops 5918162944 | bytes 17825792 | tf_op jit(solution)/shard_map/dot_general | solution.py:48
  192.9 1.5 collective-permute-start.5
  194.5 46.3 %collective-permute-done.5 = bf16[1024,1024]{0,1:T(8,128)(2,1)S(1)} collective-permute-done((bf16[1024,1024]{0,1:T(8,128)(2,1)S(1)}, bf16[1024,1024]{0,1:T(8,128)(2,1)S(1)}, u32[]{:S(2)}, u32[]{:S(2)}) %collective-permute-start.5) | collective-permute-done | bytes 2097184 | tf_op jit(solution)/shard_map/ppermute | solution.py:527
  240.8 1.6 multiply_reduce_fusion
  242.4 2.1 multiply_add_fusion
  246.5 2.7 fusion.17.upstream_ref
  250.2 24.6 %mixer_backward.1 = (bf16[1024,1664]{1,0:T(8,128)(2,1)}, f32[8,1024]{1,0:T(8,128)S(1)}, f32[8,256]{1,0:T(8,128)S(1)}) custom-call(s32[16]{0:T(128)S(1)} %get-tuple-element.130.resets_ref, f32[1024,512]{1,0:T(8,128)S(1)} %fusion.17.upstream_ref, f32[1024,1664]{1,0:T(8,128)} %fusion.33.proj_ref, f32[1024,8]{1,0:T(8,128)S(1)} %copy.111.keep_ref, ...), custom_call_target="tpu_custom_call" | custom-call | tf_op jit(solution)/shard_map/mixer_backward/pallas_call | solution.py:505
  274.9 15.4 %convolution_convert_fusion.2 = bf16[1024,1536]{1,0:T(8,128)(2,1)S(1)} fusion(bf16[1024,1664]{1,0:T(8,128)(2,1)} %get-tuple-element.41, f32[1024]{0:T(1024)S(1)} %copy-done.34, f32[1024]{0:T(1024)S(1)} %add_rsqrt_fusion.1, bf16[512,1024]{0,1:T(8,128)(2,1)S(1)} %copy-done.23, bf16[512,1024]{0,1:T(8,128)(2,1)S(1)} %copy-done.20), kind=kOutput, calls=%fused_computation.27 | convolution fusion | flops 3230138368 | bytes 8396800 | tf_op jit(solution)/shard_map/dot_general | solution.py:42
  290.3 2.7 pad_maximum_fusion.2
  294.5 5.6 %convolution_convert_fusion.1 = bf16[1024,1408]{1,0:T(8,128)(2,1)S(1)} fusion(bf16[1024,1408]{1,0:T(8,128)(2,1)} %get-tuple-element.136, bf16[1024]{0:T(1024)(128)(2,1)S(1)} %fusion.27, bf16[512,1024]{0,1:T(8,128)(2,1)S(1)} %copy-done.29, bf16[512,1024]{0,1:T(8,128)(2,1)S(1)} %copy-done.27), kind=kOutput, calls=%fused_computation.26 | convolution fusion | flops 2960523264 | bytes 7866368 | tf_op jit(solution)/shard_map/dot_general | solution.py:42
  300.1 6.6 %convolution_convert_fusion = bf16[1024,2816]{1,0:T(8,128)(2,1)S(1)} fusion(bf16[1024,1408]{1,0:T(8,128)(2,1)S(1)} %copy-done.46, bf16[1024,1408]{1,0:T(8,128)(2,1)S(1)} %copy-done.45, f32[1024,1024]{0,1:T(8,128)S(1)} %copy-done.18, f32[1024]{0:T(1024)S(1)} %copy-done.35, f32[1024]{0:T(1024)S(1)} %add_rsqrt_fusion), kind=kOutput, calls=%fused_computation.10 | convolution fusion | flops 5923143680 | bytes 15736832 | tf_op jit(solution)/shard_map/dot_general | solution.py:42
  306.7 3.8 pad_maximum_fusion
  310.6 6.4 %fusion.9 = f32[1024,1024]{0,1:T(8,128)S(1)} fusion(bf16[1024,1408]{1,0:T(8,128)(2,1)} %get-tuple-element.136, bf16[1024,5248]{1,0:T(8,128)(2,1)} %all-gather.5.cloned.1.call-done), kind=kOutput, calls=%fused_computation.31 | convolution fusion | flops 2952790016 | bytes 9961472 | tf_op jit(solution)/shard_map/dot_general | solution.py:48
  317.0 2.1 copy-done.30
  320.2 1.5 collective-permute-start.3
  321.7 6.3 %multiply_reduce_fusion.1 = (f32[1024]{0:T(1024)S(1)}, f32[1024,1024]{0,1:T(8,128)}, f32[1024,1024]{0,1:T(8,128)}) fusion(f32[1024]{0:T(1024)S(1)} %add_rsqrt_fusion.1, bf16[512,1024]{0,1:T(8,128)(2,1)S(1)} %copy-done.24, bf16[512,1024]{0,1:T(8,128)(2,1)S(1)} %copy-done.21, bf16[1024,1664]{1,0:T(8,128)(2,1)S(1)} %copy-done.43, ...), kind=kOutput, calls=%fused_computation.18 | convolution fusion | flops 3496999936 | bytes 17309696 | tf_op jit(solution)/shard_map/dot_general | solution.py:48
  328.1 1.7 fusion.21
  332.2 3.4 collective-permute-done.8
  335.6 1.5 collective-permute-start.9
  337.2 6.4 %collective-permute-done.9 = f32[12,1024]{1,0:T(8,128)S(1)} collective-permute-done((f32[12,1024]{1,0:T(8,128)S(1)}, f32[12,1024]{1,0:T(8,128)S(1)}, u32[]{:S(2)}, u32[]{:S(2)}) %collective-permute-start.9) | collective-permute-done | bytes 49184 | tf_op jit(solution)/shard_map/ppermute | solution.py:534
  345.1 3.2 add_convert_fusion
  350.1 1.4 collective-permute-start.11
  351.6 1.7 dynamic-slice_convert_fusion
  360.9 16.1 %collective-permute-done.6 = bf16[512,1024]{0,1:T(8,128)(2,1)S(1)} collective-permute-done((bf16[512,1024]{0,1:T(8,128)(2,1)S(1)}, bf16[512,1024]{0,1:T(8,128)(2,1)S(1)}, u32[]{:S(2)}, u32[]{:S(2)}) %collective-permute-start.6) | collective-permute-done | bytes 1048608 | tf_op jit(solution)/shard_map/ppermute | solution.py:527
  376.9 2.9 multiply_reduce_fusion.4
  379.9 3.3 multiply_add_fusion.1
  383.2 1.8 copy.125
  386.0 1.4 fusion.38
  388.1 1.6 fusion.37
  389.7 88.5 %reduce-scatter.5.cloned.1.call-done = bf16[64,4224]{1,0:T(8,128)(2,1)} async-done(((bf16[1024,4224]{1,0:T(8,128)(2,1)}), bf16[64,4224]{1,0:T(8,128)(2,1)}) %reduce-scatter.5.cloned.1.call-update) | async-done | bytes 540688 | tf_op jit(solution)/shard_map/reduce_scatter | solution.py:671
  480.1 1.9 fusion.36
  (211 shorter events, 43.9 us)
Async XLA Ops:
  7.2 22.3 %copy-start = (f32[4,1024]{1,0:T(4,128)S(1)}, f32[4,1024]{1,0:T(4,128)}, u32[]{:S(2)}) copy-start(f32[4,1024]{1,0:T(4,128)} %param.34) | copy-start | bytes 49156
  7.2 17.9 %copy-start.31 = (bf16[512,1024]{1,0:T(8,128)(2,1)S(1)}, bf16[512,1024]{1,0:T(8,128)(2,1)}, u32[]{:S(2)}) copy-start(bf16[512,1024]{1,0:T(8,128)(2,1)} %param.43) | copy-start | bytes 3145732
  7.2 19.3 %copy-start.38 = (s32[16]{0:T(128)S(1)}, s32[16]{0:T(128)}, u32[]{:S(2)}) copy-start(s32[16]{0:T(128)} %param.23) | copy-start | bytes 196
  7.2 19.3 %copy-start.39 = (s32[16]{0:T(128)S(1)}, s32[16]{0:T(128)}, u32[]{:S(2)}) copy-start(s32[16]{0:T(128)} %param.24) | copy-start | bytes 196
  7.2 22.1 %copy-start.40 = (f32[4]{0:T(128)S(1)}, f32[4]{0:T(128)}, u32[]{:S(2)}) copy-start(f32[4]{0:T(128)} %param.35) | copy-start | bytes 52
  7.3 22.1 %copy-start.41 = (f32[4]{0:T(128)S(1)}, f32[4]{0:T(128)}, u32[]{:S(2)}) copy-start(f32[4]{0:T(128)} %param.36) | copy-start | bytes 52
  7.3 22.2 %copy-start.36 = (f32[4,512]{1,0:T(4,128)S(1)}, f32[4,512]{1,0:T(4,128)}, u32[]{:S(2)}) copy-start(f32[4,512]{1,0:T(4,128)} %param.33) | copy-start | bytes 24580
  7.3 22.2 %copy-start.37 = (f32[4,512]{1,0:T(4,128)S(1)}, f32[4,512]{1,0:T(4,128)}, u32[]{:S(2)}) copy-start(f32[4,512]{1,0:T(4,128)} %param.32) | copy-start | bytes 24580
  7.3 54.5 %all-gather.3.cloned.1.call-start = ((), (), s32[]{:S(2)}) async-start(), calls=%async_computation.2 | async-start | bytes 3620864 | tf_op jit(solution)/shard_map/all_gather | solution.py:598
  12.3 140.2 %all-gather.5.cloned.1.call-start = ((), (), s32[]{:S(2)}) async-start(), calls=%async_computation.3 | async-start | bytes 11419648 | tf_op jit(solution)/shard_map/all_gather | solution.py:603
  12.3 5.5 %collective-permute-start.2 = (bf16[64,512]{1,0:T(8,128)(2,1)}, bf16[64,512]{1,0:T(8,128)(2,1)S(1)}, u32[]{:S(2)}, u32[]{:S(2)}) collective-permute-start(bf16[64,512]{1,0:T(8,128)(2,1)} %bitcast.64), channel_id=1, source_target_pairs={{0,1},{1,0},{2,3},{3,2},{4,5},{5,4},{6,7},{7,6},{8,9},{9,8},{10,11... | collective-permute-start | bytes 196616 | tf_op jit(solution)/shard_map/ppermute | solution.py:527
  21.5 363.5 %reduce-scatter.3.cloned.1.call-start = ((), (), s32[]{:S(2)}) async-start(), calls=%async_computation.4 | async-start | bytes 4456448 | tf_op jit(solution)/shard_map/reduce_scatter | solution.py:686
  23.0 6.5 %copy-start.25 = (bf16[512,1024]{0,1:T(8,128)(2,1)}, bf16[512,1024]{0,1:T(8,128)(2,1)S(1)}, u32[]{:S(2)}) copy-start(bf16[512,1024]{0,1:T(8,128)(2,1)S(1)} %copy.107) | copy-start | bytes 3145732
  23.1 38.7 %copy-start.34 = (f32[1024]{0:T(1024)S(1)}, f32[1024]{0:T(1024)}, u32[]{:S(2)}) copy-start(f32[1024]{0:T(1024)} %param.25) | copy-start | bytes 12292
  23.1 26.3 %collective-permute-start = (bf16[512,1024]{0,1:T(8,128)(2,1)S(1)}, bf16[512,1024]{0,1:T(8,128)(2,1)}, u32[]{:S(2)}, u32[]{:S(2)}) collective-permute-start(bf16[512,1024]{0,1:T(8,128)(2,1)S(1)} %copy.107), channel_id=1, source_target_pairs={{0,1},{1,0},{2,3},{3,2},{4,5},{5,4},{6,7},{7,6},{8,9},{9,8},{10,11... | collective-permute-start | bytes 3145736 | tf_op jit(solution)/shard_map/ppermute | solution.py:527
  26.5 97.3 %collective-permute-start.4 = (bf16[512,1024]{0,1:T(8,128)(2,1)}, bf16[512,1024]{0,1:T(8,128)(2,1)}, u32[]{:S(2)}, u32[]{:S(2)}) collective-permute-start(bf16[512,1024]{0,1:T(8,128)(2,1)} %copy.115), channel_id=1, source_target_pairs={{0,1},{1,0},{2,3},{3,2},{4,5},{5,4},{6,7},{7,6},{8,9},{9,8},{10,11... | collective-permute-start | bytes 3145736 | tf_op jit(solution)/shard_map/ppermute | solution.py:527
  51.0 19.0 %copy-start.19 = (bf16[512,1024]{0,1:T(8,128)(2,1)}, bf16[512,1024]{0,1:T(8,128)(2,1)S(1)}, u32[]{:S(2)}) copy-start(bf16[512,1024]{0,1:T(8,128)(2,1)S(1)} %get-tuple-element.141) | copy-start | bytes 3145732
  51.0 19.0 %copy-start.22 = (bf16[512,1024]{0,1:T(8,128)(2,1)}, bf16[512,1024]{0,1:T(8,128)(2,1)S(1)}, u32[]{:S(2)}) copy-start(bf16[512,1024]{0,1:T(8,128)(2,1)S(1)} %get-tuple-element.142) | copy-start | bytes 3145732
  51.5 18.5 %copy-start.12 = (f32[256]{0:T(256)S(1)}, f32[256]{0:T(256)}, u32[]{:S(2)}) copy-start(f32[256]{0:T(256)} %param.37) | copy-start | bytes 3076
  121.1 25.4 %collective-permute-start.1 = (bf16[1024,512]{1,0:T(8,128)(2,1)S(1)}, bf16[1024,512]{1,0:T(8,128)(2,1)}, u32[]{:S(2)}, u32[]{:S(2)}) collective-permute-start(bf16[1024,512]{1,0:T(8,128)(2,1)S(1)} %get-tuple-element.32), channel_id=1, source_target_pairs={{0,1},{1,0},{2,3},{3,2},{4,5},{5,4},{6,7},{7,6},{8,9},{9,8},{10,11... | collective-permute-start | bytes 3145736 | tf_op jit(solution)/shard_map/ppermute | solution.py:527
  126.9 31.0 %copy-start.35 = (f32[1024]{0:T(1024)S(1)}, f32[1024]{0:T(1024)}, u32[]{:S(2)}) copy-start(f32[1024]{0:T(1024)} %param.39) | copy-start | bytes 12292
  157.8 84.6 %copy-start.17 = (f32[1024,1024]{0,1:T(8,128)}, f32[1024,1024]{0,1:T(8,128)S(1)}, u32[]{:S(2)}) copy-start(f32[1024,1024]{0,1:T(8,128)S(1)} %get-tuple-element.173) | copy-start | bytes 12582916
  157.8 13.5 %copy-start.26 = (bf16[512,1024]{0,1:T(8,128)(2,1)S(1)}, bf16[512,1024]{0,1:T(8,128)(2,1)}, u32[]{:S(2)}) copy-start(bf16[512,1024]{0,1:T(8,128)(2,1)} %get-tuple-element.139) | copy-start | bytes 3145732
  157.9 13.5 %copy-start.28 = (bf16[512,1024]{0,1:T(8,128)(2,1)S(1)}, bf16[512,1024]{0,1:T(8,128)(2,1)}, u32[]{:S(2)}) copy-start(bf16[512,1024]{0,1:T(8,128)(2,1)} %get-tuple-element.140) | copy-start | bytes 3145732
  182.8 10.1 %copy-start.44 = (bf16[1024,1408]{1,0:T(8,128)(2,1)}, bf16[1024,1408]{1,0:T(8,128)(2,1)S(1)}, u32[]{:S(2)}) copy-start(bf16[1024,1408]{1,0:T(8,128)(2,1)S(1)} %get-tuple-element.134) | copy-start | bytes 8650756
  192.9 47.9 %collective-permute-start.5 = (bf16[1024,1024]{0,1:T(8,128)(2,1)S(1)}, bf16[1024,1024]{0,1:T(8,128)(2,1)S(1)}, u32[]{:S(2)}, u32[]{:S(2)}) collective-permute-start(bf16[1024,1024]{0,1:T(8,128)(2,1)S(1)} %get-tuple-element.174), channel_id=1, source_target_pairs={{0,1},{1,0},{2,3},{3,2},{4,5},{5,4},{6,7},{7,6},{8,9},{9,8},{10,11... | collective-permute-start | bytes 6291464 | tf_op jit(solution)/shard_map/ppermute | solution.py:527
  246.5 3.2 copy-start.7
  246.5 3.4 copy-start.9
  246.5 3.7 copy-start.11
  250.2 24.7 %copy-start.20 = (bf16[512,1024]{0,1:T(8,128)(2,1)S(1)}, bf16[512,1024]{0,1:T(8,128)(2,1)}, u32[]{:S(2)}) copy-start(bf16[512,1024]{0,1:T(8,128)(2,1)} %copy-done.19) | copy-start | bytes 3145732
  250.2 24.7 %copy-start.23 = (bf16[512,1024]{0,1:T(8,128)(2,1)S(1)}, bf16[512,1024]{0,1:T(8,128)(2,1)}, u32[]{:S(2)}) copy-start(bf16[512,1024]{0,1:T(8,128)(2,1)} %copy-done.22) | copy-start | bytes 3145732
  293.0 185.2 %reduce-scatter.5.cloned.1.call-start = ((), (), s32[]{:S(2)}) async-start(), calls=%async_computation.5 | async-start | bytes 9191424 | tf_op jit(solution)/shard_map/reduce_scatter | solution.py:671
  294.5 5.6 %copy-start.18 = (f32[1024,1024]{0,1:T(8,128)S(1)}, f32[1024,1024]{0,1:T(8,128)}, u32[]{:S(2)}) copy-start(f32[1024,1024]{0,1:T(8,128)} %copy-done.17) | copy-start | bytes 12582916
  294.5 5.6 %copy-start.45 = (bf16[1024,1408]{1,0:T(8,128)(2,1)S(1)}, bf16[1024,1408]{1,0:T(8,128)(2,1)}, u32[]{:S(2)}) copy-start(bf16[1024,1408]{1,0:T(8,128)(2,1)} %copy-done.44) | copy-start | bytes 8650756
  294.5 5.6 %copy-start.46 = (bf16[1024,1408]{1,0:T(8,128)(2,1)S(1)}, bf16[1024,1408]{1,0:T(8,128)(2,1)}, u32[]{:S(2)}) copy-start(bf16[1024,1408]{1,0:T(8,128)(2,1)} %get-tuple-element.135) | copy-start | bytes 8650756
  310.5 11.1 %copy-start.21 = (bf16[512,1024]{0,1:T(8,128)(2,1)S(1)}, bf16[512,1024]{0,1:T(8,128)(2,1)}, u32[]{:S(2)}) copy-start(bf16[512,1024]{0,1:T(8,128)(2,1)} %copy-done.19) | copy-start | bytes 3145732
  310.6 11.1 %copy-start.24 = (bf16[512,1024]{0,1:T(8,128)(2,1)S(1)}, bf16[512,1024]{0,1:T(8,128)(2,1)}, u32[]{:S(2)}) copy-start(bf16[512,1024]{0,1:T(8,128)(2,1)} %copy-done.22) | copy-start | bytes 3145732
  310.6 11.1 %copy-start.42 = (bf16[1024,1664]{1,0:T(8,128)(2,1)S(1)}, bf16[1024,1664]{1,0:T(8,128)(2,1)}, u32[]{:S(2)}) copy-start(bf16[1024,1664]{1,0:T(8,128)(2,1)} %all-gather.3.cloned.1.call-done) | copy-start | bytes 10223620
  310.6 11.1 %copy-start.43 = (bf16[1024,1664]{1,0:T(8,128)(2,1)S(1)}, bf16[1024,1664]{1,0:T(8,128)(2,1)}, u32[]{:S(2)}) copy-start(bf16[1024,1664]{1,0:T(8,128)(2,1)} %get-tuple-element.41) | copy-start | bytes 10223620
  320.2 24.9 %collective-permute-start.3 = (bf16[512,1024]{0,1:T(8,128)(2,1)}, bf16[512,1024]{0,1:T(8,128)(2,1)}, u32[]{:S(2)}, u32[]{:S(2)}) collective-permute-start(bf16[512,1024]{0,1:T(8,128)(2,1)} %dynamic-slice_convert_fusion.1), channel_id=1, source_target_pairs={{0,1},{1,0},{2,3},{3,2},{4,5},{5,4},{6,7},{7,6},{8,9},{9,8},{10,11... | collective-permute-start | bytes 3145736 | tf_op jit(solution)/shard_map/ppermute | solution.py:527
  329.9 1.3 collective-permute-start.7
  331.3 4.3 collective-permute-start.8
  335.6 8.1 %collective-permute-start.9 = (f32[12,1024]{1,0:T(8,128)S(1)}, f32[12,1024]{1,0:T(8,128)S(1)}, u32[]{:S(2)}, u32[]{:S(2)}) collective-permute-start(f32[12,1024]{1,0:T(8,128)S(1)} %add.123), channel_id=1, source_target_pairs={{0,8},{2,10},{4,12},{6,14},{8,0},{10,2},{12,4},{14,6},{16,24},{18,... | collective-permute-start | bytes 147464 | tf_op jit(solution)/shard_map/ppermute | solution.py:534
  343.7 6.5 %collective-permute-start.10 = (f32[12,1024]{1,0:T(8,128)S(1)}, f32[12,1024]{1,0:T(8,128)S(1)}, u32[]{:S(2)}, u32[]{:S(2)}) collective-permute-start(f32[12,1024]{1,0:T(8,128)S(1)} %add.124), channel_id=1, source_target_pairs={{0,16},{2,18},{4,20},{6,22},{8,24},{10,26},{12,28},{14,30},{16,0},... | collective-permute-start | bytes 147464 | tf_op jit(solution)/shard_map/ppermute | solution.py:534
  350.1 5.0 %collective-permute-start.11 = (f32[12,1024]{1,0:T(8,128)S(1)}, f32[12,1024]{1,0:T(8,128)S(1)}, u32[]{:S(2)}, u32[]{:S(2)}) collective-permute-start(f32[12,1024]{1,0:T(8,128)S(1)} %add.125), channel_id=1, source_target_pairs={{0,1},{1,0},{2,3},{3,2},{4,5},{5,4},{6,7},{7,6},{8,9},{9,8},{10,11... | collective-permute-start | bytes 147464 | tf_op jit(solution)/shard_map/ppermute | solution.py:527
  353.3 23.6 %collective-permute-start.6 = (bf16[512,1024]{0,1:T(8,128)(2,1)S(1)}, bf16[512,1024]{0,1:T(8,128)(2,1)S(1)}, u32[]{:S(2)}, u32[]{:S(2)}) collective-permute-start(bf16[512,1024]{0,1:T(8,128)(2,1)S(1)} %dynamic-slice_convert_fusion), channel_id=1, source_target_pairs={{0,1},{1,0},{2,3},{3,2},{4,5},{5,4},{6,7},{7,6},{8,9},{9,8},{10,11... | collective-permute-start | bytes 3145736 | tf_op jit(solution)/shard_map/ppermute | solution.py:527
  355.5 24.4 %copy-start.16 = (f32[1024,1024]{0,1:T(8,128)S(1)}, f32[1024,1024]{0,1:T(8,128)}, u32[]{:S(2)}) copy-start(f32[1024,1024]{0,1:T(8,128)} %copy-done.15) | copy-start | bytes 12582916
  379.9 102.1 %copy-start.1 = (f32[4,1024]{1,0:T(4,128)S(1)}, f32[4,1024]{1,0:T(4,128)}, u32[]{:S(2)}) copy-start(f32[4,1024]{1,0:T(4,128)} %param.34) | copy-start | bytes 49156
  (15 other events, 22.8 us)
Sparse Core Ops, SparseCore 0:
  12.4 49.3 all-gather.2
  64.1 88.3 all-gather.4
  293.1 74.3 reduce-scatter.2
  371.9 106.2 reduce-scatter.4

commit v3 on v2

--- a/solution.py
+++ b/solution.py
@@ -65,6 +65,8 @@
 TN = ((0,), (0,))
 FINE_GRAM = False
 FINE_INVERSE = True
+FINE_MERGE = True
+SUBS = 2
 FINE_APPLY = False
 FINE_STATE = False
 FINE_BACK = False
@@ -106,27 +108,33 @@
     return row, col, reached, reaching, joined, first * second
 
 
-def unit_lower_inverse(coupling, row, col):
+def unit_lower_inverses(couplings, row, col):
     eye = jnp.where(row == col, 1.0, 0.0)
     base = 16
-    near = jnp.where((row // base) == (col // base), coupling, 0.0)
-    inverse = eye - near
-    powered = near
+    near = (row // base) == (col // base)
+    powered = [jnp.where(near, coupling, 0.0) for coupling in couplings]
+    inverses = [eye - power for power in powered]
     size = 2
     while size < base:
-        powered = product(powered, powered, NN, FINE_INVERSE)
-        inverse = inverse + product(inverse, powered, NN, FINE_INVERSE)
+        powered = [product(power, power, NN, FINE_INVERSE) for power in powered]
+        inverses = [
+            inverse + product(inverse, power, NN, FINE_INVERSE)
+            for inverse, power in zip(inverses, powered)
+        ]
         size *= 2
     while base < ROWS:
         wide = 2 * base
-        link = jnp.where(
-            ((row // wide) == (col // wide)) & ((row // base) != (col // base)), coupling, 0.0
-        )
-        inverse = inverse - product(
-            inverse, product(link, inverse, NN, FINE_INVERSE), NN, FINE_INVERSE
-        )
+        linked = ((row // wide) == (col // wide)) & ((row // base) != (col // base))
+        steps = [
+            product(jnp.where(linked, coupling, 0.0), inverse, NN, FINE_MERGE)
+            for coupling, inverse in zip(couplings, inverses)
+        ]
+        inverses = [
+            inverse - product(inverse, step, NN, FINE_MERGE)
+            for inverse, step in zip(inverses, steps)
+        ]
         base = wide
-    return inverse
+    return inverses
 
 
 def sigmoid(values):
@@ -157,39 +165,43 @@
     rows_buf,
     state_buf,
 ):
-    chunk = pl.program_id(0)
+    step = pl.program_id(0)
     qk = heads * DK
     conv_cols = 2 * qk + heads * DV
     proj_cols = conv_cols + heads * DV
-
-    @pl.when(chunk == 0)
+    rows = SUBS * ROWS
+
+    @pl.when(step == 0)
     def _():
         rows_buf[0:8, :] = jnp.zeros((8, conv_cols), jnp.float32)
         state_buf[...] = jnp.zeros_like(state_buf)
 
-    rows_buf[8 : 8 + ROWS, :] = proj_ref[:, :conv_cols]
-    conv = rows_buf[8 : 8 + ROWS, :] * filter_ref[0:1, :]
+    rows_buf[8 : 8 + rows, :] = proj_ref[:, :conv_cols]
+    conv = rows_buf[8 : 8 + rows, :] * filter_ref[0:1, :]
     for offset in range(1, KW):
-        conv = conv + rows_buf[8 - offset : 8 - offset + ROWS, :] * (
+        conv = conv + rows_buf[8 - offset : 8 - offset + rows, :] * (
             filter_ref[offset : offset + 1, :] * keep_ref[:, offset : offset + 1]
         )
-    rows_buf[0:8, :] = rows_buf[ROWS : ROWS + 8, :]
+    rows_buf[0:8, :] = rows_buf[rows : rows + 8, :]
     conv_ref[...] = conv
 
-    row, col, reached, reaching, joined, passed = chunk_masks(resets_ref, chunk)
-    lower = jnp.where(row >= col, 1.0, 0.0)
-    lower_b = lower.astype(jnp.bfloat16)
     rate = proj_ref[:, proj_cols : proj_cols + 128]
     shifted = rate + rates_ref[0:1, :]
     decay_all = rates_ref[1:2, :] * (
         jnp.maximum(shifted, 0.0) + jnp.log1p(jnp.exp(-jnp.abs(shifted)))
     )
     beta_all = sigmoid(rate)
-    for head in range(heads):
-        decay = jnp.broadcast_to(decay_all[:, head : head + 1], (ROWS, ROWS))
-        beta = beta_all[:, heads + head : heads + head + 1]
+    units = [(sub, head) for sub in range(SUBS) for head in range(heads)]
+    prepared = []
+    for sub, head in units:
+        row, col, reached, reaching, joined, passed = chunk_masks(resets_ref, step * SUBS + sub)
+        lower = jnp.where(row >= col, 1.0, 0.0)
+        at = slice(sub * ROWS, (sub + 1) * ROWS)
+        decay = jnp.broadcast_to(decay_all[at, head : head + 1], (ROWS, ROWS))
+        beta = beta_all[at, heads + head : heads + head + 1]
         sums = summed_by(
-            lower_b, jnp.concatenate([jnp.where(row > col, decay, 0.0), decay], axis=1)
+            lower.astype(jnp.bfloat16),
+            jnp.concatenate([jnp.where(row > col, decay, 0.0), decay], axis=1),
         )
         factor = jnp.exp(sums[:, :ROWS]) * (lower * joined)
         total = sums[:, ROWS:]
@@ -198,9 +210,9 @@
         tail = jnp.exp(total_end - total) * reaching
         end_decay = jnp.exp(total_end[:, :1]) * passed
 
-        conv_q = conv[:, head * DK : (head + 1) * DK]
-        conv_k = conv[:, qk + head * DK : qk + (head + 1) * DK]
-        conv_v = conv[:, 2 * qk + head * DV : 2 * qk + (head + 1) * DV]
+        conv_q = conv[at, head * DK : (head + 1) * DK]
+        conv_k = conv[at, qk + head * DK : qk + (head + 1) * DK]
+        conv_v = conv[at, 2 * qk + head * DV : 2 * qk + (head + 1) * DV]
         query = conv_q * sigmoid(conv_q)
         query = query * (lax.rsqrt(lane_sum(query * query) + EPS) * (1.0 / math.sqrt(DK)))
         key = conv_k * sigmoid(conv_k)
@@ -209,33 +221,37 @@
 
         grams = product(jnp.concatenate([key, query], axis=0), key, NT, FINE_GRAM)
         coupling = jnp.where(row > col, factor * grams[:ROWS] * beta, 0.0)
-        inverse = unit_lower_inverse(coupling, row, col)
-        parts = product(
-            inverse,
-            jnp.concatenate([beta * value, (beta * grown) * key], axis=1),
-            NN,
-            FINE_APPLY,
-        )
+        scaled = jnp.concatenate([beta * value, (beta * grown) * key], axis=1)
+        factor_ref[sub, head] = factor
+        grams_ref[sub, head] = grams
+        prepared.append(
+            (coupling, scaled, grown * query, factor * grams[ROWS:], tail * key, end_decay)
+        )
+    row = lax.broadcasted_iota(jnp.int32, (ROWS, ROWS), 0)
+    col = lax.broadcasted_iota(jnp.int32, (ROWS, ROWS), 1)
+    inverses = unit_lower_inverses([entry[0] for entry in prepared], row, col)
+    for (sub, head), inverse, entry in zip(units, inverses, prepared):
+        _, scaled, query_grown, mixing, key_tail, end_decay = entry
+        at = slice(sub * ROWS, (sub + 1) * ROWS)
+        parts = product(inverse, scaled, NN, FINE_APPLY)
         state = state_buf[head]
         from_state = product(
-            jnp.concatenate([parts[:, DV:], grown * query], axis=0), state, NN, FINE_STATE
+            jnp.concatenate([parts[:, DV:], query_grown], axis=0), state, NN, FINE_STATE
         )
         written = parts[:, :DV] - from_state[:ROWS]
-        mixed = from_state[ROWS:] + product(factor * grams[ROWS:], written, NN, FINE_STATE)
-        state_buf[head] = end_decay * state + product(tail * key, written, TN, FINE_STATE)
-
-        gate = proj_ref[:, conv_cols + head * DV : conv_cols + (head + 1) * DV]
+        mixed = from_state[ROWS:] + product(mixing, written, NN, FINE_STATE)
+        state_buf[head] = end_decay * state + product(key_tail, written, TN, FINE_STATE)
+
+        gate = proj_ref[at, conv_cols + head * DV : conv_cols + (head + 1) * DV]
         normed = mixed * lax.rsqrt(lane_sum(mixed * mixed) * (1.0 / DV) + EPS)
-        gated_ref[:, head * DV : (head + 1) * DV] = (
+        gated_ref[at, head * DV : (head + 1) * DV] = (
             normed * gain_ref[...] * (gate * sigmoid(gate))
         ).astype(jnp.bfloat16)
-        mixed_ref[:, head * DV : (head + 1) * DV] = mixed
-        state_ref[0, head] = state
-        inverse_ref[0, head] = inverse
-        parts_ref[0, head] = parts
-        written_ref[0, head] = written
-        factor_ref[0, head] = factor
-        grams_ref[0, head] = grams
+        mixed_ref[at, head * DV : (head + 1) * DV] = mixed
+        state_ref[sub, head] = state
+        inverse_ref[sub, head] = inverse
+        parts_ref[sub, head] = parts
+        written_ref[sub, head] = written
 
 
 def backward_kernel(
@@ -432,10 +448,10 @@
         return jax.ShapeDtypeStruct((chunks, heads, rows, cols), f32)
 
     def row_block(cols):
-        return pl.BlockSpec((ROWS, cols), lambda c, r: (c, 0))
+        return pl.BlockSpec((SUBS * ROWS, cols), lambda c, r: (c, 0))
 
     def saved_block(rows, cols):
-        return pl.BlockSpec((1, heads, rows, cols), lambda c, r: (c, 0, 0, 0))
+        return pl.BlockSpec((SUBS, heads, rows, cols), lambda c, r: (c, 0, 0, 0))
 
     def whole(array):
         return pl.BlockSpec(array.shape, lambda c, r: (0, 0))
@@ -444,7 +460,7 @@
         partial(forward_kernel, heads),
         grid_spec=pltpu.PrefetchScalarGridSpec(
             num_scalar_prefetch=1,
-            grid=(chunks,),
+            grid=(chunks // SUBS,),
             in_specs=[
                 row_block(proj_width),
                 row_block(keep.shape[1]),
@@ -464,7 +480,7 @@
                 saved_block(2 * ROWS, ROWS),
             ],
             scratch_shapes=[
-                pltpu.VMEM((ROWS + 8, conv_cols), f32),
+                pltpu.VMEM((SUBS * ROWS + 8, conv_cols), f32),
                 pltpu.VMEM((heads, DK, DV), f32),
             ],
         ),
@@ -534,6 +550,49 @@
         array = array + lax.ppermute(array, "dp", [(i, i ^ step) for i in range(count)])
         step *= 2
     return array
+
+
+def dp_swap(array, bit):
+    count = lax.axis_size("dp")
+    return lax.ppermute(array, "dp", [(i, i ^ bit) for i in range(count)])
+
+
+def dp_gather(shard, cuts):
+    index = lax.axis_index("dp")
+    bits = [1 << i for i in reversed(range((lax.axis_size("dp") - 1).bit_length()))]
+    pieces = [shard[None, :, start:stop] for start, stop in cuts]
+    for bit in bits:
+        others = [dp_swap(piece, bit) for piece in pieces]
+        upper = (index & bit) != 0
+        pieces = [
+            jnp.stack(
+                [jnp.where(upper, other, piece), jnp.where(upper, piece, other)], axis=1
+            ).reshape((-1,) + piece.shape[1:])
+            for piece, other in zip(pieces, others)
+        ]
+    return [piece.reshape(-1, piece.shape[-1]) for piece in pieces]
+
+
+def dp_scatter(pieces):
+    index = lax.axis_index("dp")
+    count = lax.axis_size("dp")
+    pieces = [piece.reshape(count, -1, piece.shape[-1]) for piece in pieces]
+    bit = 1
+    while bit < count:
+        side = (index & bit) // bit
+        pairs = [piece.reshape((-1, 2) + piece.shape[1:]) for piece in pieces]
+        others = [
+            dp_swap(
+                lax.dynamic_index_in_dim(pair, 1 - side, 1, False).astype(jnp.bfloat16), bit
+            )
+            for pair in pairs
+        ]
+        pieces = [
+            lax.dynamic_index_in_dim(pair, side, 1, False) + other.astype(jnp.float32)
+            for pair, other in zip(pairs, others)
+        ]
+        bit *= 2
+    return [piece[0] for piece in pieces]
 
 
 def in_order(own, other, model_index, axis):
@@ -595,7 +654,10 @@
     shard_mix = jnp.concatenate(
         [query_weight, key_weight, value_weight, gate_weight, own_shard(small_weight)], axis=1
     )
-    mix_weight = lax.all_gather(shard_mix, "dp", axis=0, tiled=True)
+    half = proj_cols // 256 * 128
+    mix_weight = jnp.concatenate(
+        dp_gather(shard_mix, ((0, half), (half, shard_mix.shape[1]))), axis=1
+    )
     input_other = swap_halves(block_input)
     out_rows = out_weight.T
     out_other = swap_halves(out_rows)
@@ -653,22 +715,24 @@
     pre_grad = jnp.concatenate([gate_grad_pre, up_grad_pre], axis=1)
     ffn_in_part = against(pre_grad, ffn_in_weight)
     ffn_in_sent = ffn_in_part.astype(bf16)
-    ffn_in_grad = ffn_in_sent.astype(f32) + swap_halves(ffn_in_sent).astype(f32)
-
-    def own_half(array):
-        return lax.dynamic_slice_in_dim(array, model_index * local_rows, local_rows, 0)
-
-    def other_half(array):
-        return lax.dynamic_slice_in_dim(array, (1 - model_index) * local_rows, local_rows, 0)
-
-    ffn_part = against(hidden, down_weight)
-    ffn_sum = own_half(ffn_part) + swap_halves(other_half(ffn_part).astype(bf16)).astype(f32)
-    block_output = (own_half(resid) + own_half(valid_all) * ffn_sum).astype(bf16)
     rest_grads = jnp.concatenate(
         [across_rows(ffn_in, pre_grad).astype(bf16), across_rows(cot_masked, hidden).astype(bf16)],
         axis=1,
     )
     ffn_shard = lax.psum_scatter(rest_grads, "dp", scatter_dimension=0, tiled=True)
+    ffn_in_got, _ = lax.optimization_barrier((swap_halves(ffn_in_sent), rest_grads))
+    ffn_in_grad = ffn_in_sent.astype(f32) + ffn_in_got.astype(f32)
+
+    def own_half(array):
+        return lax.dynamic_slice_in_dim(array, model_index * local_rows, local_rows, 0)
+
+    def other_half(array):
+        return lax.dynamic_slice_in_dim(array, (1 - model_index) * local_rows, local_rows, 0)
+
+    ffn_part = against(hidden, down_weight)
+    ffn_sent, _ = lax.optimization_barrier((other_half(ffn_part).astype(bf16), ffn_in_got))
+    ffn_sum = own_half(ffn_part) + swap_halves(ffn_sent).astype(f32)
+    block_output = (own_half(resid) + own_half(valid_all) * ffn_sum).astype(bf16)
     ffn_gain_part = jnp.sum(ffn_in_part * normed2, 0)
     resid_grad = cot_all.astype(f32) + rms_backward(ffn_in_grad * ffn_gain, normed2, inv_rms2)
     mix_cot = (resid_grad * valid_all).astype(bf16)
@@ -676,14 +740,16 @@
     proj_grad, filter_grads, small_grads = mixer_backward(
         restarts, gated_grad, proj, keep_cols, filters, rates, gain_row, saved, heads_local
     )
-    mix_grads = jnp.concatenate(
+    split_at = cuts[1]
+    mix_shards = dp_scatter(
         [
-            across_rows(mixed_in, proj_grad[:, :proj_cols]).astype(bf16),
-            across_rows(mix_cot, gated_b).astype(bf16),
-        ],
-        axis=1,
-    )
-    mix_shard = lax.psum_scatter(mix_grads, "dp", scatter_dimension=0, tiled=True)
+            jnp.concatenate(
+                [across_rows(mix_cot, gated_b), across_rows(mixed_in, proj_grad[:, :split_at])],
+                axis=1,
+            ),
+            across_rows(mixed_in, proj_grad[:, split_at:proj_cols]),
+        ]
+    )
     rate_grads = across_rows(proj_grad[:, proj_cols:], mixed_in)[: 2 * heads_local]
     mix_in_part = against(proj_grad, mix_weight)
     mix_in_sum = own_half(mix_in_part) + swap_halves(
@@ -744,7 +810,7 @@
             ]
         )
 
-    mix_shard = mix_shard.astype(f32)
+    mix_shard = jnp.concatenate([mix_shards[0][:, v_cols:], mix_shards[1]], axis=1)
     ffn_shard = ffn_shard.astype(f32)
     return (
         block_output,
@@ -762,7 +828,7 @@
         rate_grad(0),
         rate_grad(heads_local),
         common[2, :DV],
-        mix_shard[:, proj_cols:].T,
+        mix_shards[0][:, :v_cols].T,
         common[1],
         ffn_shard[:, :ff_cols],
         ffn_shard[:, ff_cols : 2 * ff_cols],

time: 494 us -> 416 us (0.84)
  waiting for transfers between devices: 221 us -> 139 us
  Pallas kernels: 68.7 us -> 48.3 us
  starting transfers between devices: 15.6 us -> 34.2 us
  other arithmetic: 34.5 us -> 40.7 us
  matrix products: 94.4 us -> 88.6 us
    reduce_scatter x1, waiting for transfers between devices: 88.5 us -> 0.01 us  [on_device(): lax.psum_scatter(rest_grads, 'dp', scatter_dimension=0, tiled=True)]
    ppermute x0 -> x16, waiting for transfers between devices: none -> 56.9 us  [dp_swap(): return lax.ppermute(array, 'dp', [(i, i ^ bit) for i in range(count)])]
    ppermute x8, waiting for transfers between devices: 105 us -> 79.4 us  [swap_halves(): return lax.ppermute(array, 'mp', [(0, 1), (1, 0)])]
    pallas_call x1, Pallas kernels: 44 us -> 23.2 us  [mixer_forward(): pl.pallas_call(partial(forward_kernel, heads), grid_spec=pltpu.PrefetchSc...]
    ppermute x0 -> x16, starting transfers between devices: none -> 15.6 us  [dp_swap(): return lax.ppermute(array, 'dp', [(i, i ^ bit) for i in range(count)])]
    all_gather x1 -> x0, waiting for transfers between devices: 10.2 us -> none  [on_device(): mix_weight = lax.all_gather(shard_mix, 'dp', axis=0, tiled=True)]
    ppermute x4, waiting for transfers between devices: 11.6 us -> 2.99 us  [dp_total(): lax.ppermute(array, 'dp', [(i, i ^ step) for i in range(count)])]
    dot_general x5 -> x6, matrix products: 30.5 us -> 22.6 us  [across_rows(): lax.dot_general(left, right, (((0,), (0,)), ((), ())), preferred_element_...]
  transfers between devices with their start and end apart: 16 -> 30, of which waited for: 14 -> 15; matrix products, arithmetic and copies ran while one was open for 17% -> 26% of each run, Pallas kernels for 9% -> 12%
where the time goes in v3:
time: 416 us; the launch traced here: 408 us
  waiting for transfers between devices  139 us (33%)
  matrix products  88.6 us (21%)
  Pallas kernels  48.3 us (12%)
  local copies, waits for them, and re-layouts  41.6 us (10%)
  other arithmetic  40.7 us (10%)
  starting transfers between devices  34.2 us (8%)
  between operations  15.7 us (4%)
    ppermute x8, waiting for transfers between devices, swap_halves(): return lax.ppermute(array, 'mp', [(0, 1), (1, 0)])  79.4 us
    ppermute x16, waiting for transfers between devices, dp_swap(): return lax.ppermute(array, 'dp', [(i, i ^ bit) for i in range(count)])  56.9 us
    dot_general x4, matrix products, against(): lax.dot_general(left, right, (((1,), (1,)), ((), ())), preferred_element_...  31.2 us
    pallas_call x1, Pallas kernels, mixer_backward(): pl.pallas_call(partial(backward_kernel, heads, chunks), grid_spec=pltpu.P...  25.1 us
    pallas_call x1, Pallas kernels, mixer_forward(): pl.pallas_call(partial(forward_kernel, heads), grid_spec=pltpu.PrefetchSc...  23.2 us
    dot_general x6, matrix products, across_rows(): lax.dot_general(left, right, (((0,), (0,)), ((), ())), preferred_element_...  22.6 us
    unnamed x113, local copies, waits for them, and re-layouts  18.6 us
    ppermute x16, starting transfers between devices, dp_swap(): return lax.ppermute(array, 'dp', [(i, i ^ bit) for i in range(count)])  15.6 us
  transfers between devices with their start and end apart: 30, of which 15 were waited for; matrix products, arithmetic and copies ran while one was open for 26% of the time, Pallas kernels for 12%

profile of v3, /device:TPU:0, one launch (start us, length us, event | category | flops | bytes accessed | tf_op | source)
XLA Modules:
  0.0 408.5 jit_solution(4834499259234283275)
XLA Ops:
  7.3 3.0 collective-permute-start.10
  17.3 3.2 collective-permute-start.1
  23.9 1.9 collective-permute-start
  25.8 2.3 copy.171
  31.3 2.0 collective-permute-start.2
  33.6 15.0 %collective-permute-done.2 = bf16[2,64,768]{2,1,0:T(8,128)(2,1)S(1)} collective-permute-done((bf16[2,64,768]{2,1,0:T(8,128)(2,1)S(1)}, bf16[2,64,768]{2,1,0:T(8,128)(2,1)S(1)}, u32[]{:S(2)}, u32[]{:S(2)}) %collective-permute-start.2) | collective-permute-done | bytes 196640 | tf_op jit(solution)/shard_map/ppermute | solution.py:557
  50.2 10.2 %collective-permute-done.6 = bf16[2,64,896]{2,1,0:T(8,128)(2,1)S(1)} collective-permute-done((bf16[2,64,896]{2,1,0:T(8,128)(2,1)S(1)}, bf16[2,64,896]{2,1,0:T(8,128)(2,1)S(1)}, u32[]{:S(2)}, u32[]{:S(2)}) %collective-permute-start.6) | collective-permute-done | bytes 229408 | tf_op jit(solution)/shard_map/ppermute | solution.py:557
  62.4 15.5 %collective-permute-done.7 = bf16[4,64,896]{2,1,0:T(8,128)(2,1)S(1)} collective-permute-done((bf16[4,64,896]{2,1,0:T(8,128)(2,1)S(1)}, bf16[4,64,896]{2,1,0:T(8,128)(2,1)S(1)}, u32[]{:S(2)}, u32[]{:S(2)}) %collective-permute-start.7) | collective-permute-done | bytes 458784 | tf_op jit(solution)/shard_map/ppermute | solution.py:557
  81.7 7.0 %fusion.11.proj_ref = f32[1024,1664]{1,0:T(8,128)} fusion(bf16[1024,896]{1,0:T(8,128)(2,1)S(1)} %bitcast.184, bf16[1024,768]{1,0:T(8,128)(2,1)S(1)} %bitcast.187, f32[1024]{0:T(1024)S(1)} %copy-done.41, f32[1024]{0:T(1024)S(1)} %add_rsqrt_fusion.1, bf16[512,1024]{0,1:T(8,128)(2,1)S(1)} %get-tuple-element.166, bf16[512,1024]{0,1:T(8,128)(2,1)S(1)} %get-tuple-element.165), kind=kOutput, calls=%fused_computation.33 | convolution fusion | flops 3503816704 | bytes 12328960 | tf_op jit(solution)/shard_map/dot_general | solution.py:695
  88.7 23.2 %mixer_forward.1 = (bf16[1024,512]{1,0:T(8,128)(2,1)}, f32[1024,1024]{1,0:T(8,128)}, f32[1024,512]{1,0:T(8,128)S(1)}, f32[8,2,128,256]{3,2,1,0:T(8,128)S(1)}, f3...) custom-call(s32[16]{0:T(128)S(1)} %get-tuple-element.154.resets_ref,, ...), custom_call_target="tpu_custom_call" | custom-call | tf_op jit(solution)/shard_map/mixer_forward/pallas_call | solution.py:459
  120.7 3.0 broadcast_select_fusion.1
  123.7 19.7 %collective-permute-done.9 = bf16[1024,512]{1,0:T(8,128)(2,1)} collective-permute-done((bf16[1024,512]{1,0:T(8,128)(2,1)}, bf16[1024,512]{1,0:T(8,128)(2,1)}, u32[]{:S(2)}, u32[]{:S(2)}) %collective-permute-start.9) | collective-permute-done | bytes 1048608 | tf_op jit(solution)/shard_map/ppermute | solution.py:543
  143.4 5.3 %multiply_reduce_fusion.3 = (f32[1024]{0:T(1024)S(1)}, f32[1024,1024]{0,1:T(8,128)S(1)}) fusion(bf16[1024,5248]{1,0:T(8,128)(2,1)} %all-gather.2.cloned.1.call-done, bf16[1024,512]{1,0:T(8,128)(2,1)} %collective-permute-done.9, bf16[1024,512]{1,0:T(8,128)(2,1)} %get-tuple-element.34, f32[1024]{0:T(1024)S(1)} %fusion.37, bf16[512,1024]{0,1:T(8,128)(2,1)} %copy-done.25, ...), kind=kOutput, calls=%fused_computation.24 | convolution fusion | flops 2160065536 | bytes 10493952 | tf_op jit(solution)/shard_map/dot_general | solution.py:48
  148.8 13.3 %fusion.3 = f32[1024,2816]{1,0:T(8,128)} fusion(bf16[1024,5248]{1,0:T(8,128)(2,1)} %all-gather.2.cloned.1.call-done, f32[1024,1024]{0,1:T(8,128)S(1)} %get-tuple-element.213, f32[1024]{0:T(1024)S(1)} %copy-done.42, f32[1024]{0:T(1024)S(1)} %add_rsqrt_fusion), kind=kOutput, calls=%fused_computation.13 | convolution fusion | flops 5908725760 | bytes 21504000 | tf_op jit(solution)/shard_map/dot_general | solution.py:704
  162.1 10.9 %multiply_convert_fusion.1 = (bf16[1024,1408]{1,0:T(8,128)(2,1)S(1)}, bf16[1024,1408]{1,0:T(8,128)(2,1)}, bf16[1024,1408]{1,0:T(8,128)(2,1)S(1)}) fusion(f32[1024,2816]{1,0:T(8,128)} %fusion.3, bf16[1024,5248]{1,0:T(8,128)(2,1)} %all-gather.2.cloned.1.call-done, bf16[1024]{0:T(1024)(128)(2,1)S(1)} %fusion.38, bf16[512,1024]{0,1:T(8,128)(2,1)S(1)} %copy-done.32, ...), kind=kOutput, calls=%fused_computation.6 | convolution fusion | flops 2980708352 | bytes 25167872 | tf_op jit(solution)/shard_map/dot_general | solution.py:710
  173.0 9.5 %convolution_convert_fusion = bf16[1024,2816]{1,0:T(8,128)(2,1)S(1)} fusion(bf16[1024,1408]{1,0:T(8,128)(2,1)} %get-tuple-element.159, bf16[1024,1408]{1,0:T(8,128)(2,1)S(1)} %get-tuple-element.158, f32[1024,1024]{0,1:T(8,128)S(1)} %get-tuple-element.213, f32[1024]{0:T(1024)S(1)} %copy-done.42, f32[1024]{0:T(1024)S(1)} %add_rsqrt_fusion), kind=kOutput, calls=%fused_computation.10 | convolution fusion | flops 5923143680 | bytes 15736832 | tf_op jit(solution)/shard_map/dot_general | solution.py:42
  182.5 11.1 %fusion.54 = (bf16[1024,1024]{0,1:T(8,128)(2,1)}, f32[1024,1024]{0,1:T(8,128)}) fusion(bf16[1024,5248]{1,0:T(8,128)(2,1)} %all-gather.2.cloned.1.call-done, bf16[1024,1408]{1,0:T(8,128)(2,1)} %get-tuple-element.159, bf16[1024,1408]{1,0:T(8,128)(2,1)S(1)} %get-tuple-element.158), kind=kOutput, calls=%fused_computation.198 | convolution fusion | flops 5918162944 | bytes 17825792 | tf_op jit(solution)/shard_map/dot_general | solution.py:48
  194.9 3.6 convolution_convert_fusion.1
  198.6 3.8 pad_maximum_fusion
  202.4 6.3 %fusion.8 = f32[1024,1024]{0,1:T(8,128)S(1)} fusion(bf16[1024,1408]{1,0:T(8,128)(2,1)} %copy-done.50, bf16[1024,5248]{1,0:T(8,128)(2,1)} %all-gather.2.cloned.1.call-done), kind=kOutput, calls=%fused_computation.30 | convolution fusion | flops 2952790016 | bytes 9961472 | tf_op jit(solution)/shard_map/dot_general | solution.py:48
  210.0 30.7 %collective-permute-done.12 = bf16[1024,1024]{0,1:T(8,128)(2,1)} collective-permute-done((bf16[1024,1024]{0,1:T(8,128)(2,1)}, bf16[1024,1024]{0,1:T(8,128)(2,1)}, u32[]{:S(2)}, u32[]{:S(2)}) %collective-permute-start.12) | collective-permute-done | bytes 2097184 | tf_op jit(solution)/shard_map/ppermute | solution.py:543
  240.8 4.0 multiply_reduce_fusion
  244.7 3.8 multiply_add_fusion
  248.6 3.6 fusion.22.upstream_ref
  253.9 25.1 %mixer_backward.1 = (bf16[1024,1664]{1,0:T(8,128)(2,1)}, f32[8,1024]{1,0:T(8,128)S(1)}, f32[8,256]{1,0:T(8,128)S(1)}) custom-call(s32[16]{0:T(128)S(1)} %get-tuple-element.154.resets_ref, f32[1024,512]{1,0:T(8,128)S(1)} %fusion.22.upstream_ref, f32[1024,1664]{1,0:T(8,128)} %fusion.11.proj_ref, f32[1024,8]{1,0:T(8,128)S(1)} %copy.167.keep_ref, ...), custom_call_target="tpu_custom_call" | custom-call | tf_op jit(solution)/shard_map/mixer_backward/pallas_call | solution.py:521
  279.0 8.5 %multiply_reduce_fusion.1 = (f32[1024]{0:T(1024)S(1)}, f32[1024,1024]{0,1:T(8,128)}, f32[1024,1024]{0,1:T(8,128)}) fusion(f32[1024]{0:T(1024)S(1)} %add_rsqrt_fusion.1, bf16[512,1024]{0,1:T(8,128)(2,1)S(1)} %copy-done.26, bf16[512,1024]{0,1:T(8,128)(2,1)S(1)} %copy-done.23, bf16[1024,1664]{1,0:T(8,128)(2,1)} %get-tuple-element.45, ...), kind=kOutput, calls=%fused_computation.18 | convolution fusion | flops 3503815680 | bytes 17309696 | tf_op jit(solution)/shard_map/dot_general | solution.py:48
  287.7 1.7 fusion.33
  289.6 4.0 fusion.28
  293.6 2.4 fusion.16
  297.5 2.6 collective-permute-start.16
  300.4 2.3 collective-permute-done.16
  302.8 2.6 pad_maximum_fusion.2
  305.4 5.6 %copy.179 = f32[1024,1024]{1,0:T(8,128)} copy(f32[1024,1024]{0,1:T(8,128)} %pad_maximum_fusion.2) | data formatting | bytes 8388608 | tf_op jit(solution)/shard_map/concatenate | solution.py:746
  311.0 3.5 collective-permute-start.18
  314.5 1.7 fusion.20
  317.1 2.4 collective-permute-start.19
  319.5 2.7 dynamic-slice_convert_fusion.1
  322.2 2.0 collective-permute-start.13
  330.0 2.4 bitcast_add_fusion
  338.6 9.9 %collective-permute-done.14 = bf16[512,1024]{0,1:T(8,128)(2,1)S(1)} collective-permute-done((bf16[512,1024]{0,1:T(8,128)(2,1)}, bf16[512,1024]{0,1:T(8,128)(2,1)S(1)}, u32[]{:S(2)}, u32[]{:S(2)}) %collective-permute-start.14) | collective-permute-done | bytes 1048608 | tf_op jit(solution)/shard_map/ppermute | solution.py:543
  349.6 1.8 copy.183
  351.4 17.5 %collective-permute-done.13 = bf16[512,1024]{0,1:T(8,128)(2,1)} collective-permute-done((bf16[512,1024]{0,1:T(8,128)(2,1)}, bf16[512,1024]{0,1:T(8,128)(2,1)}, u32[]{:S(2)}, u32[]{:S(2)}) %collective-permute-start.13) | collective-permute-done | bytes 1048608 | tf_op jit(solution)/shard_map/ppermute | solution.py:543
  368.8 3.2 add_convert_fusion
  376.3 2.1 collective-permute-start.26
  378.3 6.9 %collective-permute-done.22 = bf16[2,64,1024]{2,1,0:T(8,128)(2,1)S(1)} collective-permute-done((bf16[2,64,1024]{2,1,0:T(8,128)(2,1)S(1)}, bf16[2,64,1024]{2,1,0:T(8,128)(2,1)S(1)}, u32[]{:S(2)}, u32[]{:S(2)}) %collective-permute-start.22) | collective-permute-done | bytes 262176 | tf_op jit(solution)/shard_map/ppermute | solution.py:557
  385.8 2.3 collective-permute-done.26
  389.7 5.6 %collective-permute-done.23 = bf16[1,64,1024]{2,1,0:T(8,128)(2,1)S(1)} collective-permute-done((bf16[1,64,1024]{2,1,0:T(8,128)(2,1)S(1)}, bf16[1,64,1024]{2,1,0:T(8,128)(2,1)S(1)}, u32[]{:S(2)}, u32[]{:S(2)}) %collective-permute-start.23) | collective-permute-done | bytes 131104 | tf_op jit(solution)/shard_map/ppermute | solution.py:557
  399.3 1.9 fusion.48
  (280 shorter events, 60.2 us)
Async XLA Ops:
  7.2 23.9 %copy-start = (f32[4,1024]{1,0:T(4,128)S(1)}, f32[4,1024]{1,0:T(4,128)}, u32[]{:S(2)}) copy-start(f32[4,1024]{1,0:T(4,128)} %param.34) | copy-start | bytes 49156
  7.2 21.1 %copy-start.45 = (s32[16]{0:T(128)S(1)}, s32[16]{0:T(128)}, u32[]{:S(2)}) copy-start(s32[16]{0:T(128)} %param.23) | copy-start | bytes 196
  7.2 21.1 %copy-start.46 = (s32[16]{0:T(128)S(1)}, s32[16]{0:T(128)}, u32[]{:S(2)}) copy-start(s32[16]{0:T(128)} %param.24) | copy-start | bytes 196
  7.2 23.9 %copy-start.44 = (f32[4,512]{1,0:T(4,128)S(1)}, f32[4,512]{1,0:T(4,128)}, u32[]{:S(2)}) copy-start(f32[4,512]{1,0:T(4,128)} %param.32) | copy-start | bytes 24580
  7.2 23.9 %copy-start.43 = (f32[4,512]{1,0:T(4,128)S(1)}, f32[4,512]{1,0:T(4,128)}, u32[]{:S(2)}) copy-start(f32[4,512]{1,0:T(4,128)} %param.33) | copy-start | bytes 24580
  7.2 23.9 %copy-start.47 = (f32[4]{0:T(128)S(1)}, f32[4]{0:T(128)}, u32[]{:S(2)}) copy-start(f32[4]{0:T(128)} %param.35) | copy-start | bytes 52
  7.3 23.9 %copy-start.48 = (f32[4]{0:T(128)S(1)}, f32[4]{0:T(128)}, u32[]{:S(2)}) copy-start(f32[4]{0:T(128)} %param.36) | copy-start | bytes 52
  7.3 136.2 %all-gather.2.cloned.1.call-start = ((), (), s32[]{:S(2)}) async-start(), calls=%async_computation.1 | async-start | bytes 11419648 | tf_op jit(solution)/shard_map/all_gather | solution.py:665
  7.3 5.5 %collective-permute-start.10 = (bf16[64,512]{1,0:T(8,128)(2,1)}, bf16[64,512]{1,0:T(8,128)(2,1)S(1)}, u32[]{:S(2)}, u32[]{:S(2)}) collective-permute-start(bf16[64,512]{1,0:T(8,128)(2,1)} %bitcast.190), channel_id=1, source_target_pairs={{0,1},{1,0},{2,3},{3,2},{4,5},{5,4},{6,7},{7,6},{8,9},{9,8},{10,11... | collective-permute-start | bytes 196616 | tf_op jit(solution)/shard_map/ppermute | solution.py:543
  16.5 380.9 %reduce-scatter.2.cloned.1.call-start = ((), (), s32[]{:S(2)}) async-start(), calls=%async_computation.2 | async-start | bytes 9191424 | tf_op jit(solution)/shard_map/reduce_scatter | solution.py:722
  17.3 14.0 %collective-permute-start.1 = (bf16[1,64,768]{2,1,0:T(8,128)(2,1)S(1)}, bf16[1,64,768]{2,1,0:T(8,128)(2,1)S(1)}, u32[]{:S(2)}, u32[]{:S(2)}) collective-permute-start(bf16[1,64,768]{2,1,0:T(8,128)(2,1)S(1)} %fusion.36), channel_id=1, source_target_pairs={{0,16},{2,18},{4,20},{6,22},{8,24},{10,26},{12,28},{14,30},{16,0},... | collective-permute-start | bytes 294920 | tf_op jit(solution)/shard_map/ppermute | solution.py:557
  22.3 11.0 %collective-permute-start.5 = (bf16[1,64,896]{2,1,0:T(8,128)(2,1)S(1)}, bf16[1,64,896]{2,1,0:T(8,128)(2,1)S(1)}, u32[]{:S(2)}, u32[]{:S(2)}) collective-permute-start(bf16[1,64,896]{2,1,0:T(8,128)(2,1)S(1)} %fusion.35), channel_id=1, source_target_pairs={{0,16},{2,18},{4,20},{6,22},{8,24},{10,26},{12,28},{14,30},{16,0},... | collective-permute-start | bytes 344072 | tf_op jit(solution)/shard_map/ppermute | solution.py:557
  23.9 54.4 %collective-permute-start = (bf16[512,1024]{0,1:T(8,128)(2,1)S(1)}, bf16[512,1024]{0,1:T(8,128)(2,1)S(1)}, u32[]{:S(2)}, u32[]{:S(2)}) collective-permute-start(bf16[512,1024]{0,1:T(8,128)(2,1)S(1)} %copy.157), channel_id=1, source_target_pairs={{0,1},{1,0},{2,3},{3,2},{4,5},{5,4},{6,7},{7,6},{8,9},{9,8},{10,11... | collective-permute-start | bytes 3145736 | tf_op jit(solution)/shard_map/ppermute | solution.py:543
  28.1 92.6 %collective-permute-start.11 = (bf16[512,1024]{0,1:T(8,128)(2,1)}, bf16[512,1024]{0,1:T(8,128)(2,1)}, u32[]{:S(2)}, u32[]{:S(2)}) collective-permute-start(bf16[512,1024]{0,1:T(8,128)(2,1)} %copy.171), channel_id=1, source_target_pairs={{0,1},{1,0},{2,3},{3,2},{4,5},{5,4},{6,7},{7,6},{8,9},{9,8},{10,11... | collective-permute-start | bytes 3145736 | tf_op jit(solution)/shard_map/ppermute | solution.py:543
  31.3 17.2 %collective-permute-start.2 = (bf16[2,64,768]{2,1,0:T(8,128)(2,1)S(1)}, bf16[2,64,768]{2,1,0:T(8,128)(2,1)S(1)}, u32[]{:S(2)}, u32[]{:S(2)}) collective-permute-start(bf16[2,64,768]{2,1,0:T(8,128)(2,1)S(1)} %maximum_bitcast_fusion.1), channel_id=1, source_target_pairs={{0,8},{2,10},{4,12},{6,14},{8,0},{10,2},{12,4},{14,6},{16,24},{18,... | collective-permute-start | bytes 589832 | tf_op jit(solution)/shard_map/ppermute | solution.py:557
  33.4 27.0 %collective-permute-start.6 = (bf16[2,64,896]{2,1,0:T(8,128)(2,1)S(1)}, bf16[2,64,896]{2,1,0:T(8,128)(2,1)S(1)}, u32[]{:S(2)}, u32[]{:S(2)}) collective-permute-start(bf16[2,64,896]{2,1,0:T(8,128)(2,1)S(1)} %maximum_bitcast_fusion), channel_id=1, source_target_pairs={{0,8},{2,10},{4,12},{6,14},{8,0},{10,2},{12,4},{14,6},{16,24},{18,... | collective-permute-start | bytes 688136 | tf_op jit(solution)/shard_map/ppermute | solution.py:557
  48.7 13.4 %collective-permute-start.3 = (bf16[4,64,768]{2,1,0:T(8,128)(2,1)S(1)}, bf16[4,64,768]{2,1,0:T(8,128)(2,1)S(1)}, u32[]{:S(2)}, u32[]{:S(2)}) collective-permute-start(bf16[4,64,768]{2,1,0:T(8,128)(2,1)S(1)} %bitcast.189), channel_id=1, source_target_pairs={{0,4},{2,6},{4,0},{6,2},{8,12},{10,14},{12,8},{14,10},{16,20},{18,... | collective-permute-start | bytes 1179656 | tf_op jit(solution)/shard_map/ppermute | solution.py:557
  60.5 17.4 %collective-permute-start.7 = (bf16[4,64,896]{2,1,0:T(8,128)(2,1)S(1)}, bf16[4,64,896]{2,1,0:T(8,128)(2,1)S(1)}, u32[]{:S(2)}, u32[]{:S(2)}) collective-permute-start(bf16[4,64,896]{2,1,0:T(8,128)(2,1)S(1)} %bitcast.186), channel_id=1, source_target_pairs={{0,4},{2,6},{4,0},{6,2},{8,12},{10,14},{12,8},{14,10},{16,20},{18,... | collective-permute-start | bytes 1376264 | tf_op jit(solution)/shard_map/ppermute | solution.py:557
  62.3 16.7 %collective-permute-start.4 = (bf16[8,64,768]{2,1,0:T(8,128)(2,1)S(1)}, bf16[8,64,768]{2,1,0:T(8,128)(2,1)S(1)}, u32[]{:S(2)}, u32[]{:S(2)}) collective-permute-start(bf16[8,64,768]{2,1,0:T(8,128)(2,1)S(1)} %bitcast.181), channel_id=1, source_target_pairs={{0,2},{2,0},{4,6},{6,4},{8,10},{10,8},{12,14},{14,12},{16,18},{18,... | collective-permute-start | bytes 2359304 | tf_op jit(solution)/shard_map/ppermute | solution.py:557
  78.3 2.5 collective-permute-start.8
  117.9 25.5 %collective-permute-start.9 = (bf16[1024,512]{1,0:T(8,128)(2,1)}, bf16[1024,512]{1,0:T(8,128)(2,1)}, u32[]{:S(2)}, u32[]{:S(2)}) collective-permute-start(bf16[1024,512]{1,0:T(8,128)(2,1)} %get-tuple-element.34), channel_id=1, source_target_pairs={{0,1},{1,0},{2,3},{3,2},{4,5},{5,4},{6,7},{7,6},{8,9},{9,8},{10,11... | collective-permute-start | bytes 3145736 | tf_op jit(solution)/shard_map/ppermute | solution.py:543
  123.7 25.0 %copy-start.42 = (f32[1024]{0:T(1024)S(1)}, f32[1024]{0:T(1024)}, u32[]{:S(2)}) copy-start(f32[1024]{0:T(1024)} %param.39) | copy-start | bytes 12292
  148.8 24.2 %copy-start.15 = (f32[1024,1024]{0,1:T(8,128)}, f32[1024,1024]{0,1:T(8,128)S(1)}, u32[]{:S(2)}) copy-start(f32[1024,1024]{0,1:T(8,128)S(1)} %get-tuple-element.213) | copy-start | bytes 12582916
  173.0 22.0 %copy-start.50 = (bf16[1024,1408]{1,0:T(8,128)(2,1)}, bf16[1024,1408]{1,0:T(8,128)(2,1)S(1)}, u32[]{:S(2)}) copy-start(bf16[1024,1408]{1,0:T(8,128)(2,1)S(1)} %get-tuple-element.160) | copy-start | bytes 8650756
  193.6 47.1 %collective-permute-start.12 = (bf16[1024,1024]{0,1:T(8,128)(2,1)}, bf16[1024,1024]{0,1:T(8,128)(2,1)}, u32[]{:S(2)}, u32[]{:S(2)}) collective-permute-start(bf16[1024,1024]{0,1:T(8,128)(2,1)} %get-tuple-element.214), channel_id=1, source_target_pairs={{0,1},{1,0},{2,3},{3,2},{4,5},{5,4},{6,7},{7,6},{8,9},{9,8},{10,11... | collective-permute-start | bytes 6291464 | tf_op jit(solution)/shard_map/ppermute | solution.py:543
  202.4 38.4 %copy-start.16 = (f32[1024,1024]{0,1:T(8,128)S(1)}, f32[1024,1024]{0,1:T(8,128)}, u32[]{:S(2)}) copy-start(f32[1024,1024]{0,1:T(8,128)} %copy-done.15) | copy-start | bytes 12582916
  202.4 38.4 %copy-start.28 = (f32[1024,1024]{0,1:T(8,128)S(1)}, f32[1024,1024]{0,1:T(8,128)}, u32[]{:S(2)}) copy-start(f32[1024,1024]{0,1:T(8,128)} %get-tuple-element.215) | copy-start | bytes 12582916
  208.6 32.1 %copy-start.34 = (f32[1024,1024]{0,1:T(8,128)}, f32[1024,1024]{0,1:T(8,128)S(1)}, u32[]{:S(2)}) copy-start(f32[1024,1024]{0,1:T(8,128)S(1)} %fusion.8) | copy-start | bytes 12582916
  253.9 25.1 %copy-start.23 = (bf16[512,1024]{0,1:T(8,128)(2,1)S(1)}, bf16[512,1024]{0,1:T(8,128)(2,1)}, u32[]{:S(2)}) copy-start(bf16[512,1024]{0,1:T(8,128)(2,1)} %copy-done.22) | copy-start | bytes 3145732
  253.9 25.1 %copy-start.26 = (bf16[512,1024]{0,1:T(8,128)(2,1)S(1)}, bf16[512,1024]{0,1:T(8,128)(2,1)}, u32[]{:S(2)}) copy-start(bf16[512,1024]{0,1:T(8,128)(2,1)} %copy-done.25) | copy-start | bytes 3145732
  253.9 25.1 %copy-start.37 = (bf16[8,2,64,896]{3,2,1,0:T(8,128)(2,1)S(1)}, bf16[8,2,64,896]{3,2,1,0:T(8,128)(2,1)}, u32[]{:S(2)}) copy-start(bf16[8,2,64,896]{3,2,1,0:T(8,128)(2,1)} %copy-done.36) | copy-start | bytes 5505028
  253.9 25.1 %copy-start.39 = (bf16[8,2,64,768]{3,2,1,0:T(8,128)(2,1)S(1)}, bf16[8,2,64,768]{3,2,1,0:T(8,128)(2,1)}, u32[]{:S(2)}) copy-start(bf16[8,2,64,768]{3,2,1,0:T(8,128)(2,1)} %copy-done.38) | copy-start | bytes 4718596
  289.5 7.9 %collective-permute-start.15 = (f32[12,1024]{1,0:T(8,128)S(1)}, f32[12,1024]{1,0:T(8,128)S(1)}, u32[]{:S(2)}, u32[]{:S(2)}) collective-permute-start(f32[12,1024]{1,0:T(8,128)S(1)} %concatenate.92), channel_id=1, source_target_pairs={{0,2},{2,0},{4,6},{6,4},{8,10},{10,8},{12,14},{14,12},{16,18},{18,... | collective-permute-start | bytes 147464 | tf_op jit(solution)/shard_map/ppermute | solution.py:550
  297.5 5.2 %collective-permute-start.16 = (f32[12,1024]{1,0:T(8,128)S(1)}, f32[12,1024]{1,0:T(8,128)S(1)}, u32[]{:S(2)}, u32[]{:S(2)}) collective-permute-start(f32[12,1024]{1,0:T(8,128)S(1)} %add.188), channel_id=1, source_target_pairs={{0,4},{2,6},{4,0},{6,2},{8,12},{10,14},{12,8},{14,10},{16,20},{18,... | collective-permute-start | bytes 147464 | tf_op jit(solution)/shard_map/ppermute | solution.py:550
  300.3 29.7 %collective-permute-start.24 = (bf16[8,64,1024]{2,1,0:T(8,128)(2,1)S(1)}, bf16[8,64,1024]{2,1,0:T(8,128)(2,1)}, u32[]{:S(2)}, u32[]{:S(2)}) collective-permute-start(bf16[8,64,1024]{2,1,0:T(8,128)(2,1)S(1)} %fusion.21), channel_id=1, source_target_pairs={{0,2},{2,0},{4,6},{6,4},{8,10},{10,8},{12,14},{14,12},{16,18},{18,... | collective-permute-start | bytes 3145736 | tf_op jit(solution)/shard_map/ppermute | solution.py:557
  302.7 8.2 %collective-permute-start.17 = (f32[12,1024]{1,0:T(8,128)S(1)}, f32[12,1024]{1,0:T(8,128)S(1)}, u32[]{:S(2)}, u32[]{:S(2)}) collective-permute-start(f32[12,1024]{1,0:T(8,128)S(1)} %add.189), channel_id=1, source_target_pairs={{0,8},{2,10},{4,12},{6,14},{8,0},{10,2},{12,4},{14,6},{16,24},{18,... | collective-permute-start | bytes 147464 | tf_op jit(solution)/shard_map/ppermute | solution.py:550
  311.0 6.1 %collective-permute-start.18 = (f32[12,1024]{1,0:T(8,128)S(1)}, f32[12,1024]{1,0:T(8,128)S(1)}, u32[]{:S(2)}, u32[]{:S(2)}) collective-permute-start(f32[12,1024]{1,0:T(8,128)S(1)} %add.190), channel_id=1, source_target_pairs={{0,16},{2,18},{4,20},{6,22},{8,24},{10,26},{12,28},{14,30},{16,0},... | collective-permute-start | bytes 147464 | tf_op jit(solution)/shard_map/ppermute | solution.py:550
  316.3 18.5 %collective-permute-start.20 = (bf16[8,64,1024]{2,1,0:T(8,128)(2,1)S(1)}, bf16[8,64,1024]{2,1,0:T(8,128)(2,1)}, u32[]{:S(2)}, u32[]{:S(2)}) collective-permute-start(bf16[8,64,1024]{2,1,0:T(8,128)(2,1)S(1)} %fusion.20), channel_id=1, source_target_pairs={{0,2},{2,0},{4,6},{6,4},{8,10},{10,8},{12,14},{14,12},{16,18},{18,... | collective-permute-start | bytes 3145736 | tf_op jit(solution)/shard_map/ppermute | solution.py:557
  317.1 7.2 %collective-permute-start.19 = (f32[12,1024]{1,0:T(8,128)S(1)}, f32[12,1024]{1,0:T(8,128)S(1)}, u32[]{:S(2)}, u32[]{:S(2)}) collective-permute-start(f32[12,1024]{1,0:T(8,128)S(1)} %add.191), channel_id=1, source_target_pairs={{0,1},{1,0},{2,3},{3,2},{4,5},{5,4},{6,7},{7,6},{8,9},{9,8},{10,11... | collective-permute-start | bytes 147464 | tf_op jit(solution)/shard_map/ppermute | solution.py:543
  322.2 26.3 %collective-permute-start.14 = (bf16[512,1024]{0,1:T(8,128)(2,1)}, bf16[512,1024]{0,1:T(8,128)(2,1)S(1)}, u32[]{:S(2)}, u32[]{:S(2)}) collective-permute-start(bf16[512,1024]{0,1:T(8,128)(2,1)} %dynamic-slice_convert_fusion.1), channel_id=1, source_target_pairs={{0,1},{1,0},{2,3},{3,2},{4,5},{5,4},{6,7},{7,6},{8,9},{9,8},{10,11... | collective-permute-start | bytes 3145736 | tf_op jit(solution)/shard_map/ppermute | solution.py:543
  322.2 46.6 %collective-permute-start.13 = (bf16[512,1024]{0,1:T(8,128)(2,1)}, bf16[512,1024]{0,1:T(8,128)(2,1)}, u32[]{:S(2)}, u32[]{:S(2)}) collective-permute-start(bf16[512,1024]{0,1:T(8,128)(2,1)} %dynamic-slice_convert_fusion.2), channel_id=1, source_target_pairs={{0,1},{1,0},{2,3},{3,2},{4,5},{5,4},{6,7},{7,6},{8,9},{9,8},{10,11... | collective-permute-start | bytes 3145736 | tf_op jit(solution)/shard_map/ppermute | solution.py:543
  330.0 18.5 %copy-start.29 = (f32[1024,1024]{0,1:T(8,128)S(1)}, f32[1024,1024]{0,1:T(8,128)}, u32[]{:S(2)}) copy-start(f32[1024,1024]{0,1:T(8,128)} %get-tuple-element.162) | copy-start | bytes 12582916
  333.3 41.7 %collective-permute-start.25 = (bf16[4,64,1024]{2,1,0:T(8,128)(2,1)}, bf16[4,64,1024]{2,1,0:T(8,128)(2,1)}, u32[]{:S(2)}, u32[]{:S(2)}) collective-permute-start(bf16[4,64,1024]{2,1,0:T(8,128)(2,1)} %fusion.29), channel_id=1, source_target_pairs={{0,4},{2,6},{4,0},{6,2},{8,12},{10,14},{12,8},{14,10},{16,20},{18,... | collective-permute-start | bytes 1572872 | tf_op jit(solution)/shard_map/ppermute | solution.py:557
  337.4 36.0 %collective-permute-start.21 = (bf16[4,64,1024]{2,1,0:T(8,128)(2,1)}, bf16[4,64,1024]{2,1,0:T(8,128)(2,1)}, u32[]{:S(2)}, u32[]{:S(2)}) collective-permute-start(bf16[4,64,1024]{2,1,0:T(8,128)(2,1)} %fusion.30), channel_id=1, source_target_pairs={{0,4},{2,6},{4,0},{6,2},{8,12},{10,14},{12,8},{14,10},{16,20},{18,... | collective-permute-start | bytes 1572872 | tf_op jit(solution)/shard_map/ppermute | solution.py:557
  374.9 10.4 %collective-permute-start.22 = (bf16[2,64,1024]{2,1,0:T(8,128)(2,1)S(1)}, bf16[2,64,1024]{2,1,0:T(8,128)(2,1)S(1)}, u32[]{:S(2)}, u32[]{:S(2)}) collective-permute-start(bf16[2,64,1024]{2,1,0:T(8,128)(2,1)S(1)} %fusion.31), channel_id=1, source_target_pairs={{0,8},{2,10},{4,12},{6,14},{8,0},{10,2},{12,4},{14,6},{16,24},{18,... | collective-permute-start | bytes 786440 | tf_op jit(solution)/shard_map/ppermute | solution.py:557
  376.3 11.8 %collective-permute-start.26 = (bf16[2,64,1024]{2,1,0:T(8,128)(2,1)S(1)}, bf16[2,64,1024]{2,1,0:T(8,128)(2,1)S(1)}, u32[]{:S(2)}, u32[]{:S(2)}) collective-permute-start(bf16[2,64,1024]{2,1,0:T(8,128)(2,1)S(1)} %fusion.32), channel_id=1, source_target_pairs={{0,8},{2,10},{4,12},{6,14},{8,0},{10,2},{12,4},{14,6},{16,24},{18,... | collective-permute-start | bytes 786440 | tf_op jit(solution)/shard_map/ppermute | solution.py:557
  385.4 9.9 %collective-permute-start.23 = (bf16[1,64,1024]{2,1,0:T(8,128)(2,1)S(1)}, bf16[1,64,1024]{2,1,0:T(8,128)(2,1)S(1)}, u32[]{:S(2)}, u32[]{:S(2)}) collective-permute-start(bf16[1,64,1024]{2,1,0:T(8,128)(2,1)S(1)} %dynamic-slice_convert_fusion.7), channel_id=1, source_target_pairs={{0,16},{2,18},{4,20},{6,22},{8,24},{10,26},{12,28},{14,30},{16,0},... | collective-permute-start | bytes 393224 | tf_op jit(solution)/shard_map/ppermute | solution.py:557
  388.2 8.5 %collective-permute-start.27 = (bf16[1,64,1024]{2,1,0:T(8,128)(2,1)S(1)}, bf16[1,64,1024]{2,1,0:T(8,128)(2,1)S(1)}, u32[]{:S(2)}, u32[]{:S(2)}) collective-permute-start(bf16[1,64,1024]{2,1,0:T(8,128)(2,1)S(1)} %dynamic-slice_convert_fusion.6), channel_id=1, source_target_pairs={{0,16},{2,18},{4,20},{6,22},{8,24},{10,26},{12,28},{14,30},{16,0},... | collective-permute-start | bytes 393224 | tf_op jit(solution)/shard_map/ppermute | solution.py:557
  (33 other events, 202.8 us)
Sparse Core Ops, SparseCore 0:
  16.6 102.5 all-gather.1
  202.5 109.3 reduce-scatter.1

commit v4 on v3

--- a/solution.py
+++ b/solution.py
@@ -63,13 +63,13 @@
 NN = ((1,), (0,))
 NT = ((1,), (1,))
 TN = ((0,), (0,))
-FINE_GRAM = False
+FINE_GRAM = True
 FINE_INVERSE = True
 FINE_MERGE = True
 SUBS = 2
-FINE_APPLY = False
-FINE_STATE = False
-FINE_BACK = False
+FINE_APPLY = True
+FINE_STATE = True
+FINE_BACK = True
 
 
 def dot(left, right, dims):
@@ -147,8 +147,11 @@
 
 def forward_kernel(
     heads,
+    base,
     resets_ref,
     proj_ref,
+    before_ref,
+    state_in_ref,
     keep_ref,
     filter_ref,
     rates_ref,
@@ -162,6 +165,7 @@
     written_ref,
     factor_ref,
     grams_ref,
+    state_out_ref,
     rows_buf,
     state_buf,
 ):
@@ -173,8 +177,11 @@
 
     @pl.when(step == 0)
     def _():
-        rows_buf[0:8, :] = jnp.zeros((8, conv_cols), jnp.float32)
-        state_buf[...] = jnp.zeros_like(state_buf)
+        if base == 0:
+            rows_buf[0:8, :] = jnp.zeros((8, conv_cols), jnp.float32)
+        else:
+            rows_buf[0:8, :] = before_ref[:, :conv_cols]
+        state_buf[...] = state_in_ref[...]
 
     rows_buf[8 : 8 + rows, :] = proj_ref[:, :conv_cols]
     conv = rows_buf[8 : 8 + rows, :] * filter_ref[0:1, :]
@@ -194,7 +201,9 @@
     units = [(sub, head) for sub in range(SUBS) for head in range(heads)]
     prepared = []
     for sub, head in units:
-        row, col, reached, reaching, joined, passed = chunk_masks(resets_ref, step * SUBS + sub)
+        row, col, reached, reaching, joined, passed = chunk_masks(
+            resets_ref, base + step * SUBS + sub
+        )
         lower = jnp.where(row >= col, 1.0, 0.0)
         at = slice(sub * ROWS, (sub + 1) * ROWS)
         decay = jnp.broadcast_to(decay_all[at, head : head + 1], (ROWS, ROWS))
@@ -253,12 +262,24 @@
         parts_ref[sub, head] = parts
         written_ref[sub, head] = written
 
+    @pl.when(step == pl.num_programs(0) - 1)
+    def _():
+        state_out_ref[...] = state_buf[...]
+
 
 def backward_kernel(
     heads,
+    base,
     chunks,
     resets_ref,
-    upstream_ref,
+    own_ref,
+    got_ref,
+    resid_ref,
+    cot_ref,
+    ffn_gain_ref,
+    out_weight_ref,
+    dstate_in_ref,
+    later_ref,
     proj_ref,
     keep_ref,
     filter_ref,
@@ -272,25 +293,47 @@
     written_ref,
     factor_ref,
     grams_ref,
-    dproj_ref,
-    dfilter_ref,
-    dsmall_ref,
-    rows_buf,
-    dstate_buf,
+    *tail_refs,
 ):
+    (
+        dproj_ref,
+        dfilter_ref,
+        dsmall_ref,
+        dmix_ref,
+        dresid_ref,
+        dffn_gain_ref,
+        dstate_out_ref,
+        first_ref,
+        rows_buf,
+        dstate_buf,
+    ) = tail_refs[-10:]
     step = pl.program_id(0)
-    chunk = chunks - 1 - step
+    chunk = base + chunks - 1 - step
     qk = heads * DK
     conv_cols = 2 * qk + heads * DV
     proj_cols = conv_cols + heads * DV
 
     @pl.when(step == 0)
     def _():
-        rows_buf[ROWS : ROWS + 8, :] = jnp.zeros((8, conv_cols), jnp.float32)
-        dstate_buf[...] = jnp.zeros_like(dstate_buf)
+        rows_buf[ROWS : ROWS + 8, :] = later_ref[...]
+        dstate_buf[...] = dstate_in_ref[...]
+        dffn_gain_ref[...] = jnp.zeros_like(dffn_gain_ref)
         dfilter_ref[...] = jnp.zeros_like(dfilter_ref)
         dsmall_ref[...] = jnp.zeros_like(dsmall_ref)
 
+    resid = resid_ref[...]
+    inv_resid = lax.rsqrt(jnp.mean(resid * resid, -1, keepdims=True) + EPS)
+    resid_normed = resid * inv_resid
+    ffn_in_own = own_ref[...].astype(jnp.float32)
+    dffn_gain_ref[0:1, :] += jnp.sum(ffn_in_own * resid_normed, 0, keepdims=True)
+    scaled_up = (ffn_in_own + got_ref[...].astype(jnp.float32)) * ffn_gain_ref[...]
+    dresid = cot_ref[...].astype(jnp.float32) + inv_resid * (
+        scaled_up - resid_normed * jnp.mean(scaled_up * resid_normed, -1, keepdims=True)
+    )
+    dresid_ref[...] = dresid
+    dmix = (dresid * keep_ref[:, 2 * KW : 2 * KW + 1]).astype(jnp.bfloat16)
+    dmix_ref[...] = dmix
+    dgated = dot(dmix, out_weight_ref[...], NN)
     row, col, reached, reaching, joined, passed = chunk_masks(resets_ref, chunk)
     lower = jnp.where(row >= col, 1.0, 0.0)
     lower_b = lower.astype(jnp.bfloat16)
@@ -339,7 +382,7 @@
         normed = mixed * inv_o
         gate = proj_ref[:, gate_at]
         sig_g = sigmoid(gate)
-        upstream = upstream_ref[:, v_at]
+        upstream = dgated[:, v_at]
         up_normed = upstream * normed
         dgain = dgain + jnp.sum(up_normed * (gate * sig_g), 0, keepdims=True)
         dproj_ref[:, gate_at] = (
@@ -434,10 +477,71 @@
     dsmall_ref[0:1, :] += dgain
     dsmall_ref[1:2, 0:128] += jnp.sum(dsums, 0, keepdims=True)
 
-
-def mixer_forward(resets, proj, keep, filters, rates, head_gain, heads):
-    row_count, proj_width = proj.shape
+    @pl.when(step == chunks - 1)
+    def _():
+        dstate_out_ref[...] = dstate_buf[...]
+        first_ref[...] = rows_buf[0:8, :]
+
+
+def ffn_kernel(
+    mix_cols,
+    ff_cols,
+    own_ref,
+    other_ref,
+    inputs_ref,
+    cot_ref,
+    keep_ref,
+    gain_ref,
+    weight_ref,
+    *tail_refs,
+):
+    resid_ref, dnormed_ref, summand_ref, normed_ref, acts_ref = tail_refs[-5:]
+    f32 = jnp.float32
+    bf16 = jnp.bfloat16
+    gate_at = slice(mix_cols, mix_cols + ff_cols)
+    up_at = slice(mix_cols + ff_cols, mix_cols + 2 * ff_cols)
+    down_at = slice(mix_cols + 2 * ff_cols, mix_cols + 3 * ff_cols)
+    gated = jnp.concatenate([own_ref[...], other_ref[...]], axis=1)
+    resid = inputs_ref[...].astype(f32) + keep_ref[:, 2 * KW : 2 * KW + 1] * dot(
+        gated, weight_ref[:, :mix_cols], NT
+    )
+    resid_ref[...] = resid
+    inv_rms = lax.rsqrt(jnp.mean(resid * resid, -1, keepdims=True) + EPS)
+    normed = (resid * inv_rms * gain_ref[...]).astype(bf16)
+    normed_ref[...] = normed
+    gate_pre = dot(normed, weight_ref[:, gate_at], NN)
+    up_pre = dot(normed, weight_ref[:, up_at], NN)
+    dhidden = dot(cot_ref[...], weight_ref[:, down_at], NN)
+    sig = sigmoid(gate_pre)
+    active = gate_pre * sig
+    hidden = (active * up_pre).astype(bf16)
+    dgate = (dhidden * up_pre * sig * (1.0 + gate_pre * (1.0 - sig))).astype(bf16)
+    dup = (dhidden * active).astype(bf16)
+    acts_ref[:, :ff_cols] = dgate
+    acts_ref[:, ff_cols : 2 * ff_cols] = dup
+    acts_ref[:, 2 * ff_cols :] = hidden
+    dnormed_ref[...] = (
+        dot(dgate, weight_ref[:, gate_at], NT) + dot(dup, weight_ref[:, up_at], NT)
+    ).astype(bf16)
+    summand_ref[...] = dot(hidden, weight_ref[:, down_at], NT).astype(bf16)
+
+
+def kernel_cost(micros):
+    return pl.CostEstimate(
+        flops=int(micros * 4e9), bytes_accessed=int(micros * 8e6), transcendentals=0
+    )
+
+
+def whole(array):
+    return pl.BlockSpec(array.shape, lambda c, r: (0,) * len(array.shape))
+
+
+def mixer_forward(resets, proj, keep, filters, rates, head_gain, heads, start, stop, state):
+    proj_width = proj.shape[1]
+    row_count = stop - start
     chunks = row_count // ROWS
+    rows = SUBS * ROWS
+    first = start // rows
     conv_cols = 2 * heads * DK + heads * DV
     f32 = jnp.float32
 
@@ -447,23 +551,26 @@
     def saved(rows, cols):
         return jax.ShapeDtypeStruct((chunks, heads, rows, cols), f32)
 
+    def part_block(cols):
+        return pl.BlockSpec((rows, cols), lambda c, r: (c + first, 0))
+
     def row_block(cols):
-        return pl.BlockSpec((SUBS * ROWS, cols), lambda c, r: (c, 0))
+        return pl.BlockSpec((rows, cols), lambda c, r: (c, 0))
 
     def saved_block(rows, cols):
         return pl.BlockSpec((SUBS, heads, rows, cols), lambda c, r: (c, 0, 0, 0))
 
-    def whole(array):
-        return pl.BlockSpec(array.shape, lambda c, r: (0, 0))
-
+    before = max(start // 8 - 1, 0)
     return pl.pallas_call(
-        partial(forward_kernel, heads),
+        partial(forward_kernel, heads, start // ROWS),
         grid_spec=pltpu.PrefetchScalarGridSpec(
             num_scalar_prefetch=1,
             grid=(chunks // SUBS,),
             in_specs=[
-                row_block(proj_width),
-                row_block(keep.shape[1]),
+                part_block(proj_width),
+                pl.BlockSpec((8, proj_width), lambda c, r: (before, 0)),
+                whole(state),
+                part_block(keep.shape[1]),
                 whole(filters),
                 whole(rates),
                 whole(head_gain),
@@ -478,9 +585,10 @@
                 saved_block(ROWS, DV),
                 saved_block(ROWS, ROWS),
                 saved_block(2 * ROWS, ROWS),
+                whole(state),
             ],
             scratch_shapes=[
-                pltpu.VMEM((SUBS * ROWS + 8, conv_cols), f32),
+                pltpu.VMEM((rows + 8, conv_cols), f32),
                 pltpu.VMEM((heads, DK, DV), f32),
             ],
         ),
@@ -494,49 +602,250 @@
             saved(ROWS, DV),
             saved(ROWS, ROWS),
             saved(2 * ROWS, ROWS),
+            jax.ShapeDtypeStruct(state.shape, f32),
         ],
-        compiler_params=pltpu.CompilerParams(vmem_limit_bytes=40 << 20),
+        compiler_params=pltpu.CompilerParams(vmem_limit_bytes=60 << 20),
+        cost_estimate=kernel_cost(24 * row_count / 1024),
         name="mixer_forward",
-    )(resets, proj, keep, filters, rates, head_gain)
-
-
-def mixer_backward(resets, upstream, proj, keep, filters, rates, head_gain, saved, heads):
-    row_count, proj_width = proj.shape
+    )(resets, proj, proj, state, keep, filters, rates, head_gain)
+
+
+def mixer_backward(
+    resets,
+    own,
+    got,
+    resid,
+    cot,
+    ffn_gain,
+    out_weight,
+    dstate,
+    later,
+    proj,
+    keep,
+    filters,
+    rates,
+    head_gain,
+    saved,
+    heads,
+    start,
+    filled,
+):
+    row_count = resid.shape[0]
+    total_rows, proj_width = proj.shape
     chunks = row_count // ROWS
+    first = start // ROWS
     conv_cols = 2 * heads * DK + heads * DV
     f32 = jnp.float32
 
     def row_block(array):
         return pl.BlockSpec((ROWS, array.shape[1]), lambda c, r: (chunks - 1 - c, 0))
 
+    def part_block(array):
+        return pl.BlockSpec((ROWS, array.shape[1]), lambda c, r: (first + chunks - 1 - c, 0))
+
     def saved_block(array):
         return pl.BlockSpec((1,) + array.shape[1:], lambda c, r: (chunks - 1 - c, 0, 0, 0))
 
-    def whole(array):
-        return pl.BlockSpec(array.shape, lambda c, r: (0, 0))
-
-    dproj = jax.ShapeDtypeStruct((row_count, proj_width), jnp.bfloat16)
+    dproj = jax.ShapeDtypeStruct((total_rows, proj_width), jnp.bfloat16)
     dfilter = jax.ShapeDtypeStruct((8, conv_cols), f32)
     dsmall = jax.ShapeDtypeStruct((8, DV), f32)
+    dmix = jax.ShapeDtypeStruct(resid.shape, jnp.bfloat16)
+    dresid = jax.ShapeDtypeStruct(resid.shape, f32)
+    dffn_gain = jax.ShapeDtypeStruct((8, resid.shape[1]), f32)
+    args = [resets, own, got, resid, cot, ffn_gain, out_weight, dstate, later]
+    args += [proj, keep, filters, rates, head_gain, *saved]
+    specs = [row_block(own), row_block(got), row_block(resid), part_block(cot), whole(ffn_gain)]
+    specs += [
+        pl.BlockSpec(
+            (resid.shape[1], heads * DV), lambda c, r: (0, 0), pipeline_mode=pl.Buffered(1)
+        )
+    ]
+    specs += [whole(dstate), whole(later), part_block(proj), part_block(keep)]
+    specs += [whole(filters), whole(rates), whole(head_gain)]
+    specs += [row_block(saved[0]), row_block(saved[1])]
+    specs += [saved_block(array) for array in saved[2:]]
+    aliases = {}
+    if filled is not None:
+        aliases = {len(args): 0}
+        args.append(filled)
+        specs.append(pl.BlockSpec(memory_space=pl.ANY))
     return pl.pallas_call(
-        partial(backward_kernel, heads, chunks),
+        partial(backward_kernel, heads, first, chunks),
         grid_spec=pltpu.PrefetchScalarGridSpec(
             num_scalar_prefetch=1,
             grid=(chunks,),
-            in_specs=[row_block(upstream), row_block(proj), row_block(keep)]
-            + [whole(filters), whole(rates), whole(head_gain)]
-            + [row_block(saved[0]), row_block(saved[1])]
-            + [saved_block(array) for array in saved[2:]],
-            out_specs=[row_block(dproj), whole(dfilter), whole(dsmall)],
+            in_specs=specs,
+            out_specs=[
+                part_block(dproj),
+                whole(dfilter),
+                whole(dsmall),
+                row_block(dmix),
+                row_block(dresid),
+                whole(dffn_gain),
+                whole(dstate),
+                whole(later),
+            ],
             scratch_shapes=[
                 pltpu.VMEM((ROWS + 8, conv_cols), f32),
                 pltpu.VMEM((heads, DK, DV), f32),
             ],
         ),
-        out_shape=[dproj, dfilter, dsmall],
-        compiler_params=pltpu.CompilerParams(vmem_limit_bytes=40 << 20),
+        out_shape=[
+            dproj,
+            dfilter,
+            dsmall,
+            dmix,
+            dresid,
+            dffn_gain,
+            jax.ShapeDtypeStruct(dstate.shape, f32),
+            jax.ShapeDtypeStruct(later.shape, f32),
+        ],
+        input_output_aliases=aliases,
+        compiler_params=pltpu.CompilerParams(vmem_limit_bytes=60 << 20),
+        cost_estimate=kernel_cost(30 * row_count / 1024),
         name="mixer_backward",
-    )(resets, upstream, proj, keep, filters, rates, head_gain, *saved)
+    )(*args)
+
+
+def ffn_both_ways(own, other, inputs, cot_masked, keep, gain, weight, ff_cols, start, filled):
+    row_count, own_cols = own.shape
+    total_rows, width = inputs.shape
+    rows = 256
+    first = start // rows
+    bf16 = jnp.bfloat16
+
+    def whole(array, **mode):
+        return pl.BlockSpec(array.shape, lambda c: (0, 0), **mode)
+
+    def row_block(cols):
+        return pl.BlockSpec((rows, cols), lambda c: (c, 0))
+
+    def part_block(cols):
+        return pl.BlockSpec((rows, cols), lambda c: (c + first, 0))
+
+    args = [own, other, inputs, cot_masked, keep, gain, weight]
+    specs = [row_block(own_cols), row_block(own_cols), part_block(width), part_block(width)]
+    specs += [part_block(keep.shape[1]), whole(gain)]
+    specs += [whole(weight, pipeline_mode=pl.Buffered(1))]
+    aliases = {}
+    if filled is not None:
+        aliases = {len(args): 3, len(args) + 1: 4}
+        args += list(filled)
+        specs += [pl.BlockSpec(memory_space=pl.ANY)] * 2
+    return pl.pallas_call(
+        partial(ffn_kernel, 2 * own_cols, ff_cols),
+        grid=(row_count // rows,),
+        in_specs=specs,
+        out_specs=[
+            row_block(width),
+            row_block(width),
+            row_block(width),
+            part_block(width),
+            part_block(3 * ff_cols),
+        ],
+        out_shape=[
+            jax.ShapeDtypeStruct((row_count, width), jnp.float32),
+            jax.ShapeDtypeStruct((row_count, width), bf16),
+            jax.ShapeDtypeStruct((row_count, width), bf16),
+            jax.ShapeDtypeStruct((total_rows, width), bf16),
+            jax.ShapeDtypeStruct((total_rows, 3 * ff_cols), bf16),
+        ],
+        input_output_aliases=aliases,
+        compiler_params=pltpu.CompilerParams(vmem_limit_bytes=60 << 20),
+        cost_estimate=kernel_cost(28 * row_count / 1024),
+        name="ffn_both_ways",
+    )(*args)
+
+
+def grads_kernel(
+    shard_rows,
+    side_ref,
+    normed_ref,
+    dproj_ref,
+    dmix_lo_ref,
+    dmix_hi_ref,
+    gated_lo_ref,
+    gated_hi_ref,
+    mine_a_ref,
+    mine_b_ref,
+    theirs_a_ref,
+    theirs_b_ref,
+    rate_ref,
+):
+    side = side_ref[0]
+    normed = normed_ref[...]
+    gate_cols = gated_lo_ref.shape[1]
+    first_cols = mine_a_ref.shape[1]
+
+    def put(grad, mine_ref, theirs_ref, cols):
+        pairs = grad.reshape(-1, 2, shard_rows, grad.shape[-1])
+        even = pairs[:, 0].reshape(-1, grad.shape[-1])
+        odd = pairs[:, 1].reshape(-1, grad.shape[-1])
+        mine_ref[:, cols] = jnp.where(side == 0, even, odd)
+        theirs_ref[:, cols] = jnp.where(side == 0, odd, even).astype(jnp.bfloat16)
+
+    put(dot(normed, dproj_ref[:, :first_cols], TN), mine_a_ref, theirs_a_ref, slice(None))
+    put(
+        dot(normed, dproj_ref[:, first_cols : first_cols + gate_cols], TN),
+        mine_b_ref,
+        theirs_b_ref,
+        slice(0, gate_cols),
+    )
+    put(
+        dot(dmix_lo_ref[...], gated_lo_ref[...], TN)
+        + dot(dmix_hi_ref[...], gated_hi_ref[...], TN),
+        mine_b_ref,
+        theirs_b_ref,
+        slice(gate_cols, 2 * gate_cols),
+    )
+    rate_ref[...] = dot(dproj_ref[:, first_cols + gate_cols :], normed, TN)[:8]
+
+
+def mixer_weight_grads(side, normed, dproj, dmix_lo, dmix_hi, gated_lo, gated_hi, shard_rows):
+    rows, width = normed.shape
+    half_rows, v_cols = gated_lo.shape
+    tile = 256
+    first_cols = 2 * v_cols
+    bf16 = jnp.bfloat16
+
+    def column_block(array):
+        return pl.BlockSpec((array.shape[0], tile), lambda c, r: (0, c))
+
+    def row_block(cols):
+        return pl.BlockSpec((tile // 2, cols), lambda c, r: (c, 0))
+
+    return pl.pallas_call(
+        partial(grads_kernel, shard_rows),
+        grid_spec=pltpu.PrefetchScalarGridSpec(
+            num_scalar_prefetch=1,
+            grid=(width // tile,),
+            in_specs=[
+                column_block(normed),
+                whole(dproj),
+                column_block(dmix_lo),
+                column_block(dmix_hi),
+                whole(gated_lo),
+                whole(gated_hi),
+            ],
+            out_specs=[
+                row_block(first_cols),
+                row_block(first_cols),
+                row_block(first_cols),
+                row_block(first_cols),
+                pl.BlockSpec((8, tile), lambda c, r: (0, c)),
+            ],
+        ),
+        out_shape=[
+            jax.ShapeDtypeStruct((width // 2, first_cols), jnp.float32),
+            jax.ShapeDtypeStruct((width // 2, first_cols), jnp.float32),
+            jax.ShapeDtypeStruct((width // 2, first_cols), bf16),
+            jax.ShapeDtypeStruct((width // 2, first_cols), bf16),
+            jax.ShapeDtypeStruct((8, width), jnp.float32),
+        ],
+        compiler_params=pltpu.CompilerParams(vmem_limit_bytes=60 << 20),
+        cost_estimate=kernel_cost(8),
+        name="mixer_weight_grads",
+    )(side, normed, dproj, dmix_lo, dmix_hi, gated_lo, gated_hi)
 
 
 def swap_halves(array):
@@ -573,12 +882,15 @@
     return [piece.reshape(-1, piece.shape[-1]) for piece in pieces]
 
 
-def dp_scatter(pieces):
+def dp_scatter(kept, sent):
     index = lax.axis_index("dp")
     count = lax.axis_size("dp")
-    pieces = [piece.reshape(count, -1, piece.shape[-1]) for piece in pieces]
-    bit = 1
+    f32 = jnp.float32
+    pieces = [mine + dp_swap(theirs, 1).astype(f32) for mine, theirs in zip(kept, sent)]
+    bit = 2
     while bit < count:
+        blocks = count // bit
+        pieces = [piece.reshape(blocks, -1, piece.shape[-1]) for piece in pieces]
         side = (index & bit) // bit
         pairs = [piece.reshape((-1, 2) + piece.shape[1:]) for piece in pieces]
         others = [
@@ -588,11 +900,11 @@
             for pair in pairs
         ]
         pieces = [
-            lax.dynamic_index_in_dim(pair, side, 1, False) + other.astype(jnp.float32)
+            lax.dynamic_index_in_dim(pair, side, 1, False) + other.astype(f32)
             for pair, other in zip(pairs, others)
         ]
         bit *= 2
-    return [piece[0] for piece in pieces]
+    return [piece.reshape(-1, piece.shape[-1]) for piece in pieces]
 
 
 def in_order(own, other, model_index, axis):
@@ -663,9 +975,6 @@
     out_other = swap_halves(out_rows)
     shard_rest = jnp.concatenate([out_rows, out_other, ffn_gate, ffn_up, ffn_down.T], axis=1)
     rest_weight = lax.all_gather(shard_rest, "dp", axis=0, tiled=True)
-    out_both = rest_weight[:, : 2 * v_cols]
-    ffn_in_weight = rest_weight[:, 2 * v_cols : 2 * v_cols + 2 * ff_cols]
-    down_weight = rest_weight[:, 2 * v_cols + 2 * ff_cols :]
     cot_other = swap_halves(cotangent)
 
     filters = jnp.concatenate(
@@ -687,41 +996,50 @@
         jnp.concatenate([keep_masks[offset, offset:], jnp.ones((offset,), f32)])
         for offset in range(KW)
     ]
-    keep_cols = jnp.stack([keep_masks[offset] for offset in range(KW)] + later_masks, axis=1)
-    inputs_f = in_order(block_input, input_other, model_index, 0).astype(f32)
+    keep_cols = jnp.stack(
+        [keep_masks[offset] for offset in range(KW)] + later_masks + [valid_rows] * 8, axis=1
+    )
+    inputs_b = in_order(block_input, input_other, model_index, 0)
+    inputs_f = inputs_b.astype(f32)
     cot_all = in_order(cotangent, cot_other, model_index, 0)
     normed1, inv_rms1 = rms_forward(inputs_f)
     mixed_in = (normed1 * mix_gain).astype(bf16)
     proj = jnp.dot(mixed_in, mix_weight, preferred_element_type=f32)
     cuts = (qk_cols, 2 * qk_cols, 2 * qk_cols + v_cols, proj_cols)
-    gated_b, *saved = mixer_forward(
-        restarts, proj, keep_cols, filters, rates, gain_row, heads_local
-    )
-    gated_both = jnp.concatenate([gated_b, swap_halves(gated_b)], axis=1)
-    resid = inputs_f + valid_all * against(gated_both, out_both)
-    normed2, inv_rms2 = rms_forward(resid)
-    ffn_in = (normed2 * ffn_gain).astype(bf16)
-    pre = jnp.dot(ffn_in, ffn_in_weight, preferred_element_type=f32)
-    gate_pre, up_pre = pre[:, :ff_cols], pre[:, ff_cols:]
-    sigmoid_gate = jax.nn.sigmoid(gate_pre)
-    activated = gate_pre * sigmoid_gate
-    hidden = (activated * up_pre).astype(bf16)
+    middle = row_count // 2
+    zero_state = jnp.zeros((heads_local, DK, DV), f32)
+    small_args = (keep_cols, filters, rates, gain_row)
+    gated_lo, *saved_lo, carried = mixer_forward(
+        restarts, proj, *small_args, heads_local, 0, middle, zero_state
+    )
     cot_masked = cot_all * valid_all.astype(bf16)
-    hidden_grad = jnp.dot(cot_masked, down_weight, preferred_element_type=f32)
-    gate_grad_pre = (
-        hidden_grad * up_pre * sigmoid_gate * (1.0 + gate_pre * (1.0 - sigmoid_gate))
-    ).astype(bf16)
-    up_grad_pre = (hidden_grad * activated).astype(bf16)
-    pre_grad = jnp.concatenate([gate_grad_pre, up_grad_pre], axis=1)
-    ffn_in_part = against(pre_grad, ffn_in_weight)
-    ffn_in_sent = ffn_in_part.astype(bf16)
+    ffn_row = ffn_gain[None]
+    carried, cot_all, cot_masked, inputs_b = lax.optimization_barrier(
+        (carried, cot_all, cot_masked, inputs_b)
+    )
+    gated_hi, *saved_hi, _ = mixer_forward(
+        restarts, proj, *small_args, heads_local, middle, row_count, carried
+    )
+    other_lo = swap_halves(gated_lo)
+    gated_sent, other_lo = lax.optimization_barrier((gated_hi, other_lo))
+    other_hi = swap_halves(gated_sent)
+    ffn_args = (inputs_b, cot_masked, keep_cols, ffn_row, rest_weight, ff_cols)
+    resid_hi, dnormed_hi, summand_hi, *filled = ffn_both_ways(
+        gated_hi, other_hi, *ffn_args, middle, None
+    )
+    resid_lo, dnormed_lo, summand_lo, ffn_in, acts = ffn_both_ways(
+        gated_lo, other_lo, *ffn_args, 0, filled
+    )
     rest_grads = jnp.concatenate(
-        [across_rows(ffn_in, pre_grad).astype(bf16), across_rows(cot_masked, hidden).astype(bf16)],
+        [
+            across_rows(ffn_in, acts[:, : 2 * ff_cols]).astype(bf16),
+            across_rows(cot_masked, acts[:, 2 * ff_cols :]).astype(bf16),
+        ],
         axis=1,
     )
     ffn_shard = lax.psum_scatter(rest_grads, "dp", scatter_dimension=0, tiled=True)
-    ffn_in_got, _ = lax.optimization_barrier((swap_halves(ffn_in_sent), rest_grads))
-    ffn_in_grad = ffn_in_sent.astype(f32) + ffn_in_got.astype(f32)
+    got_hi, _ = lax.optimization_barrier((swap_halves(dnormed_hi), rest_grads))
+    got_lo = swap_halves(dnormed_lo)
 
     def own_half(array):
         return lax.dynamic_slice_in_dim(array, model_index * local_rows, local_rows, 0)
@@ -729,34 +1047,87 @@
     def other_half(array):
         return lax.dynamic_slice_in_dim(array, (1 - model_index) * local_rows, local_rows, 0)
 
-    ffn_part = against(hidden, down_weight)
-    ffn_sent, _ = lax.optimization_barrier((other_half(ffn_part).astype(bf16), ffn_in_got))
-    ffn_sum = own_half(ffn_part) + swap_halves(ffn_sent).astype(f32)
-    block_output = (own_half(resid) + own_half(valid_all) * ffn_sum).astype(bf16)
-    ffn_gain_part = jnp.sum(ffn_in_part * normed2, 0)
-    resid_grad = cot_all.astype(f32) + rms_backward(ffn_in_grad * ffn_gain, normed2, inv_rms2)
-    mix_cot = (resid_grad * valid_all).astype(bf16)
-    gated_grad = jnp.dot(mix_cot, out_both[:, :v_cols], preferred_element_type=f32)
-    proj_grad, filter_grads, small_grads = mixer_backward(
-        restarts, gated_grad, proj, keep_cols, filters, rates, gain_row, saved, heads_local
-    )
-    split_at = cuts[1]
-    mix_shards = dp_scatter(
-        [
-            jnp.concatenate(
-                [across_rows(mix_cot, gated_b), across_rows(mixed_in, proj_grad[:, :split_at])],
-                axis=1,
-            ),
-            across_rows(mixed_in, proj_grad[:, split_at:proj_cols]),
-        ]
-    )
-    rate_grads = across_rows(proj_grad[:, proj_cols:], mixed_in)[: 2 * heads_local]
+    def own_of(low, high):
+        return jnp.where(model_index == 0, low, high)
+
+    zero_rows = jnp.zeros((8, proj_cols - v_cols), f32)
+    proj_grad, filter_hi, small_hi, dmix_hi, dresid_hi, ffn_gain_hi, carried, later = (
+        mixer_backward(
+            restarts,
+            dnormed_hi,
+            got_hi,
+            resid_hi,
+            cot_all,
+            ffn_row,
+            rest_weight,
+            zero_state,
+            zero_rows,
+            proj,
+            *small_args,
+            saved_hi,
+            heads_local,
+            middle,
+            None,
+        )
+    )
+    summand_sent, got_lo, proj_grad = lax.optimization_barrier(
+        (own_of(summand_hi, summand_lo), got_lo, proj_grad)
+    )
+    proj_grad, filter_lo, small_lo, dmix_lo, dresid_lo, ffn_gain_lo, _, _ = mixer_backward(
+        restarts,
+        dnormed_lo,
+        got_lo,
+        resid_lo,
+        cot_all,
+        ffn_row,
+        rest_weight,
+        carried,
+        later,
+        proj,
+        *small_args,
+        saved_lo,
+        heads_local,
+        0,
+        proj_grad,
+    )
+    summand_got, proj_grad, dmix_lo, filter_lo, small_lo, dresid_lo, ffn_gain_lo = (
+        lax.optimization_barrier(
+            (
+                swap_halves(summand_sent),
+                proj_grad,
+                dmix_lo,
+                filter_lo,
+                small_lo,
+                dresid_lo,
+                ffn_gain_lo,
+            )
+        )
+    )
+    ffn_sum = own_of(summand_lo, summand_hi).astype(f32) + summand_got.astype(f32)
+    block_output = (own_of(resid_lo, resid_hi) + own_half(valid_all) * ffn_sum).astype(bf16)
+    filter_grads = filter_lo + filter_hi
+    small_grads = small_lo + small_hi
+    ffn_gain_part = ffn_gain_lo[0] + ffn_gain_hi[0]
+    *grad_pieces, rate_grads = mixer_weight_grads(
+        (dp_index & 1).reshape(1),
+        mixed_in,
+        proj_grad,
+        dmix_lo,
+        dmix_hi,
+        gated_lo,
+        gated_hi,
+        shard_rows,
+    )
+    rate_grads = rate_grads[: 2 * heads_local]
+    mix_shards = dp_scatter(grad_pieces[:2], grad_pieces[2:])
+    proj_grad, _ = lax.optimization_barrier((proj_grad, rate_grads))
     mix_in_part = against(proj_grad, mix_weight)
-    mix_in_sum = own_half(mix_in_part) + swap_halves(
-        other_half(mix_in_part).astype(bf16)
-    ).astype(f32)
+    mix_in_got, _ = lax.optimization_barrier(
+        (swap_halves(other_half(mix_in_part).astype(bf16)), mix_shards[0])
+    )
+    mix_in_sum = own_half(mix_in_part) + mix_in_got.astype(f32)
     mix_gain_part = jnp.sum(mix_in_part * normed1, 0)
-    input_grad = own_half(resid_grad) + rms_backward(
+    input_grad = own_of(dresid_lo, dresid_hi) + rms_backward(
         mix_in_sum * mix_gain, own_half(normed1), own_half(inv_rms1)
     )
     common = jnp.concatenate(
@@ -776,7 +1147,7 @@
         axis=0,
     )
     totals = dp_total(jnp.concatenate([common, split_rows], axis=0))
-    totals_other = swap_halves(totals)
+    totals_other, _ = lax.optimization_barrier((swap_halves(totals), mix_shards[1]))
     common = totals[:3] + totals_other[:3]
     lower = jnp.where(model_index == 0, totals, totals_other)[3:]
     upper = jnp.where(model_index == 0, totals_other, totals)[3:]
@@ -810,16 +1181,15 @@
             ]
         )
 
-    mix_shard = jnp.concatenate([mix_shards[0][:, v_cols:], mix_shards[1]], axis=1)
     ffn_shard = ffn_shard.astype(f32)
     return (
         block_output,
         input_grad,
         common[0],
-        mix_shard[:, : cuts[0]],
-        mix_shard[:, cuts[0] : cuts[1]],
-        mix_shard[:, cuts[1] : cuts[2]],
-        mix_shard[:, cuts[2] : cuts[3]],
+        mix_shards[0][:, : cuts[0]],
+        mix_shards[0][:, cuts[0] : cuts[1]],
+        mix_shards[0][:, cuts[1] :],
+        mix_shards[1][:, :v_cols],
         rate_weight_grad(0),
         rate_weight_grad(heads_local),
         joined(at_q, q_rows, qk_cols),
@@ -828,7 +1198,7 @@
         rate_grad(0),
         rate_grad(heads_local),
         common[2, :DV],
-        mix_shards[0][:, :v_cols].T,
+        mix_shards[1][:, v_cols:].T,
         common[1],
         ffn_shard[:, :ff_cols],
         ffn_shard[:, ff_cols : 2 * ff_cols],

time: 416 us -> 391 us (0.940)
  Pallas kernels: 48.3 us -> 127 us
  matrix products: 88.6 us -> 29 us
  waiting for transfers between devices: 139 us -> 101 us
  local copies, waits for them, and re-layouts: 41.6 us -> 33.2 us
    pallas_call x2 -> x7, Pallas kernels: 48.3 us -> 127 us  [the longest x2 44.4 us: mixer_backward(): pl.pallas_call(partial(backward_kernel, heads, first, chunks), grid_spec=...]
    ppermute x8 -> x10, waiting for transfers between devices: 79.4 us -> 34.2 us  [swap_halves(): return lax.ppermute(array, 'mp', [(0, 1), (1, 0)])]
    dot_general x3 -> x0, matrix products: 27.7 us -> none  [the longest x1 13.3 us: on_device(): pre = jnp.dot(ffn_in, ffn_in_weight, preferred_element_type=f32)]
    dot_general x4 -> x1, matrix products: 31.2 us -> 9.88 us  [against(): lax.dot_general(left, right, (((1,), (1,)), ((), ())), preferred_element_...]
    dot_general x6 -> x2, matrix products: 22.6 us -> 12.7 us  [across_rows(): lax.dot_general(left, right, (((0,), (0,)), ((), ())), preferred_element_...]
    unnamed x113 -> x107, local copies, waits for them, and re-layouts: 18.6 us -> 9.79 us
    concatenate x1 -> x0, local copies, waits for them, and re-layouts: 5.59 us -> none  [on_device(): jnp.concatenate([across_rows(mix_cot, gated_b), across_rows(mixed_in, pro...]
    ppermute x4, waiting for transfers between devices: 2.99 us -> 7.38 us  [dp_total(): lax.ppermute(array, 'dp', [(i, i ^ step) for i in range(count)])]
  transfers between devices with their start and end apart: 30 -> 32, of which waited for: 15 -> 12; matrix products, arithmetic and copies ran while one was open for 26% -> 21% of each run, Pallas kernels for 12% -> 23%
where the time goes in v4:
time: 391 us; the launch traced here: 385 us
  Pallas kernels  127 us (32%)
  waiting for transfers between devices  101 us (26%)
  other arithmetic  44.4 us (11%)
  starting transfers between devices  34.3 us (9%)
  local copies, waits for them, and re-layouts  33.2 us (8%)
  matrix products  29 us (7%)
  between operations  15.6 us (4%)
    ppermute x16, waiting for transfers between devices, dp_swap(): return lax.ppermute(array, 'dp', [(i, i ^ bit) for i in range(count)])  59.6 us
    pallas_call x2, Pallas kernels, mixer_backward(): pl.pallas_call(partial(backward_kernel, heads, first, chunks), grid_spec=...  44.4 us
    pallas_call x2, Pallas kernels, ffn_both_ways(): pl.pallas_call(partial(ffn_kernel, 2 * own_cols, ff_cols), grid=(row_coun...  37.2 us
    pallas_call x2, Pallas kernels, mixer_forward(): pl.pallas_call(partial(forward_kernel, heads, start // ROWS), grid_spec=p...  35.6 us
    ppermute x10, waiting for transfers between devices, swap_halves(): return lax.ppermute(array, 'mp', [(0, 1), (1, 0)])  34.2 us
    ppermute x16, starting transfers between devices, dp_swap(): return lax.ppermute(array, 'dp', [(i, i ^ bit) for i in range(count)])  17.6 us
    ppermute x10, starting transfers between devices, swap_halves(): return lax.ppermute(array, 'mp', [(0, 1), (1, 0)])  13.3 us
    dot_general x2, matrix products, across_rows(): lax.dot_general(left, right, (((0,), (0,)), ((), ())), preferred_element_...  12.7 us
  transfers between devices with their start and end apart: 32, of which 12 were waited for; matrix products, arithmetic and copies ran while one was open for 21% of the time, Pallas kernels for 23%

profile of v4, /device:TPU:0, one launch (start us, length us, event | category | flops | bytes accessed | tf_op | source)
XLA Modules:
  0.0 384.9 jit_solution(7379427100692622660)
XLA Ops:
  7.3 3.0 collective-permute-start.11
  11.2 1.6 collective-permute-done.11
  17.4 3.2 collective-permute-start.1
  21.0 1.8 collective-permute-start
  32.5 1.9 collective-permute-start.2
  35.7 14.0 %collective-permute-done.2 = bf16[2,64,768]{2,1,0:T(8,128)(2,1)S(1)} collective-permute-done((bf16[2,64,768]{2,1,0:T(8,128)(2,1)S(1)}, bf16[2,64,768]{2,1,0:T(8,128)(2,1)S(1)}, u32[]{:S(2)}, u32[]{:S(2)}) %collective-permute-start.2) | collective-permute-done | bytes 196640 | tf_op jit(solution)/shard_map/ppermute | solution.py:866
  49.8 1.7 collective-permute-start.3
  51.4 8.9 %collective-permute-done.6 = bf16[2,64,896]{2,1,0:T(8,128)(2,1)S(1)} collective-permute-done((bf16[2,64,896]{2,1,0:T(8,128)(2,1)S(1)}, bf16[2,64,896]{2,1,0:T(8,128)(2,1)S(1)}, u32[]{:S(2)}, u32[]{:S(2)}) %collective-permute-start.6) | collective-permute-done | bytes 229408 | tf_op jit(solution)/shard_map/ppermute | solution.py:866
  60.5 1.5 collective-permute-start.7
  63.0 15.5 %collective-permute-done.7 = bf16[4,64,896]{2,1,0:T(8,128)(2,1)S(1)} collective-permute-done((bf16[4,64,896]{2,1,0:T(8,128)(2,1)S(1)}, bf16[4,64,896]{2,1,0:T(8,128)(2,1)S(1)}, u32[]{:S(2)}, u32[]{:S(2)}) %collective-permute-start.7) | collective-permute-done | bytes 458784 | tf_op jit(solution)/shard_map/ppermute | solution.py:866
  78.9 1.5 broadcast_select_fusion.2
  81.7 1.8 pad_maximum_fusion.4.inputs_ref
  83.5 2.4 broadcast_multiply_fusion
  87.5 6.4 %fusion.8.proj_ref.before_ref = f32[1024,1664]{1,0:T(8,128)} fusion(bf16[1024,1024]{1,0:T(8,128)(2,1)S(1)} %multiply_convert_fusion.normed_ref, bf16[1024,896]{1,0:T(8,128)(2,1)S(1)} %bitcast.171, bf16[1024,768]{1,0:T(8,128)(2,1)S(1)} %bitcast.174), kind=kOutput, calls=%fused_computation.13 | convolution fusion | flops 3496476672 | bytes 12320768 | tf_op jit(solution)/shard_map/dot_general | solution.py:1007
  94.7 17.9 %mixer_forward.2 = (bf16[512,512]{1,0:T(8,128)(2,1)}, f32[512,1024]{1,0:T(8,128)}, f32[512,512]{1,0:T(8,128)}, f32[4,2,128,256]{3,2,1,0:T(8,128)}, f32[4,2,128,1...) custom-call(s32[16]{0:T(128)} %get-tuple-element.160.resets_ref, ...), custom_call_target="tpu_custom_call" | custom-call | flops 48000000000 | bytes 96000000 | tf_op jit(solution)/shard_map/mixer_forward/pallas_call | solution.py:564
  112.6 1.4 collective-permute-start.10
  114.0 17.7 %mixer_forward.3 = (bf16[512,512]{1,0:T(8,128)(2,1)}, f32[512,1024]{1,0:T(8,128)}, f32[512,512]{1,0:T(8,128)}, f32[4,2,128,256]{3,2,1,0:T(8,128)}, f32[4,2,128,1...) custom-call(s32[16]{0:T(128)} %get-tuple-element.160.resets_ref, ...), custom_call_target="tpu_custom_call" | custom-call | flops 48000000000 | bytes 96000000 | tf_op jit(solution)/shard_map/mixer_forward/pallas_call | solution.py:564
  132.5 13.5 %collective-permute-done.12.other_ref = bf16[512,512]{1,0:T(8,128)(2,1)S(1)} collective-permute-done((bf16[512,512]{1,0:T(8,128)(2,1)}, bf16[512,512]{1,0:T(8,128)(2,1)S(1)}, u32[]{:S(2)}, u32[]{:S(2)}) %collective-permute-start.12) | collective-permute-done | bytes 524320 | tf_op jit(solution)/shard_map/ppermute | solution.py:852
  146.9 18.5 %ffn_both_ways.2 = (f32[512,1024]{1,0:T(8,128)}, bf16[512,1024]{1,0:T(8,128)(2,1)}, bf16[512,1024]{1,0:T(8,128)(2,1)}, bf16[1024,1024]{1,0:T(8,128)(2,1)}, bf16[1024,4224]{1,0:T(8,128)(2,1)}) custom-call(bf16[512,512]{1,0:T(8,128)(2,1)} %get-tuple-element.95.own_ref.gated_hi_ref, bf16[512,512]{1,0:T(8,128)(2,1)} %copy-done.47, ...), custom_call_target="tpu_custom_call" | custom-call | flops 56000000000 | bytes 112000000 | tf_op jit(solution)/shard_map/ffn_both_ways/pallas_call | solution.py:735
  165.5 18.6 %ffn_both_ways.3 = (f32[512,1024]{1,0:T(8,128)}, bf16[512,1024]{1,0:T(8,128)(2,1)}, bf16[512,1024]{1,0:T(8,128)(2,1)}, bf16[1024,1024]{1,0:T(8,128)(2,1)}, bf16[1024,4224]{1,0:T(8,128)(2,1)}) custom-call(bf16[512,512]{1,0:T(8,128)(2,1)} %get-tuple-element.88.own_ref.gated_lo_ref, ...), custom_call_target="tpu_custom_call", output_to_operand_aliasing={{3}: (7, {}), {4}: (8, {})} | custom-call | flops 56000000000 | bytes 112000000 | tf_op jit(solution)/shard_map/ffn_both_ways/pallas_call | solution.py:735
  184.1 5.7 %convolution_convert_fusion = bf16[1024,1408]{1,0:T(8,128)(2,1)S(1)} fusion(bf16[1024,1024]{1,0:T(8,128)(2,1)S(1)} %copy-done.17, bf16[1024,4224]{1,0:T(8,128)(2,1)} %get-tuple-element.105), kind=kOutput, calls=%fused_computation.9 | convolution fusion | flops 2954231808 | bytes 7864320 | tf_op jit(solution)/shard_map/dot_general | solution.py:42
  189.8 7.0 %fusion.2 = bf16[1024,2816]{1,0:T(8,128)(2,1)S(1)} fusion(bf16[1024,1024]{1,0:T(8,128)(2,1)S(1)} %copy-done.49, bf16[1024,4224]{1,0:T(8,128)(2,1)S(1)} %copy-done.48), kind=kOutput, calls=%fused_computation.3 | convolution fusion | flops 5908463616 | bytes 13631488 | tf_op jit(solution)/shard_map/dot_general | solution.py:42
  197.6 1.4 collective-permute-start.13
  198.9 3.7 pad_maximum_fusion
  204.2 19.1 %collective-permute-done.14.got_ref = bf16[512,1024]{1,0:T(8,128)(2,1)} collective-permute-done((bf16[512,1024]{1,0:T(8,128)(2,1)}, bf16[512,1024]{1,0:T(8,128)(2,1)}, u32[]{:S(2)}, u32[]{:S(2)}) %collective-permute-start.14) | collective-permute-done | bytes 1048608 | tf_op jit(solution)/shard_map/ppermute | solution.py:852
  223.9 22.3 %mixer_backward.2 = (bf16[1024,1664]{1,0:T(8,128)(2,1)}, f32[8,1024]{1,0:T(8,128)}, f32[8,256]{1,0:T(8,128)}, bf16[512,1024]{1,0:T(8,128)(2,1)}, f32[512,1024]{1...) custom-call(s32[16]{0:T(128)} %get-tuple-element.160.resets_ref, ...), custom_call_target="tpu_custom_call" | custom-call | flops 60000002048 | bytes 120000000 | tf_op jit(solution)/shard_map/mixer_backward/pallas_call | solution.py:672
  247.2 22.1 %mixer_backward.3 = (bf16[1024,1664]{1,0:T(8,128)(2,1)}, f32[8,1024]{1,0:T(8,128)}, f32[8,256]{1,0:T(8,128)}, bf16[512,1024]{1,0:T(8,128)(2,1)}, f32[512,1024]{1...) custom-call(s32[16]{0:T(128)} %get-tuple-element.160.resets_ref, ...), custom_call_target="tpu_custom_call", output_to_operand_aliasing={{0}: (22, {})} | custom-call | flops 60000002048 | bytes 120000000 | tf_op jit(solution)/shard_map/mixer_backward/pallas_call | solution.py:672
  270.3 10.0 %mixer_weight_grads.1 = (f32[512,1024]{1,0:T(8,128)}, f32[512,1024]{1,0:T(8,128)}, bf16[512,1024]{1,0:T(8,128)(2,1)}, bf16[512,1024]{1,0:T(8,128)(2,1)}, f32[8,1024]{1,0:T(8,128)}) custom-call(s32[1]{0:T(128)} %bitcast.45.side_ref, bf16[1024,1024]{1,0:T(8,128)(2,1)} %copy-done.16, bf16[1024,1664]{1,0:T(8,128)(2,1)} %get-tuple-element.143.dproj_ref, ...), custom_call_target="tpu_custom_call" | custom-call | flops 32000000000 | bytes 64000000 | tf_op jit(solution)/shard_map/mixer_weight_grads/pallas_call | solution.py:817
  281.6 9.9 %multiply_reduce_fusion = (f32[1024]{0:T(1024)S(1)}, f32[1024,1024]{1,0:T(8,128)}, f32[1024,1024]{1,0:T(8,128)}) fusion(f32[1024]{0:T(1024)S(1)} %copy-done.38, bf16[512,1024]{1,0:T(8,128)(2,1)S(1)} %copy-done.3, bf16[512,1024]{1,0:T(8,128)(2,1)S(1)} %copy-done.5, bf16[1024,1664]{1,0:T(8,128)(2,1)} %get-tuple-element.143.dproj_ref, ...), kind=kOutput, calls=%fused_computation.7 | convolution fusion | flops 3503815680 | bytes 17309696 | tf_op jit(solution)/shard_map/dot_general | solution.py:48
  293.9 2.4 collective-permute-start.22
  297.8 1.4 collective-permute-done.22
  299.3 2.8 dynamic-slice_convert_fusion
  302.0 1.5 collective-permute-start.16
  303.5 4.7 %collective-permute-done.23 = f32[12,1024]{1,0:T(8,128)S(1)} collective-permute-done((f32[12,1024]{1,0:T(8,128)S(1)}, f32[12,1024]{1,0:T(8,128)S(1)}, u32[]{:S(2)}, u32[]{:S(2)}) %collective-permute-start.23) | collective-permute-done | bytes 49184 | tf_op jit(solution)/shard_map/ppermute | solution.py:859
  309.1 1.7 convert_add_fusion
  310.9 1.4 collective-permute-start.27
  312.3 1.7 convert_add_fusion.1
  315.4 1.6 add_convert_fusion
  317.0 1.5 collective-permute-start.25
  318.5 7.3 %collective-permute-done.27 = bf16[4,64,1024]{2,1,0:T(8,128)(2,1)S(1)} collective-permute-done((bf16[4,64,1024]{2,1,0:T(8,128)(2,1)S(1)}, bf16[4,64,1024]{2,1,0:T(8,128)(2,1)S(1)}, u32[]{:S(2)}, u32[]{:S(2)}) %collective-permute-start.27) | collective-permute-done | bytes 524320 | tf_op jit(solution)/shard_map/ppermute | solution.py:866
  326.0 2.6 collective-permute-start.28
  328.7 6.4 %collective-permute-done.18 = bf16[4,64,1024]{2,1,0:T(8,128)(2,1)S(1)} collective-permute-done((bf16[4,64,1024]{2,1,0:T(8,128)(2,1)S(1)}, bf16[4,64,1024]{2,1,0:T(8,128)(2,1)S(1)}, u32[]{:S(2)}, u32[]{:S(2)}) %collective-permute-start.18) | collective-permute-done | bytes 524320 | tf_op jit(solution)/shard_map/ppermute | solution.py:866
  335.3 3.2 collective-permute-start.19
  338.9 7.5 %collective-permute-done.19 = bf16[2,64,1024]{2,1,0:T(8,128)(2,1)S(1)} collective-permute-done((bf16[2,64,1024]{2,1,0:T(8,128)(2,1)S(1)}, bf16[2,64,1024]{2,1,0:T(8,128)(2,1)S(1)}, u32[]{:S(2)}, u32[]{:S(2)}) %collective-permute-start.19) | collective-permute-done | bytes 262176 | tf_op jit(solution)/shard_map/ppermute | solution.py:866
  363.5 1.3 maximum_bitcast_fusion.3
  364.9 1.3 maximum_bitcast_fusion.2
  366.2 2.8 multiply_reduce_fusion.1
  371.0 3.7 multiply_add_fusion
  (274 shorter events, 58.7 us)
Async XLA Ops:
  7.2 23.3 %copy-start = (f32[4,1024]{1,0:T(4,128)S(1)}, f32[4,1024]{1,0:T(4,128)}, u32[]{:S(2)}) copy-start(f32[4,1024]{1,0:T(4,128)} %param.34) | copy-start | bytes 49156
  7.2 13.6 %copy-start.29 = (bf16[64,512]{1,0:T(8,128)(2,1)S(1)}, bf16[64,512]{1,0:T(8,128)(2,1)}, u32[]{:S(2)}) copy-start(bf16[64,512]{1,0:T(8,128)(2,1)} %param.28) | copy-start | bytes 196612
  7.2 13.3 %copy-start.43 = (bf16[1024,4]{0,1:T(4,128)(2,1)S(1)}, bf16[1024,4]{0,1:T(4,128)(2,1)}, u32[]{:S(2)}) copy-start(bf16[1024,4]{0,1:T(4,128)(2,1)} %param.30) | copy-start | bytes 24580
  7.2 13.3 %copy-start.42 = (bf16[1024,4]{0,1:T(4,128)(2,1)S(1)}, bf16[1024,4]{0,1:T(4,128)(2,1)}, u32[]{:S(2)}) copy-start(bf16[1024,4]{0,1:T(4,128)(2,1)} %param.31) | copy-start | bytes 24580
  7.2 13.6 %copy-start.32 = (bf16[64,512]{1,0:T(8,128)(2,1)S(1)}, bf16[64,512]{1,0:T(8,128)(2,1)}, u32[]{:S(2)}) copy-start(bf16[64,512]{1,0:T(8,128)(2,1)} %param.29) | copy-start | bytes 196612
  7.3 13.7 %copy-start.25 = (bf16[512,1024]{1,0:T(8,128)(2,1)S(1)}, bf16[512,1024]{1,0:T(8,128)(2,1)}, u32[]{:S(2)}) copy-start(bf16[512,1024]{1,0:T(8,128)(2,1)} %param.22) | copy-start | bytes 3145732
  7.3 15.5 %copy-start.24 = (bf16[512,1024]{1,0:T(8,128)(2,1)S(1)}, bf16[512,1024]{1,0:T(8,128)(2,1)}, u32[]{:S(2)}) copy-start(bf16[512,1024]{1,0:T(8,128)(2,1)} %param.43) | copy-start | bytes 3145732
  7.3 15.8 %copy-start.44 = (s32[16]{0:T(128)S(1)}, s32[16]{0:T(128)}, u32[]{:S(2)}) copy-start(s32[16]{0:T(128)} %param.23) | copy-start | bytes 196
  7.3 15.7 %copy-start.45 = (s32[16]{0:T(128)S(1)}, s32[16]{0:T(128)}, u32[]{:S(2)}) copy-start(s32[16]{0:T(128)} %param.24) | copy-start | bytes 196
  7.3 138.8 %all-gather.2.cloned.1.call-start = ((), (), s32[]{:S(2)}) async-start(), calls=%async_computation.1 | async-start | bytes 11419648 | tf_op jit(solution)/shard_map/all_gather | solution.py:977
  7.3 5.5 %collective-permute-start.11 = (bf16[64,512]{1,0:T(8,128)(2,1)}, bf16[64,512]{1,0:T(8,128)(2,1)S(1)}, u32[]{:S(2)}, u32[]{:S(2)}) collective-permute-start(bf16[64,512]{1,0:T(8,128)(2,1)} %bitcast.177), channel_id=1, source_target_pairs={{0,1},{1,0},{2,3},{3,2},{4,5},{5,4},{6,7},{7,6},{8,9},{9,8},{10,11... | collective-permute-start | bytes 196616 | tf_op jit(solution)/shard_map/ppermute | solution.py:852
  16.5 358.2 %reduce-scatter.2.cloned.1.call-start = ((), (), s32[]{:S(2)}) async-start(), calls=%async_computation.2 | async-start | bytes 9191424 | tf_op jit(solution)/shard_map/reduce_scatter | solution.py:1040
  17.4 15.1 %collective-permute-start.1 = (bf16[1,64,768]{2,1,0:T(8,128)(2,1)S(1)}, bf16[1,64,768]{2,1,0:T(8,128)(2,1)S(1)}, u32[]{:S(2)}, u32[]{:S(2)}) collective-permute-start(bf16[1,64,768]{2,1,0:T(8,128)(2,1)S(1)} %fusion.14), channel_id=1, source_target_pairs={{0,16},{2,18},{4,20},{6,22},{8,24},{10,26},{12,28},{14,30},{16,0},... | collective-permute-start | bytes 294920 | tf_op jit(solution)/shard_map/ppermute | solution.py:866
  20.8 13.6 %collective-permute-start.5 = (bf16[1,64,896]{2,1,0:T(8,128)(2,1)S(1)}, bf16[1,64,896]{2,1,0:T(8,128)(2,1)}, u32[]{:S(2)}, u32[]{:S(2)}) collective-permute-start(bf16[1,64,896]{2,1,0:T(8,128)(2,1)S(1)} %fusion.13), channel_id=1, source_target_pairs={{0,16},{2,18},{4,20},{6,22},{8,24},{10,26},{12,28},{14,30},{16,0},... | collective-permute-start | bytes 344072 | tf_op jit(solution)/shard_map/ppermute | solution.py:866
  21.0 57.9 %collective-permute-start = (bf16[512,1024]{1,0:T(8,128)(2,1)S(1)}, bf16[512,1024]{1,0:T(8,128)(2,1)S(1)}, u32[]{:S(2)}, u32[]{:S(2)}) collective-permute-start(bf16[512,1024]{1,0:T(8,128)(2,1)S(1)} %copy-done.25), channel_id=1, source_target_pairs={{0,1},{1,0},{2,3},{3,2},{4,5},{5,4},{6,7},{7,6},{8,9},{9,8},{10,11... | collective-permute-start | bytes 3145736 | tf_op jit(solution)/shard_map/ppermute | solution.py:852
  22.7 56.1 %collective-permute-start.9 = (bf16[512,1024]{1,0:T(8,128)(2,1)S(1)}, bf16[512,1024]{1,0:T(8,128)(2,1)}, u32[]{:S(2)}, u32[]{:S(2)}) collective-permute-start(bf16[512,1024]{1,0:T(8,128)(2,1)S(1)} %copy-done.24), channel_id=1, source_target_pairs={{0,1},{1,0},{2,3},{3,2},{4,5},{5,4},{6,7},{7,6},{8,9},{9,8},{10,11... | collective-permute-start | bytes 3145736 | tf_op jit(solution)/shard_map/ppermute | solution.py:852
  32.5 17.2 %collective-permute-start.2 = (bf16[2,64,768]{2,1,0:T(8,128)(2,1)S(1)}, bf16[2,64,768]{2,1,0:T(8,128)(2,1)S(1)}, u32[]{:S(2)}, u32[]{:S(2)}) collective-permute-start(bf16[2,64,768]{2,1,0:T(8,128)(2,1)S(1)} %maximum_bitcast_fusion.1), channel_id=1, source_target_pairs={{0,8},{2,10},{4,12},{6,14},{8,0},{10,2},{12,4},{14,6},{16,24},{18,... | collective-permute-start | bytes 589832 | tf_op jit(solution)/shard_map/ppermute | solution.py:866
  35.4 25.0 %collective-permute-start.6 = (bf16[2,64,896]{2,1,0:T(8,128)(2,1)S(1)}, bf16[2,64,896]{2,1,0:T(8,128)(2,1)S(1)}, u32[]{:S(2)}, u32[]{:S(2)}) collective-permute-start(bf16[2,64,896]{2,1,0:T(8,128)(2,1)S(1)} %maximum_bitcast_fusion), channel_id=1, source_target_pairs={{0,8},{2,10},{4,12},{6,14},{8,0},{10,2},{12,4},{14,6},{16,24},{18,... | collective-permute-start | bytes 688136 | tf_op jit(solution)/shard_map/ppermute | solution.py:866
  49.8 12.9 %collective-permute-start.3 = (bf16[4,64,768]{2,1,0:T(8,128)(2,1)S(1)}, bf16[4,64,768]{2,1,0:T(8,128)(2,1)S(1)}, u32[]{:S(2)}, u32[]{:S(2)}) collective-permute-start(bf16[4,64,768]{2,1,0:T(8,128)(2,1)S(1)} %bitcast.176), channel_id=1, source_target_pairs={{0,4},{2,6},{4,0},{6,2},{8,12},{10,14},{12,8},{14,10},{16,20},{18,... | collective-permute-start | bytes 1179656 | tf_op jit(solution)/shard_map/ppermute | solution.py:866
  60.5 18.0 %collective-permute-start.7 = (bf16[4,64,896]{2,1,0:T(8,128)(2,1)S(1)}, bf16[4,64,896]{2,1,0:T(8,128)(2,1)S(1)}, u32[]{:S(2)}, u32[]{:S(2)}) collective-permute-start(bf16[4,64,896]{2,1,0:T(8,128)(2,1)S(1)} %bitcast.173), channel_id=1, source_target_pairs={{0,4},{2,6},{4,0},{6,2},{8,12},{10,14},{12,8},{14,10},{16,20},{18,... | collective-permute-start | bytes 1376264 | tf_op jit(solution)/shard_map/ppermute | solution.py:866
  62.9 23.0 %collective-permute-start.4 = (bf16[8,64,768]{2,1,0:T(8,128)(2,1)S(1)}, bf16[8,64,768]{2,1,0:T(8,128)(2,1)S(1)}, u32[]{:S(2)}, u32[]{:S(2)}) collective-permute-start(bf16[8,64,768]{2,1,0:T(8,128)(2,1)S(1)} %bitcast.170), channel_id=1, source_target_pairs={{0,2},{2,0},{4,6},{6,4},{8,10},{10,8},{12,14},{14,12},{16,18},{18,... | collective-permute-start | bytes 2359304 | tf_op jit(solution)/shard_map/ppermute | solution.py:866
  78.8 7.6 %collective-permute-start.8 = (bf16[8,64,896]{2,1,0:T(8,128)(2,1)S(1)}, bf16[8,64,896]{2,1,0:T(8,128)(2,1)S(1)}, u32[]{:S(2)}, u32[]{:S(2)}) collective-permute-start(bf16[8,64,896]{2,1,0:T(8,128)(2,1)S(1)} %bitcast.165), channel_id=1, source_target_pairs={{0,2},{2,0},{4,6},{6,4},{8,10},{10,8},{12,14},{14,12},{16,18},{18,... | collective-permute-start | bytes 2752520 | tf_op jit(solution)/shard_map/ppermute | solution.py:866
  112.6 19.1 %collective-permute-start.10 = (bf16[512,512]{1,0:T(8,128)(2,1)}, bf16[512,512]{1,0:T(8,128)(2,1)S(1)}, u32[]{:S(2)}, u32[]{:S(2)}) collective-permute-start(bf16[512,512]{1,0:T(8,128)(2,1)} %get-tuple-element.88.own_ref.gated_lo_ref), channel_id=1, source_target_pairs={{0,1},{1,0},{2,3},{3,2},{4,5},{5,4},{6,7},{7,6},{8,9},{9,8},{10,11... | collective-permute-start | bytes 1572872 | tf_op jit(solution)/shard_map/ppermute | solution.py:852
  131.7 33.7 %copy-start.46 = (bf16[512,512]{1,0:T(8,128)(2,1)}, bf16[512,512]{1,0:T(8,128)(2,1)S(1)}, u32[]{:S(2)}) copy-start(bf16[512,512]{1,0:T(8,128)(2,1)S(1)} %collective-permute-done.10.other_ref) | copy-start | bytes 1572868
  131.7 14.4 %collective-permute-start.12 = (bf16[512,512]{1,0:T(8,128)(2,1)}, bf16[512,512]{1,0:T(8,128)(2,1)S(1)}, u32[]{:S(2)}, u32[]{:S(2)}) collective-permute-start(bf16[512,512]{1,0:T(8,128)(2,1)} %get-tuple-element.95.own_ref.gated_hi_ref), channel_id=1, source_target_pairs={{0,1},{1,0},{2,3},{3,2},{4,5},{5,4},{6,7},{7,6},{8,9},{9,8},{10,11... | collective-permute-start | bytes 1572872 | tf_op jit(solution)/shard_map/ppermute | solution.py:852
  165.4 18.6 %copy-start.17 = (bf16[1024,1024]{1,0:T(8,128)(2,1)S(1)}, bf16[1024,1024]{1,0:T(8,128)(2,1)}, u32[]{:S(2)}) copy-start(bf16[1024,1024]{1,0:T(8,128)(2,1)} %get-tuple-element.94.cot_ref) | copy-start | bytes 6291460
  196.8 26.5 %collective-permute-start.14 = (bf16[512,1024]{1,0:T(8,128)(2,1)}, bf16[512,1024]{1,0:T(8,128)(2,1)}, u32[]{:S(2)}, u32[]{:S(2)}) collective-permute-start(bf16[512,1024]{1,0:T(8,128)(2,1)} %get-tuple-element.103.own_ref), channel_id=1, source_target_pairs={{0,1},{1,0},{2,3},{3,2},{4,5},{5,4},{6,7},{7,6},{8,9},{9,8},{10,11... | collective-permute-start | bytes 3145736 | tf_op jit(solution)/shard_map/ppermute | solution.py:852
  197.6 48.7 %collective-permute-start.13 = (bf16[512,1024]{1,0:T(8,128)(2,1)}, bf16[512,1024]{1,0:T(8,128)(2,1)}, u32[]{:S(2)}, u32[]{:S(2)}) collective-permute-start(bf16[512,1024]{1,0:T(8,128)(2,1)} %get-tuple-element.102.own_ref), channel_id=1, source_target_pairs={{0,1},{1,0},{2,3},{3,2},{4,5},{5,4},{6,7},{7,6},{8,9},{9,8},{10,11... | collective-permute-start | bytes 3145736 | tf_op jit(solution)/shard_map/ppermute | solution.py:852
  246.3 23.0 %collective-permute-start.15 = (bf16[512,1024]{1,0:T(8,128)(2,1)S(1)}, bf16[512,1024]{1,0:T(8,128)(2,1)S(1)}, u32[]{:S(2)}, u32[]{:S(2)}) collective-permute-start(bf16[512,1024]{1,0:T(8,128)(2,1)S(1)} %broadcast_select_fusion), channel_id=1, source_target_pairs={{0,1},{1,0},{2,3},{3,2},{4,5},{5,4},{6,7},{7,6},{8,9},{9,8},{10,11... | collective-permute-start | bytes 3145736 | tf_op jit(solution)/shard_map/ppermute | solution.py:852
  270.3 11.3 %copy-start.3 = (bf16[512,1024]{1,0:T(8,128)(2,1)S(1)}, bf16[512,1024]{1,0:T(8,128)(2,1)}, u32[]{:S(2)}) copy-start(bf16[512,1024]{1,0:T(8,128)(2,1)} %copy-done.2) | copy-start | bytes 3145732
  270.3 11.3 %copy-start.5 = (bf16[512,1024]{1,0:T(8,128)(2,1)S(1)}, bf16[512,1024]{1,0:T(8,128)(2,1)}, u32[]{:S(2)}) copy-start(bf16[512,1024]{1,0:T(8,128)(2,1)} %copy-done.4) | copy-start | bytes 3145732
  280.3 28.8 %collective-permute-start.26 = (bf16[512,1024]{1,0:T(8,128)(2,1)}, bf16[512,1024]{1,0:T(8,128)(2,1)}, u32[]{:S(2)}, u32[]{:S(2)}) collective-permute-start(bf16[512,1024]{1,0:T(8,128)(2,1)} %get-tuple-element.154), channel_id=1, source_target_pairs={{0,2},{2,0},{4,6},{6,4},{8,10},{10,8},{12,14},{14,12},{16,18},{18,... | collective-permute-start | bytes 3145736 | tf_op jit(solution)/shard_map/ppermute | solution.py:866
  281.1 31.1 %collective-permute-start.17 = (bf16[512,1024]{1,0:T(8,128)(2,1)}, bf16[512,1024]{1,0:T(8,128)(2,1)}, u32[]{:S(2)}, u32[]{:S(2)}) collective-permute-start(bf16[512,1024]{1,0:T(8,128)(2,1)} %get-tuple-element.145), channel_id=1, source_target_pairs={{0,2},{2,0},{4,6},{6,4},{8,10},{10,8},{12,14},{14,12},{16,18},{18,... | collective-permute-start | bytes 3145736 | tf_op jit(solution)/shard_map/ppermute | solution.py:866
  291.5 17.6 %copy-start.15 = (f32[512,1024]{1,0:T(8,128)S(1)}, f32[512,1024]{1,0:T(8,128)}, u32[]{:S(2)}) copy-start(f32[512,1024]{1,0:T(8,128)} %get-tuple-element.153) | copy-start | bytes 6291460
  292.6 1.3 collective-permute-start.21
  293.9 5.2 %collective-permute-start.22 = (f32[12,1024]{1,0:T(8,128)S(1)}, f32[12,1024]{1,0:T(8,128)S(1)}, u32[]{:S(2)}, u32[]{:S(2)}) collective-permute-start(f32[12,1024]{1,0:T(8,128)S(1)} %add.174), channel_id=1, source_target_pairs={{0,4},{2,6},{4,0},{6,2},{8,12},{10,14},{12,8},{14,10},{16,20},{18,... | collective-permute-start | bytes 147464 | tf_op jit(solution)/shard_map/ppermute | solution.py:859
  299.2 9.0 %collective-permute-start.23 = (f32[12,1024]{1,0:T(8,128)S(1)}, f32[12,1024]{1,0:T(8,128)S(1)}, u32[]{:S(2)}, u32[]{:S(2)}) collective-permute-start(f32[12,1024]{1,0:T(8,128)S(1)} %add.175), channel_id=1, source_target_pairs={{0,8},{2,10},{4,12},{6,14},{8,0},{10,2},{12,4},{14,6},{16,24},{18,... | collective-permute-start | bytes 147464 | tf_op jit(solution)/shard_map/ppermute | solution.py:859
  302.0 55.5 %collective-permute-start.16 = (bf16[512,1024]{1,0:T(8,128)(2,1)}, bf16[512,1024]{1,0:T(8,128)(2,1)S(1)}, u32[]{:S(2)}, u32[]{:S(2)}) collective-permute-start(bf16[512,1024]{1,0:T(8,128)(2,1)} %dynamic-slice_convert_fusion), channel_id=1, source_target_pairs={{0,1},{1,0},{2,3},{3,2},{4,5},{5,4},{6,7},{7,6},{8,9},{9,8},{10,11... | collective-permute-start | bytes 3145736 | tf_op jit(solution)/shard_map/ppermute | solution.py:852
  308.2 8.8 %collective-permute-start.24 = (f32[12,1024]{1,0:T(8,128)S(1)}, f32[12,1024]{1,0:T(8,128)S(1)}, u32[]{:S(2)}, u32[]{:S(2)}) collective-permute-start(f32[12,1024]{1,0:T(8,128)S(1)} %add.176), channel_id=1, source_target_pairs={{0,16},{2,18},{4,20},{6,22},{8,24},{10,26},{12,28},{14,30},{16,0},... | collective-permute-start | bytes 147464 | tf_op jit(solution)/shard_map/ppermute | solution.py:859
  310.9 14.9 %collective-permute-start.27 = (bf16[4,64,1024]{2,1,0:T(8,128)(2,1)S(1)}, bf16[4,64,1024]{2,1,0:T(8,128)(2,1)S(1)}, u32[]{:S(2)}, u32[]{:S(2)}) collective-permute-start(bf16[4,64,1024]{2,1,0:T(8,128)(2,1)S(1)} %fusion.10), channel_id=1, source_target_pairs={{0,4},{2,6},{4,0},{6,2},{8,12},{10,14},{12,8},{14,10},{16,20},{18,... | collective-permute-start | bytes 1572872 | tf_op jit(solution)/shard_map/ppermute | solution.py:866
  314.1 20.9 %collective-permute-start.18 = (bf16[4,64,1024]{2,1,0:T(8,128)(2,1)S(1)}, bf16[4,64,1024]{2,1,0:T(8,128)(2,1)S(1)}, u32[]{:S(2)}, u32[]{:S(2)}) collective-permute-start(bf16[4,64,1024]{2,1,0:T(8,128)(2,1)S(1)} %fusion.9), channel_id=1, source_target_pairs={{0,4},{2,6},{4,0},{6,2},{8,12},{10,14},{12,8},{14,10},{16,20},{18,... | collective-permute-start | bytes 1572872 | tf_op jit(solution)/shard_map/ppermute | solution.py:866
  317.0 31.0 %collective-permute-start.25 = (f32[12,1024]{1,0:T(8,128)S(1)}, f32[12,1024]{1,0:T(8,128)S(1)}, u32[]{:S(2)}, u32[]{:S(2)}) collective-permute-start(f32[12,1024]{1,0:T(8,128)S(1)} %add.177), channel_id=1, source_target_pairs={{0,1},{1,0},{2,3},{3,2},{4,5},{5,4},{6,7},{7,6},{8,9},{9,8},{10,11... | collective-permute-start | bytes 147464 | tf_op jit(solution)/shard_map/ppermute | solution.py:852
  326.0 12.4 %collective-permute-start.28 = (bf16[2,64,1024]{2,1,0:T(8,128)(2,1)S(1)}, bf16[2,64,1024]{2,1,0:T(8,128)(2,1)S(1)}, u32[]{:S(2)}, u32[]{:S(2)}) collective-permute-start(bf16[2,64,1024]{2,1,0:T(8,128)(2,1)S(1)} %fusion.12), channel_id=1, source_target_pairs={{0,8},{2,10},{4,12},{6,14},{8,0},{10,2},{12,4},{14,6},{16,24},{18,... | collective-permute-start | bytes 786440 | tf_op jit(solution)/shard_map/ppermute | solution.py:866
  335.3 11.1 %collective-permute-start.19 = (bf16[2,64,1024]{2,1,0:T(8,128)(2,1)S(1)}, bf16[2,64,1024]{2,1,0:T(8,128)(2,1)S(1)}, u32[]{:S(2)}, u32[]{:S(2)}) collective-permute-start(bf16[2,64,1024]{2,1,0:T(8,128)(2,1)S(1)} %fusion.11), channel_id=1, source_target_pairs={{0,8},{2,10},{4,12},{6,14},{8,0},{10,2},{12,4},{14,6},{16,24},{18,... | collective-permute-start | bytes 786440 | tf_op jit(solution)/shard_map/ppermute | solution.py:866
  338.6 9.4 %collective-permute-start.29 = (bf16[1,64,1024]{2,1,0:T(8,128)(2,1)S(1)}, bf16[1,64,1024]{2,1,0:T(8,128)(2,1)S(1)}, u32[]{:S(2)}, u32[]{:S(2)}) collective-permute-start(bf16[1,64,1024]{2,1,0:T(8,128)(2,1)S(1)} %dynamic-slice_convert_fusion.3), channel_id=1, source_target_pairs={{0,16},{2,18},{4,20},{6,22},{8,24},{10,26},{12,28},{14,30},{16,0},... | collective-permute-start | bytes 393224 | tf_op jit(solution)/shard_map/ppermute | solution.py:866
  346.4 24.6 %copy-start.19 = (f32[512,1024]{1,0:T(8,128)S(1)}, f32[512,1024]{1,0:T(8,128)}, u32[]{:S(2)}) copy-start(f32[512,1024]{1,0:T(8,128)} %get-tuple-element.137) | copy-start | bytes 6291460
  347.9 7.7 %collective-permute-start.20 = (bf16[1,64,1024]{2,1,0:T(8,128)(2,1)}, bf16[1,64,1024]{2,1,0:T(8,128)(2,1)}, u32[]{:S(2)}, u32[]{:S(2)}) collective-permute-start(bf16[1,64,1024]{2,1,0:T(8,128)(2,1)} %dynamic-slice_convert_fusion.4), channel_id=1, source_target_pairs={{0,16},{2,18},{4,20},{6,22},{8,24},{10,26},{12,28},{14,30},{16,0},... | collective-permute-start | bytes 393224 | tf_op jit(solution)/shard_map/ppermute | solution.py:866
  355.7 15.3 %copy-start.18 = (f32[512,1024]{1,0:T(8,128)S(1)}, f32[512,1024]{1,0:T(8,128)}, u32[]{:S(2)}) copy-start(f32[512,1024]{1,0:T(8,128)} %get-tuple-element.138) | copy-start | bytes 6291460
  (34 other events, 143.6 us)
Sparse Core Ops, SparseCore 0:
  16.6 102.6 all-gather.1
  202.7 109.3 reduce-scatter.1
